TPU v7x, 32 devices: a whole 2x2x4 slice. The times are simulated.
32 devices in a mesh: dp: 16 (over z, y, core), tensor: 2 (over x).
Axes of the slice: x: 2, y: 2, z: 4, core: 2. Of those that a mesh axis runs over, the one named last changes fastest.
Arguments:
- states_in: bfloat16 [16, 1024, 1024], P('dp', 'tensor'), may hold values from -6 to 6
- teacher: bfloat16 [16, 1024, 1024], P('dp', 'tensor'), may hold values from -6 to 6
- valid_mask: int32 [16, 1024], P('dp', 'tensor'), may hold values from 0 to 1, as said below
- prefix_len: int32 [16], P('dp'), may hold values from 102 to 512, as said below
- ln1_gain: bfloat16 [2, 1024], P(None, ('dp', 'tensor')), may hold values from 0.5 to 1.5
- ln1_shift: bfloat16 [2, 1024], P(None, ('dp', 'tensor')), may hold values from -2.5 to 2.5
- qkv_weight: bfloat16 [2, 1024, 3, 1024], P(None, 'dp', None, 'tensor'), may hold values from -0.1875 to 0.1875
- qkv_bias: bfloat16 [2, 3, 16, 64], P(None, None, 'tensor', 'dp'), may hold values from -2.5 to 2.5
- out_weight: bfloat16 [2, 1024, 1024], P(None, 'tensor', 'dp'), may hold values from -0.75 to 0.75
- out_bias: bfloat16 [2, 1024], P(None, ('dp', 'tensor')), may hold values from -2.5 to 2.5
- ln2_gain: bfloat16 [2, 1024], P(None, ('dp', 'tensor')), may hold values from 0.5 to 1.5
- ln2_shift: bfloat16 [2, 1024], P(None, ('dp', 'tensor')), may hold values from -2.5 to 2.5
- up_weight: bfloat16 [2, 1024, 4096], P(None, 'dp', 'tensor'), may hold values from -0.1875 to 0.1875
- up_bias: bfloat16 [2, 64, 64], P(None, 'tensor', 'dp'), may hold values from -2.5 to 2.5
- down_weight: bfloat16 [2, 4096, 1024], P(None, 'tensor', 'dp'), may hold values from -0.09375 to 0.09375
- down_bias: bfloat16 [2, 1024], P(None, ('dp', 'tensor')), may hold values from -2.5 to 2.5
Outputs:
- final_states: bfloat16 [16, 1024, 1024], P('dp', 'tensor')
- input_grad: float32 [16, 1024, 1024], P('dp', 'tensor')
- ln1_gain_grad: float32 [2, 1024], P(None, ('dp', 'tensor'))
- ln1_shift_grad: float32 [2, 1024], P(None, ('dp', 'tensor'))
- qkv_weight_grad: float32 [2, 1024, 3, 1024], P(None, 'dp', None, 'tensor')
- qkv_bias_grad: float32 [2, 3, 16, 64], P(None, None, 'tensor', 'dp')
- out_weight_grad: float32 [2, 1024, 1024], P(None, 'tensor', 'dp')
- out_bias_grad: float32 [2, 1024], P(None, ('dp', 'tensor'))
- ln2_gain_grad: float32 [2, 1024], P(None, ('dp', 'tensor'))
- ln2_shift_grad: float32 [2, 1024], P(None, ('dp', 'tensor'))
- up_weight_grad: float32 [2, 1024, 4096], P(None, 'dp', 'tensor')
- up_bias_grad: float32 [2, 64, 64], P(None, 'tensor', 'dp')
- down_weight_grad: float32 [2, 4096, 1024], P(None, 'tensor', 'dp')
- down_bias_grad: float32 [2, 1024], P(None, ('dp', 'tensor'))
Inputs may be any that keep to these rules, and one draw needn't show every extreme that they name: `valid_mask`: the first token of every sequence has 1. `prefix_len`: some sequence has exactly 512 and some exactly 102.
All inputs are finite; a program needn't handle non-finite values.
Results may differ from a plain program's by a relative error of at most 0.015.
Values may be sent and summed in bfloat16 or wider, within the bound.
A program may use at most 256 MiB of HBM per device.

v0:
```python
import jax
import jax.numpy as jnp
from jax import lax
from jax.sharding import PartitionSpec as P

H = 16
HD = 64


EPS = 1e-05
BIG = 1000000000.0
ROWS_CONTRACT = (((0,), (0,)), ((), ()))
LAST_CONTRACT = (((1,), (1,)), ((), ()))


def norm_rows(states, norm_gain, norm_shift):
    row_mean = jnp.mean(states, axis=-1, keepdims=True)
    centered = states - row_mean
    row_var = jnp.mean(centered * centered, axis=-1, keepdims=True)
    return centered * lax.rsqrt(row_var + EPS) * norm_gain + norm_shift


def gelu_tanh(values):
    return (
        0.5
        * values
        * (1.0 + jnp.tanh(0.7978845608028654 * (values + 0.044715 * values * values * values)))
    )


def fetch_weights(qkv_weight, qkv_bias, out_weight, up_weight, up_bias, down_weight, layer):
    return (
        lax.all_gather(qkv_weight[layer], "dp", axis=0, tiled=True),
        lax.all_gather(qkv_bias[layer], "dp", axis=2, tiled=True),
        lax.all_gather(out_weight[layer], "dp", axis=1, tiled=True),
        lax.all_gather(up_weight[layer], "dp", axis=0, tiled=True),
        lax.all_gather(up_bias[layer], "dp", axis=1, tiled=True),
        lax.all_gather(down_weight[layer], "dp", axis=1, tiled=True),
    )


def fetch_again(qkv_weight, qkv_bias, out_weight, up_weight, up_bias, down_weight, layer):
    return (
        lax.all_gather(qkv_weight[layer], "dp", axis=0, tiled=True),
        lax.all_gather(qkv_bias[layer], "dp", axis=2, tiled=True),
        lax.all_gather(out_weight[layer], "dp", axis=1, tiled=True),
        lax.all_gather(up_weight[layer], "dp", axis=0, tiled=True),
        lax.all_gather(up_bias[layer], "dp", axis=1, tiled=True),
        lax.all_gather(down_weight[layer], "dp", axis=1, tiled=True),
    )


def unpack(gathered):
    qkv_proj = gathered[0].reshape(gathered[0].shape[0], -1)
    qkv_add = gathered[1].reshape(-1).astype(jnp.float32)
    up_add = gathered[4].reshape(-1).astype(jnp.float32)
    return (qkv_proj, qkv_add, gathered[2], gathered[3], up_add, gathered[5])


def spread_rows(local_rows, weight):
    row_piece = lax.all_gather(local_rows, "tensor", axis=0, tiled=True)
    product = jnp.dot(row_piece, weight, preferred_element_type=jnp.float32)
    return (row_piece, product)


def gather_sum(rows_low, weight):
    return lax.psum_scatter(
        jnp.dot(rows_low, weight, preferred_element_type=jnp.float32).astype(jnp.bfloat16),
        "tensor",
        scatter_dimension=0,
        tiled=True,
    ).astype(jnp.float32)


def collect_grads(local_grad, weight, kept_rows):
    grad_piece = lax.all_gather(local_grad, "tensor", axis=0, tiled=True)
    product = lax.dot_general(grad_piece, weight, LAST_CONTRACT, preferred_element_type=jnp.float32)
    weight_grad = lax.dot_general(
        kept_rows, grad_piece, ROWS_CONTRACT, preferred_element_type=jnp.float32
    )
    return (product, weight_grad)


def return_grads(grad_low, weight):
    return lax.psum_scatter(
        lax.dot_general(grad_low, weight, LAST_CONTRACT, preferred_element_type=jnp.float32).astype(
            jnp.bfloat16
        ),
        "tensor",
        scatter_dimension=0,
        tiled=True,
    ).astype(jnp.float32)


def head_slopes(heads_local):
    heads_whole = heads_local * lax.axis_size("tensor")
    numbers = lax.axis_index("tensor") * heads_local + jnp.arange(heads_local, dtype=jnp.int32)
    return jnp.exp2(-(numbers.astype(jnp.float32) + 1.0) * 8.0 / heads_whole)


def block_scores(query_block, keys_all, offset, seq_prefix, slopes, scale):
    block_len = query_block.shape[0]
    key_pos = jnp.arange(keys_all.shape[0], dtype=jnp.int32)
    positions = offset + jnp.arange(block_len, dtype=jnp.int32)
    distance = jnp.abs(positions[:, None] - key_pos[None, :]).astype(jnp.float32)
    raw = jnp.einsum("qhd,khd->hqk", query_block, keys_all, preferred_element_type=jnp.float32)
    scores = raw * scale - slopes[:, None, None] * distance[None]
    visible = (key_pos[None, :] <= positions[:, None]) | (key_pos[None, :] < seq_prefix)
    return jnp.where(visible[None], scores, -BIG)


def attention_forward(qkv_low, seq_prefix, slopes, scale):
    row_total = qkv_low.shape[0]
    block_len = min(512, row_total)
    queries = qkv_low[:, 0]
    keys_all = qkv_low[:, 1]
    values_all = qkv_low[:, 2]

    def one_block(block_index):
        offset = block_index * block_len
        query_block = lax.dynamic_slice_in_dim(queries, offset, block_len, 0)
        scores = block_scores(query_block, keys_all, offset, seq_prefix, slopes, scale)
        row_max = jnp.max(scores, axis=-1, keepdims=True)
        raised = jnp.exp(scores - row_max)
        row_sum = jnp.sum(raised, axis=-1, keepdims=True)
        shares = (raised / row_sum).astype(jnp.bfloat16)
        outputs = jnp.einsum("hqk,khd->qhd", shares, values_all, preferred_element_type=jnp.float32)
        return (outputs, (row_max + jnp.log(row_sum))[:, :, 0])

    outputs, log_totals = lax.map(one_block, jnp.arange(row_total // block_len, dtype=jnp.int32))
    return (outputs.reshape(row_total, -1), log_totals)


def attention_backward(qkv_low, log_totals, grad_low, seq_prefix, slopes, scale):
    row_total, unused, heads_local, head_size = qkv_low.shape
    block_len = min(512, row_total)
    queries = qkv_low[:, 0]
    keys_all = qkv_low[:, 1]
    values_all = qkv_low[:, 2]
    grads_heads = grad_low.reshape(row_total, heads_local, head_size)

    def one_block(carry_grads, block_item):
        block_index, block_log = block_item
        offset = block_index * block_len
        query_block = lax.dynamic_slice_in_dim(queries, offset, block_len, 0)
        grad_block = lax.dynamic_slice_in_dim(grads_heads, offset, block_len, 0)
        scores = block_scores(query_block, keys_all, offset, seq_prefix, slopes, scale)
        shares = jnp.exp(scores - block_log[:, :, None])
        grad_shares = jnp.einsum(
            "qhd,khd->hqk", grad_block, values_all, preferred_element_type=jnp.float32
        )
        inner = jnp.sum(shares * grad_shares, axis=-1, keepdims=True)
        grad_scores = (shares * (grad_shares - inner)).astype(jnp.bfloat16)
        grad_query = (
            jnp.einsum("hqk,khd->qhd", grad_scores, keys_all, preferred_element_type=jnp.float32)
            * scale
        )
        grad_keys = (
            carry_grads[0]
            + jnp.einsum(
                "hqk,qhd->khd", grad_scores, query_block, preferred_element_type=jnp.float32
            )
            * scale
        )
        grad_values = carry_grads[1] + jnp.einsum(
            "hqk,qhd->khd",
            shares.astype(jnp.bfloat16),
            grad_block,
            preferred_element_type=jnp.float32,
        )
        return ((grad_keys, grad_values), grad_query)

    zeros_heads = jnp.zeros((row_total, heads_local, head_size), jnp.float32)
    block_ids = jnp.arange(row_total // block_len, dtype=jnp.int32)
    (grad_keys, grad_values), grad_queries = lax.scan(
        one_block, (zeros_heads, zeros_heads), (block_ids, log_totals)
    )
    grad_queries = grad_queries.reshape(row_total, heads_local, head_size)
    return jnp.stack([grad_queries, grad_keys, grad_values], axis=1)


def local(
    states_in,
    teacher,
    valid_mask,
    prefix_len,
    ln1_gain,
    ln1_shift,
    qkv_weight,
    qkv_bias,
    out_weight,
    out_bias,
    ln2_gain,
    ln2_shift,
    up_weight,
    up_bias,
    down_weight,
    down_bias,
):
    valid_count = lax.psum(jnp.sum(valid_mask).astype(jnp.float32), ("dp", "tensor"))
    gathered_small = (
        lax.all_gather(ln1_gain, ("dp", "tensor"), axis=1, tiled=True),
        lax.all_gather(ln1_shift, ("dp", "tensor"), axis=1, tiled=True),
        lax.all_gather(out_bias, ("dp", "tensor"), axis=1, tiled=True),
        lax.all_gather(ln2_gain, ("dp", "tensor"), axis=1, tiled=True),
        lax.all_gather(ln2_shift, ("dp", "tensor"), axis=1, tiled=True),
        lax.all_gather(down_bias, ("dp", "tensor"), axis=1, tiled=True),
    )
    small = [member.astype(jnp.float32) for member in gathered_small]
    layers = qkv_weight.shape[0]
    local_rows = states_in.shape[1]
    row_total = local_rows * lax.axis_size("tensor")
    heads_local = H // lax.axis_size("tensor")
    scale = HD ** (-0.5)
    slopes = head_slopes(heads_local)
    seq_prefix = prefix_len[0]
    states = states_in[0].astype(jnp.float32)
    kept = []
    for layer in range(layers):
        gathered = fetch_weights(
            qkv_weight, qkv_bias, out_weight, up_weight, up_bias, down_weight, layer
        )
        qkv_proj, qkv_add, out_proj, up_proj, up_add, down_proj = unpack(gathered)
        normed = norm_rows(states, small[0][layer], small[1][layer]).astype(jnp.bfloat16)
        normed_all, mixed = spread_rows(normed, qkv_proj)
        qkv_low = (mixed + qkv_add).astype(jnp.bfloat16).reshape(row_total, 3, heads_local, HD)
        heads_out, log_totals = attention_forward(qkv_low, seq_prefix, slopes, scale)
        heads_low = heads_out.astype(jnp.bfloat16)
        middle = states + gather_sum(heads_low, out_proj) + small[2][layer]
        normed_two = norm_rows(middle, small[3][layer], small[4][layer]).astype(jnp.bfloat16)
        normed_two_all, hidden = spread_rows(normed_two, up_proj)
        hidden = hidden + up_add
        active = gelu_tanh(hidden).astype(jnp.bfloat16)
        stored = None
        kept.append(
            (
                states,
                middle,
                normed_all,
                qkv_low,
                log_totals,
                heads_low,
                normed_two_all,
                hidden,
                active,
                stored,
            )
        )
        states = middle + gather_sum(active, down_proj) + small[5][layer]
    final_states = states.astype(jnp.bfloat16)[None]
    token_total = local_rows * lax.axis_size("tensor") * lax.axis_size("dp")
    factor = token_total / valid_count
    grad = (
        factor
        * valid_mask[0][:, None].astype(jnp.float32)
        * (states - teacher[0].astype(jnp.float32))
    )
    big_grads = [None] * layers
    small_grads = [None] * layers
    for layer in reversed(range(layers)):
        (
            before,
            middle,
            normed_all,
            qkv_low,
            log_totals,
            heads_low,
            normed_two_all,
            hidden,
            active,
            stored,
        ) = kept[layer]
        gathered = fetch_again(
            qkv_weight, qkv_bias, out_weight, up_weight, up_bias, down_weight, layer
        )
        qkv_proj, qkv_add, out_proj, up_proj, up_add, down_proj = unpack(gathered)
        grad_mlp = grad.astype(jnp.bfloat16)
        down_shift_grad = jnp.sum(grad_mlp.astype(jnp.float32), axis=0)
        grad_active, down_grad = collect_grads(grad_mlp, down_proj, active)
        unused, gelu_back = jax.vjp(gelu_tanh, hidden)
        grad_hidden = gelu_back(grad_active)[0].astype(jnp.bfloat16)
        up_shift_grad = jnp.sum(grad_hidden.astype(jnp.float32), axis=0)
        up_grad = lax.dot_general(
            normed_two_all, grad_hidden, ROWS_CONTRACT, preferred_element_type=jnp.float32
        )
        grad_normed_two = return_grads(grad_hidden, up_proj)
        unused, norm_back = jax.vjp(norm_rows, middle, small[3][layer], small[4][layer])
        part_states, gain_two_grad, shift_two_grad = norm_back(grad_normed_two)
        grad_middle = grad + part_states
        grad_attn = grad_middle.astype(jnp.bfloat16)
        out_shift_grad = jnp.sum(grad_attn.astype(jnp.float32), axis=0)
        grad_heads, out_grad = collect_grads(grad_attn, out_proj, heads_low)
        grad_qkv = attention_backward(
            qkv_low, log_totals, grad_heads.astype(jnp.bfloat16), seq_prefix, slopes, scale
        )
        qkv_grad_low = grad_qkv.reshape(row_total, -1).astype(jnp.bfloat16)
        qkv_shift_grad = jnp.sum(qkv_grad_low.astype(jnp.float32), axis=0)
        qkv_grad = lax.dot_general(
            normed_all, qkv_grad_low, ROWS_CONTRACT, preferred_element_type=jnp.float32
        )
        grad_normed = return_grads(qkv_grad_low, qkv_proj)
        unused, norm_back = jax.vjp(norm_rows, before, small[0][layer], small[1][layer])
        part_states, gain_one_grad, shift_one_grad = norm_back(grad_normed)
        grad = grad_middle + part_states
        layer_grads = (
            qkv_grad.reshape(gathered[0].shape),
            qkv_shift_grad.reshape(gathered[1].shape),
            out_grad,
            up_grad,
            up_shift_grad.reshape(gathered[4].shape),
            down_grad,
        )
        layer_grads = (
            lax.psum_scatter(layer_grads[0], "dp", scatter_dimension=0, tiled=True),
            lax.psum_scatter(layer_grads[1], "dp", scatter_dimension=2, tiled=True),
            lax.psum_scatter(layer_grads[2], "dp", scatter_dimension=1, tiled=True),
            lax.psum_scatter(layer_grads[3], "dp", scatter_dimension=0, tiled=True),
            lax.psum_scatter(layer_grads[4], "dp", scatter_dimension=1, tiled=True),
            lax.psum_scatter(layer_grads[5], "dp", scatter_dimension=1, tiled=True),
        )
        big_grads[layer] = layer_grads
        small_grads[layer] = (
            gain_one_grad,
            shift_one_grad,
            out_shift_grad,
            gain_two_grad,
            shift_two_grad,
            down_shift_grad,
        )
    stacked = [
        jnp.stack([big_grads[layer][member] for layer in range(layers)]) for member in range(6)
    ]
    small_stacked = [
        jnp.stack([small_grads[layer][member] for layer in range(layers)]) for member in range(6)
    ]
    small_sums = (
        lax.psum_scatter(small_stacked[0], ("dp", "tensor"), scatter_dimension=1, tiled=True),
        lax.psum_scatter(small_stacked[1], ("dp", "tensor"), scatter_dimension=1, tiled=True),
        lax.psum_scatter(small_stacked[2], ("dp", "tensor"), scatter_dimension=1, tiled=True),
        lax.psum_scatter(small_stacked[3], ("dp", "tensor"), scatter_dimension=1, tiled=True),
        lax.psum_scatter(small_stacked[4], ("dp", "tensor"), scatter_dimension=1, tiled=True),
        lax.psum_scatter(small_stacked[5], ("dp", "tensor"), scatter_dimension=1, tiled=True),
    )
    return (
        final_states,
        grad[None],
        small_sums[0],
        small_sums[1],
        stacked[0],
        stacked[1],
        stacked[2],
        small_sums[2],
        small_sums[3],
        small_sums[4],
        stacked[3],
        stacked[4],
        stacked[5],
        small_sums[5],
    )


def solution(mesh):
    return jax.shard_map(
        local,
        mesh=mesh,
        in_specs=(
            P("dp", "tensor", None),
            P("dp", "tensor", None),
            P("dp", "tensor"),
            P("dp"),
            P(None, ("dp", "tensor")),
            P(None, ("dp", "tensor")),
            P(None, "dp", None, "tensor"),
            P(None, None, "tensor", "dp"),
            P(None, "tensor", "dp"),
            P(None, ("dp", "tensor")),
            P(None, ("dp", "tensor")),
            P(None, ("dp", "tensor")),
            P(None, "dp", "tensor"),
            P(None, "tensor", "dp"),
            P(None, "tensor", "dp"),
            P(None, ("dp", "tensor")),
        ),
        out_specs=(
            P("dp", "tensor", None),
            P("dp", "tensor", None),
            P(None, ("dp", "tensor")),
            P(None, ("dp", "tensor")),
            P(None, "dp", None, "tensor"),
            P(None, None, "tensor", "dp"),
            P(None, "tensor", "dp"),
            P(None, ("dp", "tensor")),
            P(None, ("dp", "tensor")),
            P(None, ("dp", "tensor")),
            P(None, "dp", "tensor"),
            P(None, "tensor", "dp"),
            P(None, "tensor", "dp"),
            P(None, ("dp", "tensor")),
        ),
        check_vma=False,
    )
```

profile of v0, /device:TPU:0, one launch (start us, length us, event | category | flops | bytes accessed | tf_op | source)
XLA Modules:
  0.0 3138.2 jit_solution(378144109788344655)
XLA Ops:
  9.2 69.6 %all-gather.12 = bf16[32,32,2]{1,2,0:T(2,128)(2,1)S(1)} all-gather(bf16[1,32,2]{1,2,0:T(2,128)(2,1)} %bitcast.503), channel_id=1, replica_groups=mesh['dp'=16,'tensor'=2] {'dp','tensor'}, dimensions={0}, use_global_device_ids=true | all-gather | bytes 4224 | tf_op jit(solution)/shard_map/all_gather | solution.py:202
  78.9 63.1 %all-gather.13 = bf16[32,32,2]{1,2,0:T(2,128)(2,1)S(1)} all-gather(bf16[1,32,2]{1,2,0:T(2,128)(2,1)} %bitcast.504), channel_id=1, replica_groups=mesh['dp'=16,'tensor'=2] {'dp','tensor'}, dimensions={0}, use_global_device_ids=true | all-gather | bytes 4224 | tf_op jit(solution)/shard_map/all_gather | solution.py:203
  148.2 17.3 all-gather.1
  192.5 41.0 %while.56 = (s32[]{:T(128)}, bf16[2,512,8,64]{1,3,2,0:T(8,128)(2,1)}, f32[2,8,512]{2,1,0:T(8,128)S(1)}, s32[2]{0:T(128)S(1)}, s32[]{:T(128)}, /*index=5*/bf16[10...) while((s32[]{:T(128)}, ...), condition=%wide.region_5.6_spmd.clone, body=%wide.region_2.5_spmd.clone.sunk | while | flops 1118303744 | bytes 59385068 | solution.py:130
  244.0 66.8 %all-gather.14 = bf16[32,32,2]{1,2,0:T(2,128)(2,1)S(1)} all-gather(bf16[1,32,2]{1,2,0:T(2,128)(2,1)S(1)} %bitcast.505), channel_id=1, replica_groups=mesh['dp'=16,'tensor'=2] {'dp','tensor'}, dimensions={0}, use_global_device_ids=true | all-gather | bytes 4224 | tf_op jit(solution)/shard_map/all_gather | solution.py:204
  310.9 63.1 %all-gather.15 = bf16[32,32,2]{1,2,0:T(2,128)(2,1)S(1)} all-gather(bf16[1,32,2]{1,2,0:T(2,128)(2,1)S(1)} %bitcast.506), channel_id=1, replica_groups=mesh['dp'=16,'tensor'=2] {'dp','tensor'}, dimensions={0}, use_global_device_ids=true | all-gather | bytes 4224 | tf_op jit(solution)/shard_map/all_gather | solution.py:205
  374.1 65.2 %all-gather.16 = bf16[32,32,2]{1,2,0:T(2,128)(2,1)S(1)} all-gather(bf16[1,32,2]{1,2,0:T(2,128)(2,1)S(1)} %bitcast.507), channel_id=1, replica_groups=mesh['dp'=16,'tensor'=2] {'dp','tensor'}, dimensions={0}, use_global_device_ids=true | all-gather | bytes 4224 | tf_op jit(solution)/shard_map/all_gather | solution.py:206
  447.3 17.2 all-gather.4
  485.5 42.9 %all-gather.57.cloned.1.call-done = bf16[1,2048,1024]{1,2,0:T(8,128)(2,1)} async-done(((bf16[1,2048,64]{1,2,0:T(8,128)(2,1)}), bf16[1,2048,1024]{1,2,0:T(8,128)(2,1)}) %all-gather.57.cloned.1.call-update) | async-done | bytes 4194320 | tf_op jit(solution)/shard_map/all_gather | solution.py:38
  540.5 65.6 %all-gather.17 = bf16[32,32,2]{1,2,0:T(2,128)(2,1)S(1)} all-gather(bf16[1,32,2]{1,2,0:T(2,128)(2,1)S(1)} %bitcast.508), channel_id=1, replica_groups=mesh['dp'=16,'tensor'=2] {'dp','tensor'}, dimensions={0}, use_global_device_ids=true | all-gather | bytes 4224 | tf_op jit(solution)/shard_map/all_gather | solution.py:207
  612.8 17.7 all-gather.7
  633.8 18.1 all-gather.39.cloned.1.call-done
  666.5 31.0 while.57
  706.9 31.2 reduce-scatter.43.cloned.1.call-done
  743.1 21.4 all-gather.10
  764.7 26.4 all-gather.63.cloned.1.call-done
  791.1 33.7 %all-gather.41.cloned.1.call-done = bf16[1024,1024]{1,0:T(8,128)(2,1)} async-done(((bf16[512,1024]{1,0:T(8,128)(2,1)}), bf16[1024,1024]{1,0:T(8,128)(2,1)}) %all-gather.41.cloned.1.call-update) | async-done | bytes 2097168 | tf_op jit(solution)/shard_map/all_gather | solution.py:61
  835.5 42.9 %all-gather.65.cloned.1.call-done = bf16[1,2048,1024]{1,2,0:T(8,128)(2,1)} async-done(((bf16[1,2048,64]{1,2,0:T(8,128)(2,1)}), bf16[1,2048,1024]{1,2,0:T(8,128)(2,1)}) %all-gather.65.cloned.1.call-update) | async-done | bytes 4194320 | tf_op jit(solution)/shard_map/all_gather | solution.py:38
  891.0 39.9 %psum.7 = f32[]{:T(128)} all-reduce(f32[]{:T(128)S(6)} %convert_element_type.334), channel_id=1, replica_groups=mesh['dp'=16,'tensor'=2] {'dp','tensor'}, use_global_device_ids=true, to_apply=%region_21.22 | all-reduce | flops 1 | bytes 8 | tf_op jit(solution)/shard_map/psum | solution.py:200
  936.5 33.6 %all-gather.43.cloned.1.call-done = bf16[1024,1024]{1,0:T(8,128)(2,1)} async-done(((bf16[512,1024]{1,0:T(8,128)(2,1)}), bf16[1024,1024]{1,0:T(8,128)(2,1)}) %all-gather.43.cloned.1.call-update) | async-done | bytes 2097168 | tf_op jit(solution)/shard_map/all_gather | solution.py:76
  970.1 15.0 convert_reduce_fusion
  992.9 31.9 %reduce-scatter.47.cloned.1.call-done = bf16[512,1024]{1,0:T(8,128)(2,1)} async-done(((bf16[1024,1024]{1,0:T(8,128)(2,1)}), bf16[512,1024]{1,0:T(8,128)(2,1)}) %reduce-scatter.47.cloned.1.call-update) | async-done | bytes 1048592 | tf_op jit(solution)/shard_map/reduce_scatter | solution.py:85
  1031.1 33.2 %all-gather.45.cloned.1.call-done = bf16[1024,1024]{1,0:T(8,128)(2,1)} async-done(((bf16[512,1024]{1,0:T(8,128)(2,1)}), bf16[1024,1024]{1,0:T(8,128)(2,1)}) %all-gather.45.cloned.1.call-update) | async-done | bytes 2097168 | tf_op jit(solution)/shard_map/all_gather | solution.py:76
  1070.0 149.0 %while.58 = (s32[]{:T(128)}, f32[1024,8,64]{0,2,1:T(8,128)S(1)}, f32[1024,8,64]{0,2,1:T(8,128)}, bf16[2,512,8,64]{1,0,3,2:T(2,128)(2,1)}, s32[2]{0:T(128)S(1)}, ...) while((s32[]{:T(128)}, f32[1024,8,64]{0,2,1:T(8,128)S(1)}, ...), condition=%wide.region_27.28_spmd.clone, body=%wide.region_25.27_spmd.clone.sunk | while | flops 2736256512 | bytes 201941968 | solution.py:175
  1111.5 18.3 dynamic_update_slice.40
  1185.4 18.3 dynamic_update_slice.40
  1229.8 31.9 %reduce-scatter.49.cloned.1.call-done = bf16[512,1024]{1,0:T(8,128)(2,1)} async-done(((bf16[1024,1024]{1,0:T(8,128)(2,1)}), bf16[512,1024]{1,0:T(8,128)(2,1)}) %reduce-scatter.49.cloned.1.call-update) | async-done | bytes 1048592 | tf_op jit(solution)/shard_map/reduce_scatter | solution.py:85
  1269.0 33.2 %all-gather.47.cloned.1.call-done = bf16[1024,1024]{1,0:T(8,128)(2,1)} async-done(((bf16[512,1024]{1,0:T(8,128)(2,1)}), bf16[1024,1024]{1,0:T(8,128)(2,1)}) %all-gather.47.cloned.1.call-update) | async-done | bytes 2097168 | tf_op jit(solution)/shard_map/all_gather | solution.py:76
  1325.1 31.9 %reduce-scatter.51.cloned.1.call-done = bf16[512,1024]{1,0:T(8,128)(2,1)} async-done(((bf16[1024,1024]{1,0:T(8,128)(2,1)}), bf16[512,1024]{1,0:T(8,128)(2,1)}) %reduce-scatter.51.cloned.1.call-update) | async-done | bytes 1048592 | tf_op jit(solution)/shard_map/reduce_scatter | solution.py:85
  1364.5 33.2 %all-gather.49.cloned.1.call-done = bf16[1024,1024]{1,0:T(8,128)(2,1)} async-done(((bf16[512,1024]{1,0:T(8,128)(2,1)}), bf16[1024,1024]{1,0:T(8,128)(2,1)}) %all-gather.49.cloned.1.call-update) | async-done | bytes 2097168 | tf_op jit(solution)/shard_map/all_gather | solution.py:76
  1403.3 148.5 %while.59 = (s32[]{:T(128)}, f32[1024,8,64]{0,2,1:T(8,128)S(1)}, f32[1024,8,64]{0,2,1:T(8,128)}, bf16[2,512,8,64]{1,0,3,2:T(2,128)(2,1)}, s32[2]{0:T(128)S(1)}, ...) while((s32[]{:T(128)}, f32[1024,8,64]{0,2,1:T(8,128)S(1)}, ...), condition=%wide.region_36.37_spmd.clone, body=%wide.region_34.36_spmd.clone.sunk | while | flops 2736256512 | bytes 197747632 | solution.py:175
  1444.8 18.3 dynamic_update_slice.41
  1518.5 18.3 dynamic_update_slice.41
  1575.5 18.5 reduce-scatter.53.cloned.1.call-done
  1666.2 64.1 %reduce-scatter.81.cloned.1.call-done = f32[32,2]{1,0:T(8,128)} async-done(((f32[1024,2]{1,0:T(8,128)}), f32[32,2]{1,0:T(8,128)}) %reduce-scatter.81.cloned.1.call-update) | async-done | bytes 272
  1731.8 130.8 %reduce-scatter.79.cloned.1.call-done = f32[32,2]{1,0:T(8,128)} async-done(((f32[1024,2]{1,0:T(8,128)}), f32[32,2]{1,0:T(8,128)}) %reduce-scatter.79.cloned.1.call-update) | async-done | bytes 272
  1863.9 130.7 %reduce-scatter.77.cloned.1.call-done = f32[32,2]{1,0:T(8,128)} async-done(((f32[1024,2]{1,0:T(8,128)}), f32[32,2]{1,0:T(8,128)}) %reduce-scatter.77.cloned.1.call-update) | async-done | bytes 272
  1995.9 131.0 %reduce-scatter.75.cloned.1.call-done = f32[32,2]{1,0:T(8,128)} async-done(((f32[1024,2]{1,0:T(8,128)}), f32[32,2]{1,0:T(8,128)}) %reduce-scatter.75.cloned.1.call-update) | async-done | bytes 272
  2128.4 61.3 %all-reduce.4 = (f32[3,8,64]{1,2,0:T(8,128)}, f32[3,8,64]{1,2,0:T(8,128)}, f32[32,64]{1,0:T(8,128)S(1)}, f32[32,64]{1,0:T(8,128)S(1)}) all-reduce(f32[3,8,64]{1,2,0:T(8,128)S(1)} %copy.113, f32[3,8,64]{1,2,0:T(8,128)S(1)} %copy.112, f32[32,64]{1,0:T(8,128)S(1)} %reshape.604, ...), channel_id=27, replica_groups=mesh['dp'=16,'tensor'=2] {'dp'}, use_global_device_ids=true, to_apply=%region_51.52.clone | all-reduce | flops 7168 | bytes 57344
  2191.8 61.5 %reduce-scatter.59.cloned.1.call-done = f32[512,64]{0,1:T(8,128)} async-done(((f32[512,1024]{0,1:T(8,128)}), f32[512,64]{0,1:T(8,128)}) %reduce-scatter.59.cloned.1.call-update) | async-done | bytes 131088 | tf_op jit(solution)/shard_map/reduce_scatter | solution.py:316
  2259.4 129.8 %reduce-scatter.73.cloned.1.call-done = f32[32,2]{1,0:T(8,128)} async-done(((f32[1024,2]{1,0:T(8,128)}), f32[32,2]{1,0:T(8,128)}) %reduce-scatter.73.cloned.1.call-update) | async-done | bytes 272
  2390.5 131.6 %reduce-scatter.71.cloned.1.call-done = f32[32,2]{1,0:T(8,128)} async-done(((f32[1024,2]{1,0:T(8,128)}), f32[32,2]{1,0:T(8,128)}) %reduce-scatter.71.cloned.1.call-update) | async-done | bytes 272
  2523.5 103.2 %reduce-scatter.69.cloned.1.call-done = f32[2048,64]{0,1:T(8,128)} async-done(((f32[2048,1024]{0,1:T(8,128)}), f32[2048,64]{0,1:T(8,128)}) %reduce-scatter.69.cloned.1.call-update) | async-done | bytes 524304 | tf_op jit(solution)/shard_map/reduce_scatter | solution.py:319
  2626.6 108.5 %reduce-scatter.67.cloned.1.call-done = f32[2048,64]{0,1:T(8,128)} async-done(((f32[2048,1024]{0,1:T(8,128)}), f32[2048,64]{0,1:T(8,128)}) %reduce-scatter.67.cloned.1.call-update) | async-done | bytes 524304 | tf_op jit(solution)/shard_map/reduce_scatter | solution.py:319
  2737.4 106.2 %reduce-scatter.65.cloned.1.call-done = f32[64,2048]{1,0:T(8,128)} async-done(((f32[1024,2048]{1,0:T(8,128)}), f32[64,2048]{1,0:T(8,128)}) %reduce-scatter.65.cloned.1.call-update) | async-done | bytes 524304 | tf_op jit(solution)/shard_map/reduce_scatter | solution.py:317
  2843.5 108.3 %reduce-scatter.63.cloned.1.call-done = f32[64,2048]{1,0:T(8,128)} async-done(((f32[1024,2048]{1,0:T(8,128)}), f32[64,2048]{1,0:T(8,128)}) %reduce-scatter.63.cloned.1.call-update) | async-done | bytes 524304 | tf_op jit(solution)/shard_map/reduce_scatter | solution.py:317
  2954.1 86.5 %reduce-scatter.57.cloned.1.call-done = f32[64,3,512]{2,0,1:T(8,128)} async-done(((f32[1024,3,512]{2,0,1:T(8,128)}), f32[64,3,512]{2,0,1:T(8,128)}) %reduce-scatter.57.cloned.1.call-update) | async-done | bytes 393232 | tf_op jit(solution)/shard_map/reduce_scatter | solution.py:314
  3040.6 88.8 %reduce-scatter.55.cloned.1.call-done = f32[64,3,512]{2,0,1:T(8,128)} async-done(((f32[1024,3,512]{2,0,1:T(8,128)}), f32[64,3,512]{2,0,1:T(8,128)}) %reduce-scatter.55.cloned.1.call-update) | async-done | bytes 393232 | tf_op jit(solution)/shard_map/reduce_scatter | solution.py:314
  (630 shorter events, 623.4 us)
Async XLA Ops:
  7.2 158.4 %all-gather.51.cloned.1.call-start = ((), (), s32[]{:S(2)}) async-start(), calls=%async_computation.46 | async-start | bytes 3342336 | tf_op jit(solution)/shard_map/all_gather | solution.py:33
  9.1 168.8 %all-gather.35.cloned.1.call-start = ((), (), s32[]{:S(2)}) async-start(), calls=%async_computation.22 | async-start | bytes 3145728 | tf_op jit(solution)/shard_map/all_gather | solution.py:61
  146.7 91.2 %all-gather.53.cloned.1.call-start = ((), (), s32[]{:S(2)}) async-start(), calls=%async_computation.47 | async-start | bytes 1114112 | tf_op jit(solution)/shard_map/all_gather | solution.py:35
  147.5 293.7 %reduce-scatter.39.cloned.1.call-start = ((), (), s32[]{:S(2)}) async-start(), calls=%async_computation.23 | async-start | bytes 3145728 | tf_op jit(solution)/shard_map/reduce_scatter | solution.py:67
  242.1 199.1 %copy-start.3 = (bf16[1,512,1024]{2,1,0:T(8,128)(2,1)S(1)}, bf16[1,512,1024]{2,1,0:T(8,128)(2,1)}, u32[]{:S(2)}) copy-start(bf16[1,512,1024]{2,1,0:T(8,128)(2,1)} %param.24) | copy-start | bytes 3145732
  242.1 222.5 %all-gather.55.cloned.1.call-start = ((), (), s32[]{:S(2)}) async-start(), calls=%async_computation.48 | async-start | bytes 4456448 | tf_op jit(solution)/shard_map/all_gather | solution.py:36
  244.0 230.9 %all-gather.37.cloned.1.call-start = ((), (), s32[]{:S(2)}) async-start(), calls=%async_computation.24 | async-start | bytes 3145728 | tf_op jit(solution)/shard_map/all_gather | solution.py:61
  445.7 82.7 %all-gather.57.cloned.1.call-start = ((), (), s32[]{:S(2)}) async-start(), calls=%async_computation.49 | async-start | bytes 4456448 | tf_op jit(solution)/shard_map/all_gather | solution.py:38
  446.6 160.2 %reduce-scatter.41.cloned.1.call-start = ((), (), s32[]{:S(2)}) async-start(), calls=%async_computation.25 | async-start | bytes 3145728 | tf_op jit(solution)/shard_map/reduce_scatter | solution.py:67
  539.7 90.9 %all-gather.59.cloned.1.call-start = ((), (), s32[]{:S(2)}) async-start(), calls=%async_computation.50 | async-start | bytes 3342336 | tf_op jit(solution)/shard_map/all_gather | solution.py:33
  540.4 111.5 %all-gather.39.cloned.1.call-start = ((), (), s32[]{:S(2)}) async-start(), calls=%async_computation.26 | async-start | bytes 3145728 | tf_op jit(solution)/shard_map/all_gather | solution.py:61
  612.0 89.9 %all-gather.61.cloned.1.call-start = ((), (), s32[]{:S(2)}) async-start(), calls=%async_computation.51 | async-start | bytes 1114112 | tf_op jit(solution)/shard_map/all_gather | solution.py:35
  612.7 125.4 %reduce-scatter.43.cloned.1.call-start = ((), (), s32[]{:S(2)}) async-start(), calls=%async_computation.27 | async-start | bytes 3145728 | tf_op jit(solution)/shard_map/reduce_scatter | solution.py:67
  706.1 85.0 %all-gather.63.cloned.1.call-start = ((), (), s32[]{:S(2)}) async-start(), calls=%async_computation.52 | async-start | bytes 4456448 | tf_op jit(solution)/shard_map/all_gather | solution.py:36
  706.9 118.0 %all-gather.41.cloned.1.call-start = ((), (), s32[]{:S(2)}) async-start(), calls=%async_computation.28 | async-start | bytes 3145728 | tf_op jit(solution)/shard_map/all_gather | solution.py:61
  742.5 135.9 %all-gather.65.cloned.1.call-start = ((), (), s32[]{:S(2)}) async-start(), calls=%async_computation.53 | async-start | bytes 4456448 | tf_op jit(solution)/shard_map/all_gather | solution.py:38
  743.1 188.6 %reduce-scatter.45.cloned.1.call-start = ((), (), s32[]{:S(2)}) async-start(), calls=%async_computation.29 | async-start | bytes 3145728 | tf_op jit(solution)/shard_map/reduce_scatter | solution.py:67
  764.7 205.4 %copy-start.110 = (f32[2048]{0:T(1024)}, f32[2048]{0:T(1024)S(1)}, u32[]{:S(2)}) copy-start(f32[2048]{0:T(1024)S(1)} %reshape.608) | copy-start | bytes 24580
  889.7 80.4 %all-gather.43.cloned.1.call-start = ((), (), s32[]{:S(2)}) async-start(), calls=%async_computation.30 | async-start | bytes 3145728 | tf_op jit(solution)/shard_map/all_gather | solution.py:76
  936.5 88.4 %reduce-scatter.47.cloned.1.call-start = ((), (), s32[]{:S(2)}) async-start(), calls=%async_computation.31 | async-start | bytes 3145728 | tf_op jit(solution)/shard_map/reduce_scatter | solution.py:85
  992.8 71.4 %all-gather.45.cloned.1.call-start = ((), (), s32[]{:S(2)}) async-start(), calls=%async_computation.32 | async-start | bytes 3145728 | tf_op jit(solution)/shard_map/all_gather | solution.py:76
  1031.0 230.7 %reduce-scatter.49.cloned.1.call-start = ((), (), s32[]{:S(2)}) async-start(), calls=%async_computation.33 | async-start | bytes 3145728 | tf_op jit(solution)/shard_map/reduce_scatter | solution.py:85
  1229.8 72.5 %all-gather.47.cloned.1.call-start = ((), (), s32[]{:S(2)}) async-start(), calls=%async_computation.34 | async-start | bytes 3145728 | tf_op jit(solution)/shard_map/all_gather | solution.py:76
  1269.0 88.1 %reduce-scatter.51.cloned.1.call-start = ((), (), s32[]{:S(2)}) async-start(), calls=%async_computation.35 | async-start | bytes 3145728 | tf_op jit(solution)/shard_map/reduce_scatter | solution.py:85
  1325.1 72.6 %all-gather.49.cloned.1.call-start = ((), (), s32[]{:S(2)}) async-start(), calls=%async_computation.36 | async-start | bytes 3145728 | tf_op jit(solution)/shard_map/all_gather | solution.py:76
  1364.4 229.6 %reduce-scatter.53.cloned.1.call-start = ((), (), s32[]{:S(2)}) async-start(), calls=%async_computation.37 | async-start | bytes 3145728 | tf_op jit(solution)/shard_map/reduce_scatter | solution.py:85
  1562.1 168.3 %reduce-scatter.81.cloned.1.call-start = ((), (), s32[]{:S(2)}) async-start(), calls=%async_computation.59 | async-start | bytes 540672
  1563.7 298.8 %reduce-scatter.79.cloned.1.call-start = ((), (), s32[]{:S(2)}) async-start(), calls=%async_computation.58 | async-start | bytes 540672
  1564.9 429.7 %reduce-scatter.77.cloned.1.call-start = ((), (), s32[]{:S(2)}) async-start(), calls=%async_computation.57 | async-start | bytes 540672
  1566.1 560.9 %reduce-scatter.75.cloned.1.call-start = ((), (), s32[]{:S(2)}) async-start(), calls=%async_computation.56 | async-start | bytes 540672
  1567.2 624.6 %reduce-scatter.61.cloned.1.call-start = ((), (), s32[]{:S(2)}) async-start(), calls=%async_computation.41 | async-start | bytes 2228224 | tf_op jit(solution)/shard_map/reduce_scatter | solution.py:316
  1570.0 683.4 %reduce-scatter.59.cloned.1.call-start = ((), (), s32[]{:S(2)}) async-start(), calls=%async_computation.40 | async-start | bytes 2228224 | tf_op jit(solution)/shard_map/reduce_scatter | solution.py:316
  1575.5 813.7 %reduce-scatter.73.cloned.1.call-start = ((), (), s32[]{:S(2)}) async-start(), calls=%async_computation.55 | async-start | bytes 540672
  1597.2 925.0 %reduce-scatter.71.cloned.1.call-start = ((), (), s32[]{:S(2)}) async-start(), calls=%async_computation.54 | async-start | bytes 540672
  1599.5 1027.2 %reduce-scatter.69.cloned.1.call-start = ((), (), s32[]{:S(2)}) async-start(), calls=%async_computation.45 | async-start | bytes 8912896 | tf_op jit(solution)/shard_map/reduce_scatter | solution.py:319
  1612.2 1122.9 %reduce-scatter.67.cloned.1.call-start = ((), (), s32[]{:S(2)}) async-start(), calls=%async_computation.44 | async-start | bytes 8912896 | tf_op jit(solution)/shard_map/reduce_scatter | solution.py:319
  1625.3 1218.2 %reduce-scatter.65.cloned.1.call-start = ((), (), s32[]{:S(2)}) async-start(), calls=%async_computation.43 | async-start | bytes 8912896 | tf_op jit(solution)/shard_map/reduce_scatter | solution.py:317
  1635.9 1315.9 %reduce-scatter.63.cloned.1.call-start = ((), (), s32[]{:S(2)}) async-start(), calls=%async_computation.42 | async-start | bytes 8912896 | tf_op jit(solution)/shard_map/reduce_scatter | solution.py:317
  1646.4 1394.2 %reduce-scatter.57.cloned.1.call-start = ((), (), s32[]{:S(2)}) async-start(), calls=%async_computation.39 | async-start | bytes 6684672 | tf_op jit(solution)/shard_map/reduce_scatter | solution.py:314
  1655.3 1474.2 %reduce-scatter.55.cloned.1.call-start = ((), (), s32[]{:S(2)}) async-start(), calls=%async_computation.38 | async-start | bytes 6684672 | tf_op jit(solution)/shard_map/reduce_scatter | solution.py:314
  1664.2 590.9 %copy-start.18 = (bf16[512,1024]{1,0:T(8,128)(2,1)S(1)}, bf16[512,1024]{1,0:T(8,128)(2,1)}, u32[]{:S(2)}) copy-start(bf16[512,1024]{1,0:T(8,128)(2,1)} %reduce-scatter.39.cloned.1.call-done) | copy-start | bytes 3145732
  1664.2 590.9 %copy-start.35 = (bf16[512,1024]{1,0:T(8,128)(2,1)S(1)}, bf16[512,1024]{1,0:T(8,128)(2,1)}, u32[]{:S(2)}) copy-start(bf16[512,1024]{1,0:T(8,128)(2,1)} %reduce-scatter.51.cloned.1.call-done) | copy-start | bytes 3145732
  1664.2 590.9 %copy-start.53 = (f32[1,1024]{1,0:T(1,128)S(1)}, f32[1,1024]{1,0:T(1,128)}, u32[]{:S(2)}) copy-start(f32[1,1024]{1,0:T(1,128)} %copy-done.51) | copy-start | bytes 12292
  1664.2 590.9 %copy-start.56 = (f32[1,1024]{1,0:T(1,128)S(1)}, f32[1,1024]{1,0:T(1,128)}, u32[]{:S(2)}) copy-start(f32[1,1024]{1,0:T(1,128)} %copy-done.54) | copy-start | bytes 12292
  1664.2 590.9 %copy-start.64 = (f32[512]{0:T(512)S(1)}, f32[512]{0:T(512)}, u32[]{:S(2)}) copy-start(f32[512]{0:T(512)} %copy-done.62) | copy-start | bytes 6148
  1664.2 590.9 %copy-start.72 = (f32[512]{0:T(512)S(1)}, f32[512]{0:T(512)}, u32[]{:S(2)}) copy-start(f32[512]{0:T(512)} %copy-done.70) | copy-start | bytes 6148
  1664.2 590.9 %copy-start.75 = (f32[512]{0:T(512)S(1)}, f32[512]{0:T(512)}, u32[]{:S(2)}) copy-start(f32[512]{0:T(512)} %copy-done.74) | copy-start | bytes 6148
  1664.2 590.9 %copy-start.81 = (f32[512]{0:T(512)S(1)}, f32[512]{0:T(512)}, u32[]{:S(2)}) copy-start(f32[512]{0:T(512)} %copy-done.80) | copy-start | bytes 6148
  (132 other events, 1789.3 us)
Sparse Core Ops, SparseCore 0:
  10.8 47.9 all-gather.50
  146.9 31.0 all-gather.34
  180.7 37.9 all-gather.52
  242.3 31.9 reduce-scatter.38
  277.1 50.7 all-gather.54
  445.9 28.9 all-gather.36
  477.8 50.5 all-gather.56
  539.8 30.4 reduce-scatter.40
  572.5 45.8 all-gather.58
  620.3 31.5 all-gather.38
  654.1 37.9 all-gather.60
  706.2 31.8 reduce-scatter.42
  740.5 50.6 all-gather.62
  793.2 31.5 all-gather.40
  827.6 50.7 all-gather.64
  889.8 31.0 reduce-scatter.44
  936.6 33.4 all-gather.42
  993.0 31.8 reduce-scatter.46
  1031.1 33.1 all-gather.44
  1229.9 31.8 reduce-scatter.48
  1269.1 33.1 all-gather.46
  1325.2 31.8 reduce-scatter.50
  1364.5 33.1 all-gather.48
  1562.2 31.8 reduce-scatter.52
  1596.3 134.0 reduce-scatter.80
  1732.5 129.9 reduce-scatter.78
  1864.7 129.8 reduce-scatter.76
  1996.9 129.9 reduce-scatter.74
  2130.7 57.9 reduce-scatter.60
  2192.7 60.6 reduce-scatter.58
  2256.2 132.9 reduce-scatter.72
  2392.1 129.9 reduce-scatter.70
  2526.0 100.5 reduce-scatter.68
  2630.7 104.3 reduce-scatter.66
  2739.2 104.3 reduce-scatter.64
  2847.4 104.3 reduce-scatter.62
  2955.6 84.9 reduce-scatter.56
  3045.1 84.3 reduce-scatter.54
where the time goes:
time: 3160 us; the launch traced here: 3140 us
  waiting for transfers between devices  1850 us (59%)
  blocking collectives  568 us (18%)
  matrix products  384 us (12%)
  local copies, waits for them, and re-layouts  170 us (5%)
  other arithmetic  133 us (4%)
    unnamed x44, waiting for transfers between devices  721 us
    reduce_scatter x2, waiting for transfers between devices, local(): lax.psum_scatter(layer_grads[3], 'dp', scatter_dimension=0, tiled=True)  214 us
    reduce_scatter x2, waiting for transfers between devices, local(): lax.psum_scatter(layer_grads[5], 'dp', scatter_dimension=1, tiled=True)  212 us
    reduce_scatter x2, waiting for transfers between devices, local(): lax.psum_scatter(layer_grads[0], 'dp', scatter_dimension=0, tiled=True)  175 us
    all_gather x4, waiting for transfers between devices, collect_grads(): grad_piece = lax.all_gather(local_grad, 'tensor', axis=0, tiled=True)  133 us
    reduce_scatter x4, waiting for transfers between devices, return_grads(): lax.psum_scatter(lax.dot_general(grad_low, weight, LAST_CONTRACT, preferr...  114 us
    all_gather x2, waiting for transfers between devices, fetch_weights(): lax.all_gather(down_weight[layer], 'dp', axis=1, tiled=True)  85.9 us
    dynamic_update_slice x8, local copies, waits for them, and re-layouts, attention_forward(): lax.map(one_block, jnp.arange(row_total // block_len, dtype=jnp.int32))  76.5 us
  transfers between devices with their start and end apart: 38, of which 29 were waited for; matrix products, arithmetic and copies ran while one was open for 8% of the time, Pallas kernels for 0%

commit v1 on v0

v1 whole, which is shorter than its diff:
```python
import functools

import jax
import jax.numpy as jnp
import numpy as np
from jax import lax
from jax.experimental import pallas as pl
from jax.experimental.pallas import tpu as pltpu
from jax.sharding import PartitionSpec as P

LOG2E = 1.4426950408889634
BIG = 1000000000.0
NT = (((1,), (1,)), ((), ()))
NN = (((1,), (0,)), ((), ()))


def mm(a, b, dims):
    return lax.dot_general(a, b, dims, preferred_element_type=jnp.float32)


def lane_masks(width):
    lanes = lax.broadcasted_iota(jnp.int32, (1, width), 1)
    low = jnp.where(lanes < width // 2, 1.0, 0.0)
    return (low.astype(jnp.bfloat16), (1.0 - low).astype(jnp.bfloat16))


def rows_iota(n, m):
    return lax.broadcasted_iota(jnp.int32, (n, m), 0)


def cols_iota(n, m):
    return lax.broadcasted_iota(jnp.int32, (n, m), 1)


def scores_first(keys, query, slope, scale, prefix, start):
    n, m = (keys.shape[0], query.shape[0])
    key_pos = rows_iota(n, m)
    query_pos = cols_iota(n, m) + start
    distance = jnp.abs(query_pos - key_pos).astype(jnp.float32)
    raw = mm(keys, query, NT) * scale - slope * distance
    visible = (key_pos <= query_pos) | (key_pos < prefix)
    return jnp.where(visible, raw, -BIG)


def scores_second(keys, query, slope, scale, offset, mask_start):
    n, m = (keys.shape[0], query.shape[0])
    bias = slope * (rows_iota(n, 1) + offset).astype(jnp.float32)
    raw = mm(keys, query, NT) * scale + bias
    if mask_start is None:
        return raw
    return jnp.where(rows_iota(n, m) + mask_start <= cols_iota(n, m), raw, -BIG)


def score_parts(half, k_ref, k0_ref, query, slope, scale, prefix, start, step):
    rows = k_ref.shape[0]
    if half == 0:
        return [(None, 0, rows, scores_first(k_ref[...], query, slope, scale, prefix, start))]
    parts = [(0, 0, rows, scores_second(k0_ref[...], query, slope, scale, -2 * rows, None))]
    if start > 0:
        parts.append((1, 0, start, scores_second(k_ref[:start], query, slope, scale, -rows, None)))
    parts.append(
        (1, start, start + step, scores_second(k_ref[start : start + step], query, slope, scale, start - rows, 0))
    )
    return parts


def forward_body(half, slopes, prefix, scale, q_ref, k_ref, v_ref, k0_ref, v0_ref, o_ref, lse_ref, step):
    rows, width = q_ref.shape
    masks = lane_masks(width)
    pair = pl.program_id(0)
    head = width // 2
    values = v_ref[...].T
    values0 = v0_ref[...].T if half else None
    for start in range(0, rows, step):
        outs = []
        for side in range(2):
            query = q_ref[start : start + step] * masks[side]
            slope = slopes[pair * 2 + side]
            parts = score_parts(half, k_ref, k0_ref, query, slope, scale, prefix, start, step)
            top = parts[0][3].max(axis=0, keepdims=True)
            for part in parts[1:]:
                top = jnp.maximum(top, part[3].max(axis=0, keepdims=True))
            total = None
            out = None
            for which, low, high, raw in parts:
                raised = jnp.exp2(raw - top)
                part_sum = raised.sum(axis=0, keepdims=True)
                held = values0 if which == 0 else values
                held = held[side * head : (side + 1) * head, low:high]
                part_out = mm(held, raised.astype(jnp.bfloat16), NN)
                total = part_sum if total is None else total + part_sum
                out = part_out if out is None else out + part_out
            outs.append(out / total)
            lse_ref[0, side : side + 1, start : start + step] = top + jnp.log2(total)
        o_ref[start : start + step] = jnp.concatenate(outs, axis=0).T.astype(jnp.bfloat16)


def forward_kernel(meta, slopes, q_ref, k_ref, v_ref, k0_ref, v0_ref, o_ref, lse_ref, *, scale, step):
    args = (slopes, meta[1], scale, q_ref, k_ref, v_ref, k0_ref, v0_ref, o_ref, lse_ref, step)

    @pl.when(meta[0] == 0)
    def first():
        forward_body(0, *args)

    @pl.when(meta[0] != 0)
    def second():
        forward_body(1, *args)


def attention_forward(meta, slopes, qkv, kv0, scale):
    rows, width = qkv.shape
    pairs = width // 3 // 128
    block = lambda base: pl.BlockSpec((rows, 128), lambda j, *_: (0, base + j))
    return pl.pallas_call(
        functools.partial(forward_kernel, scale=scale * LOG2E, step=rows // 2),
        grid_spec=pltpu.PrefetchScalarGridSpec(
            num_scalar_prefetch=2,
            grid=(pairs,),
            in_specs=[block(0), block(pairs), block(2 * pairs), block(0), block(pairs)],
            out_specs=[block(0), pl.BlockSpec((1, 2, rows), lambda j, *_: (j, 0, 0))],
        ),
        out_shape=[
            jax.ShapeDtypeStruct((rows, width // 3), jnp.bfloat16),
            jax.ShapeDtypeStruct((pairs, 2, rows), jnp.float32),
        ],
        compiler_params=pltpu.CompilerParams(vmem_limit_bytes=40 * 1024 * 1024),
        cost_estimate=pl.CostEstimate(
            flops=pairs * 2 * rows * rows * 128 * 8, bytes_accessed=rows * width * 4, transcendentals=pairs * 4 * rows * rows
        ),
        name="attention_forward",
    )(meta, slopes, qkv, qkv, qkv, kv0, kv0)


def backward_body(half, slopes, prefix, scale, refs, step):
    q_ref, k_ref, v_ref, k0_ref, v0_ref, g_ref, lse_ref, gq_ref, gk_ref, gv_ref, gk0_ref, gv0_ref, sums = refs
    rows, width = q_ref.shape
    masks = lane_masks(width)
    pair = pl.program_id(0)
    head = width // 2
    keys = k_ref[...].T
    keys0 = k0_ref[...].T if half else None
    sums[...] = jnp.zeros_like(sums)
    for start in range(0, rows, step):
        outs = []
        for side in range(2):
            query = q_ref[start : start + step] * masks[side]
            grad = g_ref[start : start + step] * masks[side]
            slope = slopes[pair * 2 + side]
            parts = score_parts(half, k_ref, k0_ref, query, slope, scale * LOG2E, prefix, start, step)
            lse = lse_ref[0, side : side + 1, start : start + step]
            inner = None
            held = []
            for which, low, high, raw in parts:
                share = jnp.exp2(raw - lse)
                value = v0_ref[low:high] if which == 0 else v_ref[low:high]
                slot = 2 if which == 0 else 0
                grad_share = mm(value, grad, NT)
                part = (share * grad_share).sum(axis=0, keepdims=True)
                inner = part if inner is None else inner + part
                sums[slot + 1, low:high] += mm(share.astype(jnp.bfloat16), grad, NN)
                held.append((which, low, high, share, grad_share, slot))
            out = None
            for which, low, high, share, grad_share, slot in held:
                grad_score = (share * (grad_share - inner)).astype(jnp.bfloat16)
                sums[slot, low:high] += mm(grad_score, query, NN)
                key = keys0 if which == 0 else keys
                part = mm(key[side * head : (side + 1) * head, low:high], grad_score, NN)
                out = part if out is None else out + part
            outs.append(out)
        gq_ref[start : start + step] = (jnp.concatenate(outs, axis=0).T * scale).astype(jnp.bfloat16)
    gk_ref[...] = (sums[0] * scale).astype(jnp.bfloat16)
    gv_ref[...] = sums[1].astype(jnp.bfloat16)
    gk0_ref[...] = (sums[2] * scale).astype(jnp.bfloat16)
    gv0_ref[...] = sums[3].astype(jnp.bfloat16)


def backward_kernel(meta, slopes, *refs, scale, step):
    @pl.when(meta[0] == 0)
    def first():
        backward_body(0, slopes, meta[1], scale, refs, step)

    @pl.when(meta[0] != 0)
    def second():
        backward_body(1, slopes, meta[1], scale, refs, step)


def attention_backward(meta, slopes, qkv, kv0, grad_heads, lse, scale):
    rows, width = qkv.shape
    pairs = width // 3 // 128
    block = lambda base: pl.BlockSpec((rows, 128), lambda j, *_: (0, base + j))
    full = jax.ShapeDtypeStruct((rows, width // 3), jnp.bfloat16)
    return pl.pallas_call(
        functools.partial(backward_kernel, scale=scale, step=rows // 2),
        grid_spec=pltpu.PrefetchScalarGridSpec(
            num_scalar_prefetch=2,
            grid=(pairs,),
            in_specs=[
                block(0),
                block(pairs),
                block(2 * pairs),
                block(0),
                block(pairs),
                block(0),
                pl.BlockSpec((1, 2, rows), lambda j, *_: (j, 0, 0)),
            ],
            out_specs=[block(0)] * 5,
            scratch_shapes=[pltpu.VMEM((4, rows, 128), jnp.float32)],
        ),
        out_shape=[full] * 5,
        compiler_params=pltpu.CompilerParams(vmem_limit_bytes=40 * 1024 * 1024),
        cost_estimate=pl.CostEstimate(
            flops=pairs * 2 * rows * rows * 128 * 20, bytes_accessed=rows * width * 8, transcendentals=pairs * 4 * rows * rows
        ),
        name="attention_backward",
    )(meta, slopes, qkv, qkv, qkv, kv0, kv0, grad_heads, lse)


EPS = 1e-05
H = 16
HD = 64
ROWS_CONTRACT = (((0,), (0,)), ((), ()))


def norm_parts(states):
    centered = states - jnp.mean(states, axis=-1, keepdims=True)
    inverse = lax.rsqrt(jnp.mean(centered * centered, axis=-1, keepdims=True) + EPS)
    return (centered * inverse, inverse)


def norm_rows(states, gain, shift):
    return norm_parts(states)[0] * gain + shift


def norm_back(states, gain, grad):
    unit, inverse = norm_parts(states)
    scaled = grad * gain
    first = jnp.mean(scaled, axis=-1, keepdims=True)
    second = jnp.mean(scaled * unit, axis=-1, keepdims=True)
    return (inverse * (scaled - first - unit * second), jnp.sum(grad * unit, axis=0), jnp.sum(grad, axis=0))


def gelu_tanh(values):
    return 0.5 * values * (1.0 + jnp.tanh(0.7978845608028654 * (values + 0.044715 * values * values * values)))


class Ring:
    def __init__(self, devices):
        self.chips = devices // 2
        self.order = list(range(0, self.chips, 2)) + list(range(self.chips - 1, 0, -2))
        self.place = {chip: spot for spot, chip in enumerate(self.order)}
        self.ahead = self.pairs(1)
        self.behind = self.pairs(-1)
        self.sibling = [(i, i ^ 1) for i in range(devices)]

    def pairs(self, step):
        return [
            (2 * self.order[spot] + core, 2 * self.order[(spot + step) % self.chips] + core)
            for spot in range(self.chips)
            for core in range(2)
        ]

    def owners(self):
        table = []
        for device in range(2 * self.chips):
            spot = self.place[device // 2]
            table.append(
                [
                    2 * self.order[(spot - step) % self.chips] + ((device % 2) ^ core)
                    for core in range(2)
                    for step in range(self.chips)
                ]
            )
        return np.array(table, np.int32)

    def gather(self, block):
        half = self.chips // 2
        blocks = [None] * self.chips
        blocks[0] = block
        up = down = block
        for hop in range(1, half):
            up = lax.ppermute(up, "dp", self.ahead)
            down = lax.ppermute(down, "dp", self.behind)
            blocks[hop] = up
            blocks[self.chips - hop] = down
        middle = block.shape[0] // 2
        blocks[half] = jnp.concatenate(
            [lax.ppermute(up[:middle], "dp", self.ahead), lax.ppermute(down[middle:], "dp", self.behind)], axis=0
        )
        return blocks

    def scatter(self, parts):
        half = self.chips // 2
        middle = parts[0].shape[0] // 2
        low = jnp.bfloat16
        up = lax.ppermute(parts[half][middle:].astype(low), "dp", self.ahead)
        down = lax.ppermute(parts[half][:middle].astype(low), "dp", self.behind)
        zeros = jnp.zeros_like(up)
        up = jnp.concatenate([zeros, up], axis=0)
        down = jnp.concatenate([down, zeros], axis=0)
        for hop in range(half - 1, 0, -1):
            up = lax.ppermute(wide_sum(parts[self.chips - hop], up).astype(low), "dp", self.ahead)
            down = lax.ppermute(wide_sum(parts[hop], down).astype(low), "dp", self.behind)
        return wide_sum(wide_sum(parts[0], up), down)


def wide_sum(left, right):
    return left.astype(jnp.float32) + right.astype(jnp.float32)


SWAP = [(0, 1), (1, 0)]


def swap(block):
    return lax.ppermute(block, "tensor", SWAP)


def rows_of(blocks, low, high):
    return jnp.concatenate([block[:, low:high] for block in blocks], axis=0)


def fetch_attention(ring, qkv_shard, out_shard):
    rows = qkv_shard.shape[0]
    own = jnp.concatenate([qkv_shard.reshape(rows, -1), out_shard.T], axis=1)
    other = swap(own)
    size = own.shape[1] // 4
    both = [side[:, i * size : (i + 1) * size] for i in range(4) for side in (own, other)]
    blocks = ring.gather(jnp.concatenate(both, axis=1))
    blocks = blocks + [lax.ppermute(block, "dp", ring.sibling) for block in blocks]
    return (rows_of(blocks, 0, 6 * size), rows_of(blocks, 6 * size, 8 * size))


def fetch_mlp(ring, up_shard, down_shard):
    size = up_shard.shape[1]
    own = ring.gather(jnp.concatenate([up_shard, down_shard.T], axis=1))
    other = [swap(block) for block in own]
    own = own + [lax.ppermute(block, "dp", ring.sibling) for block in own]
    other = other + [lax.ppermute(block, "dp", ring.sibling) for block in other]
    return (
        [rows_of(own, 0, size), rows_of(other, 0, size)],
        [rows_of(own, size, 2 * size), rows_of(other, size, 2 * size)],
    )


def grad_rows(left, right, extra=None):
    half = left.shape[1] // 2

    def product(part):
        columns = slice(part * half, (part + 1) * half)
        out = lax.dot_general(left[:, columns], right, ROWS_CONTRACT, preferred_element_type=jnp.float32)
        if extra is not None:
            more = lax.dot_general(extra[0][:, columns], extra[1], ROWS_CONTRACT, preferred_element_type=jnp.float32)
            out = out + more
        return out

    return product


def sibling_sum(ring, product):
    arrived = lax.ppermute(product(1).astype(jnp.bfloat16), "dp", ring.sibling)
    return (product(0) + arrived.astype(jnp.float32)).astype(jnp.bfloat16)


def ring_sum(ring, total):
    rows = total.shape[0] // ring.chips
    return ring.scatter([total[i * rows : (i + 1) * rows] for i in range(ring.chips)])


def local(
    states_in,
    teacher,
    valid_mask,
    prefix_len,
    ln1_gain,
    ln1_shift,
    qkv_weight,
    qkv_bias,
    out_weight,
    out_bias,
    ln2_gain,
    ln2_shift,
    up_weight,
    up_bias,
    down_weight,
    down_bias,
):
    f32, low = (jnp.float32, jnp.bfloat16)
    layers, local_rows = (qkv_weight.shape[0], states_in.shape[1])
    width = states_in.shape[2]
    dp, tensor = (lax.axis_size("dp"), lax.axis_size("tensor"))
    here, side = (lax.axis_index("dp"), lax.axis_index("tensor"))
    ring = Ring(dp)
    piece = width // (dp * tensor)

    def by_half(pair, axis):
        return jnp.where(side == 0, pair, jnp.flip(pair, axis))

    owners = lax.dynamic_index_in_dim(jnp.asarray(ring.owners()), here, 0, keepdims=False)
    rows = width // dp
    columns = (owners[:, None] * rows + jnp.arange(rows, dtype=jnp.int32)[None]).reshape(1, width)
    to_ring = (jnp.arange(width, dtype=jnp.int32)[:, None] == columns).astype(low)

    def into_ring(values):
        return jnp.dot(values, to_ring, preferred_element_type=f32)

    def from_ring(values, precision=None):
        return lax.dot_general(
            values, to_ring.astype(values.dtype), NT, precision=precision, preferred_element_type=f32
        )

    count = jnp.sum(valid_mask)
    vectors = jnp.stack([ln1_gain, ln1_shift, out_bias, ln2_gain, ln2_shift, down_bias])
    packed = jnp.concatenate(
        [vectors.reshape(-1), qkv_bias.reshape(-1), up_bias.reshape(-1), jnp.stack([count // 256, count % 256]).astype(low)]
    )
    everything = lax.all_gather(packed, ("dp", "tensor"), axis=0, tiled=False)
    first, second, third = (vectors.size, vectors.size + qkv_bias.size, vectors.size + qkv_bias.size + up_bias.size)
    vectors = everything[:, :first].reshape(dp * tensor, 6 * layers, piece).transpose(1, 0, 2)
    small = into_ring(vectors.reshape(6 * layers, width)).reshape(6, layers, 1, width)
    qkv_add = everything[:, first:second].reshape((dp, tensor) + qkv_bias.shape).transpose(2, 3, 1, 4, 0, 5)
    qkv_add = by_half(qkv_add, 2).reshape(layers, 1, 3 * width).astype(f32)
    up_add = everything[:, second:third].reshape((dp, tensor) + up_bias.shape).transpose(2, 1, 3, 0, 4)
    up_add = by_half(up_add, 1).reshape(layers, tensor, 1, -1).astype(f32)
    counts = jnp.sum(everything[:, third:].astype(f32), axis=0)
    valid_count = counts[0] * 256.0 + counts[1]

    scale = HD ** (-0.5)
    pieces = jnp.arange(H, dtype=jnp.int32)
    heads_half = H // tensor
    heads = (pieces // heads_half ^ side) * heads_half + pieces % heads_half
    slopes = jnp.exp2(-(heads.astype(f32) + 1.0) * 8.0 / H) * LOG2E
    meta = jnp.stack([side.astype(jnp.int32), prefix_len[0]])

    before_first = lax.ppermute(states_in[0], "tensor", [(0, 1)])
    attention = []
    mlp = []
    for layer in range(layers):
        attention.append(fetch_attention(ring, qkv_weight[layer], out_weight[layer]))
        mlp.append(fetch_mlp(ring, up_weight[layer], down_weight[layer]))

    states = into_ring(states_in[0])
    target = into_ring(teacher[0])
    kept = []
    for layer in range(layers):
        qkv_proj, out_proj = attention[layer]
        up_proj, down_proj = mlp[layer]
        normed = norm_rows(states, small[0][layer], small[1][layer]).astype(low)
        if layer == 0:
            normed_first = norm_rows(into_ring(before_first), small[0][layer], small[1][layer]).astype(low)
        else:
            normed_first = lax.ppermute(normed, "tensor", [(0, 1)])
        qkv = (jnp.dot(normed, qkv_proj, preferred_element_type=f32) + qkv_add[layer]).astype(low)
        kv_first = jnp.dot(normed_first, qkv_proj[:, width:], preferred_element_type=f32) + qkv_add[layer][:, width:]
        kv_first = kv_first.astype(low)
        heads_out, lse = attention_forward(meta, slopes, qkv, kv_first, scale)
        middle = states + mm(heads_out, out_proj, NT) + small[2][layer]
        normed_two = norm_rows(middle, small[3][layer], small[4][layer]).astype(low)
        hidden = [jnp.dot(normed_two, up_proj[i], preferred_element_type=f32) + up_add[layer][i] for i in range(tensor)]
        active = [gelu_tanh(values).astype(low) for values in hidden]
        kept.append((states, normed, normed_first, qkv, kv_first, lse, heads_out, middle, normed_two, hidden, active))
        states = middle + mm(active[0], down_proj[0], NT) + mm(active[1], down_proj[1], NT) + small[5][layer]

    final_states = from_ring(states.astype(low)).astype(low)[None]
    factor = local_rows * tensor * dp / valid_count
    grad = factor * valid_mask[0][:, None].astype(f32) * (states - target)
    weight_grads = [None] * layers
    vector_grads = [None] * layers
    bias_grads = [None] * layers
    for layer in reversed(range(layers)):
        before, normed, normed_first, qkv, kv_first, lse, heads_out, middle, normed_two, hidden, active = kept[layer]
        qkv_proj, out_proj = attention[layer]
        up_proj, down_proj = mlp[layer]
        grad_mlp = grad.astype(low)
        down_shift = jnp.sum(grad_mlp.astype(f32), axis=0)
        grad_hidden = []
        for i in range(tensor):
            grad_active = jnp.dot(grad_mlp, down_proj[i], preferred_element_type=f32)
            grad_hidden.append(jax.vjp(gelu_tanh, hidden[i])[1](grad_active)[0].astype(low))
        down_grads = [sibling_sum(ring, grad_rows(grad_mlp, active[i])) for i in range(tensor)]
        down_grad = ring_sum(ring, wide_sum(down_grads[0], swap(down_grads[1])).astype(low))
        up_shift = jnp.stack([jnp.sum(values.astype(f32), axis=0) for values in grad_hidden])
        grad_normed = mm(grad_hidden[0], up_proj[0], NT) + mm(grad_hidden[1], up_proj[1], NT)
        up_grads = [sibling_sum(ring, grad_rows(normed_two, grad_hidden[i])) for i in range(tensor)]
        up_grad = ring_sum(ring, wide_sum(up_grads[0], swap(up_grads[1])).astype(low))
        part, gain_two, shift_two = norm_back(middle, small[3][layer], grad_normed)
        grad_middle = grad + part
        grad_attn = grad_middle.astype(low)
        out_shift = jnp.sum(grad_attn.astype(f32), axis=0)
        grad_heads = jnp.dot(grad_attn, out_proj, preferred_element_type=f32).astype(low)
        out_grad = ring_sum(ring, sibling_sum(ring, grad_rows(grad_attn, heads_out)))
        half = out_grad.shape[1] // 2
        out_grad = wide_sum(out_grad[:, :half], swap(out_grad[:, half:].astype(low)))
        grads = attention_backward(meta, slopes, qkv, kv_first, grad_heads, lse, scale)
        grad_qkv = jnp.concatenate(grads[:3], axis=1)
        grad_first = jnp.concatenate(grads[3:], axis=1)
        sent = mm(grad_first, qkv_proj[:, width:], NT).astype(low)
        arrived = lax.ppermute(sent, "tensor", [(1, 0)])
        qkv_shift = jnp.sum(grad_qkv.astype(f32), axis=0)
        first_shift = jnp.sum(grad_first.astype(f32), axis=0)
        qkv_shift = qkv_shift + jnp.pad(first_shift, (width, 0))
        query_grad = sibling_sum(ring, grad_rows(normed, grad_qkv[:, :width]))
        rest_grad = sibling_sum(ring, grad_rows(normed, grad_qkv[:, width:], (normed_first, grad_first)))
        qkv_grad = jnp.concatenate([ring_sum(ring, query_grad), ring_sum(ring, rest_grad)], axis=1)
        qkv_grad = qkv_grad.reshape(rows, 3, tensor, -1)
        qkv_grad = wide_sum(qkv_grad[:, :, 0], swap(qkv_grad[:, :, 1].astype(low)))
        grad_normed = mm(grad_qkv, qkv_proj, NT) + arrived.astype(f32)
        part, gain_one, shift_one = norm_back(before, small[0][layer], grad_normed)
        grad = grad_middle + part
        weight_grads[layer] = (qkv_grad, out_grad.T, up_grad, down_grad)
        vector_grads[layer] = (gain_one, shift_one, out_shift, gain_two, shift_two, down_shift)
        bias_grads[layer] = (qkv_shift, up_shift)

    input_grad = from_ring(grad, lax.Precision.HIGHEST)[None]
    qkv_grad, out_grad, up_grad, down_grad = [
        jnp.stack([weight_grads[layer][i] for layer in range(layers)]) for i in range(4)
    ]
    vectors = jnp.stack([vector_grads[layer][i] for i in range(6) for layer in range(layers)])
    vectors = from_ring(vectors, lax.Precision.HIGHEST).reshape(6 * layers, dp, tensor, piece).transpose(1, 2, 0, 3)
    qkv_shift = jnp.stack([bias_grads[layer][0] for layer in range(layers)])
    lane = qkv_bias.shape[3]
    qkv_shift = by_half(qkv_shift.reshape(layers, 3, tensor, -1, dp, lane), 2).transpose(4, 2, 0, 1, 3, 5)
    up_shift = jnp.stack([bias_grads[layer][1] for layer in range(layers)])
    up_shift = by_half(up_shift.reshape(layers, tensor, -1, dp, lane), 1).transpose(3, 1, 0, 2, 4)
    packed = jnp.concatenate([member.reshape(dp * tensor, -1) for member in (vectors, qkv_shift, up_shift)], axis=1)
    summed = lax.psum_scatter(packed, ("dp", "tensor"), scatter_dimension=0, tiled=True)[0]
    vectors = summed[:first].reshape(6, layers, piece)
    return (
        final_states,
        input_grad,
        vectors[0],
        vectors[1],
        qkv_grad,
        summed[first:second].reshape(qkv_bias.shape),
        out_grad,
        vectors[2],
        vectors[3],
        vectors[4],
        up_grad,
        summed[second:third].reshape(up_bias.shape),
        down_grad.transpose(0, 2, 1),
        vectors[5],
    )


def solution(mesh):
    return jax.shard_map(
        local,
        mesh=mesh,
        in_specs=(
            P("dp", "tensor", None),
            P("dp", "tensor", None),
            P("dp", "tensor"),
            P("dp"),
            P(None, ("dp", "tensor")),
            P(None, ("dp", "tensor")),
            P(None, "dp", None, "tensor"),
            P(None, None, "tensor", "dp"),
            P(None, "tensor", "dp"),
            P(None, ("dp", "tensor")),
            P(None, ("dp", "tensor")),
            P(None, ("dp", "tensor")),
            P(None, "dp", "tensor"),
            P(None, "tensor", "dp"),
            P(None, "tensor", "dp"),
            P(None, ("dp", "tensor")),
        ),
        out_specs=(
            P("dp", "tensor", None),
            P("dp", "tensor", None),
            P(None, ("dp", "tensor")),
            P(None, ("dp", "tensor")),
            P(None, "dp", None, "tensor"),
            P(None, None, "tensor", "dp"),
            P(None, "tensor", "dp"),
            P(None, ("dp", "tensor")),
            P(None, ("dp", "tensor")),
            P(None, ("dp", "tensor")),
            P(None, "dp", "tensor"),
            P(None, "tensor", "dp"),
            P(None, "tensor", "dp"),
            P(None, ("dp", "tensor")),
        ),
        check_vma=False,
    )
```

time: 3160 us -> 1490 us (0.47)
  waiting for transfers between devices: 1850 us -> 684 us
  blocking collectives: 568 us -> 42.8 us
  starting transfers between devices: 2.15 us -> 187 us
  matrix products: 384 us -> 227 us
  Pallas kernels: 0 us -> 83.2 us
  other arithmetic: 133 us -> 83.7 us
    reduce_scatter x16 -> x0, waiting for transfers between devices: 808 us -> none  [the longest x2 214 us: local(): lax.psum_scatter(layer_grads[3], 'dp', scatter_dimension=0, tiled=True)]
    unnamed x44 -> x2, waiting for transfers between devices: 721 us -> 102 us
    ppermute x0 -> x204, waiting for transfers between devices: none -> 582 us  [the longest x26 179 us: swap(): return lax.ppermute(block, 'tensor', SWAP)]
    all_gather x10 -> x0, blocking collectives: 467 us -> none  [the longest x1 69.6 us: local(): lax.all_gather(ln1_gain, ('dp', 'tensor'), axis=1, tiled=True)]
    all_gather x16 -> x0, waiting for transfers between devices: 317 us -> none  [the longest x4 133 us: collect_grads(): grad_piece = lax.all_gather(local_grad, 'tensor', axis=0, tiled=True)]
    ppermute x0 -> x204, starting transfers between devices: none -> 187 us  [the longest x30 40 us: scatter(): lax.ppermute(wide_sum(parts[hop], down).astype(low), 'dp', self.behind)]
    dot_general x52 -> x67, matrix products: 384 us -> 227 us  [the longest x28 78.3 us: product(): lax.dot_general(left[:, columns], right, ROWS_CONTRACT, preferred_element...]
    pallas_call x0 -> x4, Pallas kernels: none -> 83.2 us  [the longest x2 45.8 us: attention_backward(): pl.pallas_call(functools.partial(backward_kernel, scale=scale, step=rows...]
  transfers between devices with their start and end apart: 38 -> 205, of which waited for: 29 -> 105; matrix products, arithmetic and copies ran while one was open for 8% -> 24% of each run, Pallas kernels for 0% -> 3%
where the time goes in v1:
time: 1490 us; the launch traced here: 1480 us
  waiting for transfers between devices  684 us (46%)
  matrix products  227 us (15%)
  starting transfers between devices  187 us (13%)
  local copies, waits for them, and re-layouts  151 us (10%)
  other arithmetic  83.7 us (6%)
  Pallas kernels  83.2 us (6%)
  blocking collectives  42.8 us (3%)
  between operations  22.7 us (2%)
    ppermute x26, waiting for transfers between devices, swap(): return lax.ppermute(block, 'tensor', SWAP)  179 us
    unnamed x2, waiting for transfers between devices  102 us
    unnamed x545, local copies, waits for them, and re-layouts  96.7 us
    ppermute x30, waiting for transfers between devices, scatter(): lax.ppermute(wide_sum(parts[hop], down).astype(low), 'dp', self.behind)  82.9 us
    ppermute x30, waiting for transfers between devices, scatter(): lax.ppermute(wide_sum(parts[self.chips - hop], up).astype(low), 'dp', sel...  78.5 us
    dot_general x28, matrix products, product(): lax.dot_general(left[:, columns], right, ROWS_CONTRACT, preferred_element...  78.3 us
    ppermute x12, waiting for transfers between devices, gather(): up = lax.ppermute(up, 'dp', self.ahead)  68.5 us
    dot_general x14, matrix products, mm(): return lax.dot_general(a, b, dims, preferred_element_type=jnp.float32)  47.8 us
  transfers between devices with their start and end apart: 205, of which 105 were waited for; matrix products, arithmetic and copies ran while one was open for 24% of the time, Pallas kernels for 3%

profile of v1, /device:TPU:0, one launch (start us, length us, event | category | flops | bytes accessed | tf_op | source)
XLA Modules:
  0.0 1481.9 jit_solution(13322958344310422044)
XLA Ops:
  24.2 42.8 %all-reduce.22 = bf16[26688]{0:T(1024)(128)(2,1)S(1)} all-reduce(bf16[26688]{0:T(1024)(128)(2,1)S(1)} %dynamic-update-slice), channel_id=2, replica_groups=mesh['dp'=16,'tensor'=2] {'dp','tensor'}, use_global_device_ids=true, to_apply=%add.22 | all-reduce | flops 26688 | bytes 106752
  119.6 8.2 collective-permute-done.68
  133.8 6.2 collective-permute-done.51
  141.0 9.1 collective-permute-done.1
  151.6 11.7 collective-permute-done.85
  174.6 6.0 collective-permute-done.69
  184.7 7.2 collective-permute-done.19
  194.5 8.7 collective-permute-done.52
  205.7 8.6 collective-permute-done.2
  217.3 12.2 collective-permute-done.70
  233.2 8.0 collective-permute-done.74
  251.5 15.3 %collective-permute-done.75 = bf16[32,4096]{1,0:T(8,128)(2,1)S(1)} collective-permute-done((bf16[32,4096]{1,0:T(8,128)(2,1)S(1)}, bf16[32,4096]{1,0:T(8,128)(2,1)S(1)}, u32[]{:S(2)}, u32[]{:S(2)}) %collective-permute-start.75) | collective-permute-done | bytes 262176 | tf_op jit(solution)/shard_map/ppermute | solution.py:287
  297.0 6.7 collective-permute-done.56
  304.3 9.6 collective-permute-done.6
  321.6 7.2 collective-permute-done.57
  328.9 9.4 collective-permute-done.7
  340.0 7.1 collective-permute-done.58
  348.6 6.4 collective-permute-done.4
  378.3 21.5 %collective-permute-done.87 = bf16[64,4096]{1,0:T(8,128)(2,1)S(1)} collective-permute-done((bf16[64,4096]{1,0:T(8,128)(2,1)S(1)}, bf16[64,4096]{1,0:T(8,128)(2,1)S(1)}, u32[]{:S(2)}, u32[]{:S(2)}) %collective-permute-start.87) | collective-permute-done | bytes 524320 | tf_op jit(solution)/shard_map/ppermute | solution.py:314
  406.2 21.5 %collective-permute-done.88 = bf16[64,4096]{1,0:T(8,128)(2,1)S(1)} collective-permute-done((bf16[64,4096]{1,0:T(8,128)(2,1)S(1)}, bf16[64,4096]{1,0:T(8,128)(2,1)S(1)}, u32[]{:S(2)}, u32[]{:S(2)}) %collective-permute-start.88) | collective-permute-done | bytes 524320 | tf_op jit(solution)/shard_map/ppermute | solution.py:314
  429.9 12.7 collective-permute-done.90
  442.6 9.5 collective-permute-done.91
  456.2 12.5 collective-permute-done.38
  470.1 9.9 collective-permute-done.39
  480.1 10.4 collective-permute-done.40
  522.8 18.8 %attention_forward.2 = (bf16[512,1024]{1,0:T(8,128)(2,1)S(1)}, f32[8,2,512]{2,1,0:T(2,128)S(1)}) custom-call(s32[2]{0:T(128)S(1)} %pad_add_fusion.2.meta, f32[16]{0:T(128)S(1)} %fusion.167.slopes, bf16[512,3072]{1,0:T(8,128)(2,1)S(1)} %add_convert_fusion.1.q_ref.k_ref.v_ref.refs_0_.refs_1_.refs_2_, ...), custom_call_target="tpu_custom_call" | custom-call | flops 4294967296 | bytes 6291456 | tf_op jit(solution)/shard_map/attention_forward/pallas_call | solution.py:114
  586.8 14.3 collective-permute-done.67
  604.5 18.6 %attention_forward.3 = (bf16[512,1024]{1,0:T(8,128)(2,1)S(1)}, f32[8,2,512]{2,1,0:T(2,128)S(1)}) custom-call(s32[2]{0:T(128)S(1)} %pad_add_fusion.2.meta, f32[16]{0:T(128)S(1)} %fusion.167.slopes, bf16[512,3072]{1,0:T(8,128)(2,1)S(1)} %add_convert_fusion.q_ref.k_ref.v_ref.refs_0_.refs_1_.refs_2_, ...), custom_call_target="tpu_custom_call" | custom-call | flops 4294967296 | bytes 6291456 | tf_op jit(solution)/shard_map/attention_forward/pallas_call | solution.py:114
  647.8 7.7 convert_reduce_fusion.2
  655.5 9.6 convert_reduce_fusion.3
  677.0 22.8 %attention_backward.2 = (bf16[512,1024]{1,0:T(8,128)(2,1)S(1)}, bf16[512,1024]{1,0:T(8,128)(2,1)S(1)}, bf16[512,1024]{1,0:T(8,128)(2,1)S(1)}, bf16[512,1024]{1,0:T(8,128)(2,1)S(1)}, bf16[512,1024]{1,0:T(8,128)(2,1)S(1)}) custom-call(s32[2]{0:T(128)S(1)} %pad_add_fusion.2.meta, f32[16]{0:T(128)S(1)} %fusion.167.slopes, ...), custom_call_target="tpu_custom_call" | custom-call | flops 10737418240 | bytes 12582912 | tf_op jit(solution)/shard_map/attention_backward/pallas_call | solution.py:192
  745.3 27.3 %collective-permute-done.100 = bf16[512,1024]{0,1:T(8,128)(2,1)} collective-permute-done((bf16[512,1024]{0,1:T(8,128)(2,1)}, bf16[512,1024]{0,1:T(8,128)(2,1)}, u32[]{:S(2)}, u32[]{:S(2)}) %collective-permute-start.100) | collective-permute-done | bytes 1048608 | tf_op jit(solution)/shard_map/ppermute | solution.py:496
  772.7 7.9 multiply_reduce_fusion.2
  807.3 23.0 %attention_backward.3 = (bf16[512,1024]{1,0:T(8,128)(2,1)S(1)}, bf16[512,1024]{1,0:T(8,128)(2,1)S(1)}, bf16[512,1024]{1,0:T(8,128)(2,1)S(1)}, bf16[512,1024]{1,0:T(8,128)(2,1)S(1)}, bf16[512,1024]{1,0:T(8,128)(2,1)S(1)}) custom-call(s32[2]{0:T(128)S(1)} %pad_add_fusion.2.meta, f32[16]{0:T(128)S(1)} %fusion.167.slopes, bf16[512,3072]{1,0:T(8,128)(2,1)S(1)} %copy-done.14, ...), custom_call_target="tpu_custom_call" | custom-call | flops 10737418240 | bytes 12582912 | tf_op jit(solution)/shard_map/attention_backward/pallas_call | solution.py:192
  948.6 7.4 collective-permute-start.159
  977.6 13.0 collective-permute-done.101
  1005.5 11.7 fusion.63
  1022.1 101.6 %all-reduce.26.cloned.1.call-done = f32[32,832]{1,0:T(8,128)} async-done(((f32[32,832]{1,0:T(8,128)}), f32[32,832]{1,0:T(8,128)}) %all-reduce.26.cloned.1.call-update) | async-done | bytes 106512
  1226.3 6.0 collective-permute-done.113
  1248.3 13.0 collective-permute-done.139
  1276.3 30.0 %collective-permute-done.173 = bf16[512,2048]{1,0:T(8,128)(2,1)S(1)} collective-permute-done((bf16[512,2048]{1,0:T(8,128)(2,1)}, bf16[512,2048]{1,0:T(8,128)(2,1)S(1)}, u32[]{:S(2)}, u32[]{:S(2)}) %collective-permute-start.173) | collective-permute-done | bytes 2097184 | tf_op jit(solution)/shard_map/ppermute | solution.py:314
  1345.1 7.9 collective-permute-done.120
  1367.2 8.4 collective-permute-done.201
  1376.1 8.5 collective-permute-done.179
  1392.2 12.5 collective-permute-done.162
  1421.8 7.0 collective-permute-done.186
  1429.2 8.9 collective-permute-done.164
  1438.9 7.7 collective-permute-done.187
  (1225 shorter events, 777.1 us)
Async XLA Ops:
  7.3 1116.4 %all-reduce.26.cloned.1.call-start = ((), (), s32[]{:S(2)}) async-start(), calls=%async_computation | async-start | bytes 229376
  11.2 105.7 %collective-permute-start.34 = (bf16[64,4096]{1,0:T(8,128)(2,1)}, bf16[64,4096]{1,0:T(8,128)(2,1)}, u32[]{:S(2)}, u32[]{:S(2)}) collective-permute-start(bf16[64,4096]{1,0:T(8,128)(2,1)} %pad_maximum_fusion.4), channel_id=1, source_target_pairs={{0,1},{1,0},{2,3},{3,2},{4,5},{5,4},{6,7},{7,6},{8,9},{9,8},{10,11... | collective-permute-start | bytes 1572872 | tf_op jit(solution)/shard_map/ppermute | solution.py:314
  14.1 277.8 %collective-permute-start.26 = (bf16[64,4096]{1,0:T(8,128)(2,1)}, bf16[64,4096]{1,0:T(8,128)(2,1)}, u32[]{:S(2)}, u32[]{:S(2)}) collective-permute-start(bf16[64,4096]{1,0:T(8,128)(2,1)} %pad_maximum_fusion.4), channel_id=1, source_target_pairs={{0,2},{2,0},{4,6},{6,4},{8,10},{10,8},{12,14},{14,12},{16,18},{18,... | collective-permute-start | bytes 1572872 | tf_op jit(solution)/shard_map/ppermute | solution.py:336
  14.1 155.1 %collective-permute-start.22 = (bf16[64,4096]{1,0:T(8,128)(2,1)}, bf16[64,4096]{1,0:T(8,128)(2,1)}, u32[]{:S(2)}, u32[]{:S(2)}) collective-permute-start(bf16[64,4096]{1,0:T(8,128)(2,1)} %pad_maximum_fusion.4), channel_id=1, source_target_pairs={{0,4},{2,6},{8,0},{10,2},{16,8},{18,10},{24,16},{26,18},{28,24},{3... | collective-permute-start | bytes 1572872 | tf_op jit(solution)/shard_map/ppermute | solution.py:282
  15.7 113.0 %collective-permute-start.18 = (bf16[64,4096]{1,0:T(8,128)(2,1)}, bf16[64,4096]{1,0:T(8,128)(2,1)}, u32[]{:S(2)}, u32[]{:S(2)}) collective-permute-start(bf16[64,4096]{1,0:T(8,128)(2,1)} %pad_maximum_fusion.4), channel_id=1, source_target_pairs={{0,8},{2,10},{8,16},{10,18},{16,24},{18,26},{24,28},{26,30},{28,20... | collective-permute-start | bytes 1572872 | tf_op jit(solution)/shard_map/ppermute | solution.py:281
  19.8 71.9 %collective-permute-start.50 = (bf16[64,2048]{1,0:T(8,128)(2,1)}, bf16[64,2048]{1,0:T(8,128)(2,1)}, u32[]{:S(2)}, u32[]{:S(2)}) collective-permute-start(bf16[64,2048]{1,0:T(8,128)(2,1)} %pad_maximum_fusion.7), channel_id=1, source_target_pairs={{0,1},{1,0},{2,3},{3,2},{4,5},{5,4},{6,7},{7,6},{8,9},{9,8},{10,11... | collective-permute-start | bytes 786440 | tf_op jit(solution)/shard_map/ppermute | solution.py:314
  116.9 53.4 %collective-permute-start.72 = (bf16[64,4096]{1,0:T(8,128)(2,1)S(1)}, bf16[64,4096]{1,0:T(8,128)(2,1)S(1)}, u32[]{:S(2)}, u32[]{:S(2)}) collective-permute-start(bf16[64,4096]{1,0:T(8,128)(2,1)S(1)} %copy-done.87), channel_id=1, source_target_pairs={{0,4},{2,6},{8,0},{10,2},{16,8},{18,10},{24,16},{26,18},{28,24},{3... | collective-permute-start | bytes 1572872 | tf_op jit(solution)/shard_map/ppermute | solution.py:282
  128.7 37.1 %collective-permute-start.17 = (bf16[512,1024]{1,0:T(8,128)(2,1)S(1)}, bf16[512,1024]{1,0:T(8,128)(2,1)S(1)}, u32[]{:S(2)}, u32[]{:S(2)}) collective-permute-start(bf16[512,1024]{1,0:T(8,128)(2,1)S(1)} %bitcast.348), channel_id=1, source_target_pairs={{0,1},{2,3},{4,5},{6,7},{8,9},{10,11},{12,13},{14,15},{16,17},{18,... | collective-permute-start | bytes 3145736 | tf_op jit(solution)/shard_map/ppermute | solution.py:433
  170.3 46.7 %collective-permute-start.23 = (bf16[64,4096]{1,0:T(8,128)(2,1)}, bf16[64,4096]{1,0:T(8,128)(2,1)S(1)}, u32[]{:S(2)}, u32[]{:S(2)}) collective-permute-start(bf16[64,4096]{1,0:T(8,128)(2,1)} %collective-permute-done.22), channel_id=1, source_target_pairs={{0,4},{2,6},{8,0},{10,2},{16,8},{18,10},{24,16},{26,18},{28,24},{3... | collective-permute-start | bytes 1572872 | tf_op jit(solution)/shard_map/ppermute | solution.py:282
  173.1 44.0 %collective-permute-start.73 = (bf16[64,4096]{1,0:T(8,128)(2,1)S(1)}, bf16[64,4096]{1,0:T(8,128)(2,1)S(1)}, u32[]{:S(2)}, u32[]{:S(2)}) collective-permute-start(bf16[64,4096]{1,0:T(8,128)(2,1)S(1)} %collective-permute-done.72), channel_id=1, source_target_pairs={{0,4},{2,6},{8,0},{10,2},{16,8},{18,10},{24,16},{26,18},{28,24},{3... | collective-permute-start | bytes 1572872 | tf_op jit(solution)/shard_map/ppermute | solution.py:282
  233.1 53.0 %collective-permute-start.76 = (bf16[64,4096]{1,0:T(8,128)(2,1)S(1)}, bf16[64,4096]{1,0:T(8,128)(2,1)S(1)}, u32[]{:S(2)}, u32[]{:S(2)}) collective-permute-start(bf16[64,4096]{1,0:T(8,128)(2,1)S(1)} %copy-done.87), channel_id=1, source_target_pairs={{0,2},{2,0},{4,6},{6,4},{8,10},{10,8},{12,14},{14,12},{16,18},{18,... | collective-permute-start | bytes 1572872 | tf_op jit(solution)/shard_map/ppermute | solution.py:336
  241.2 47.1 %collective-permute-start.55 = (bf16[64,4096]{1,0:T(8,128)(2,1)S(1)}, bf16[64,4096]{1,0:T(8,128)(2,1)S(1)}, u32[]{:S(2)}, u32[]{:S(2)}) collective-permute-start(bf16[64,4096]{1,0:T(8,128)(2,1)S(1)} %copy-done.140), channel_id=1, source_target_pairs={{0,4},{2,6},{8,0},{10,2},{16,8},{18,10},{24,16},{26,18},{28,24},{3... | collective-permute-start | bytes 1572872 | tf_op jit(solution)/shard_map/ppermute | solution.py:282
  243.8 45.1 %collective-permute-start.5 = (bf16[64,4096]{1,0:T(8,128)(2,1)S(1)}, bf16[64,4096]{1,0:T(8,128)(2,1)S(1)}, u32[]{:S(2)}, u32[]{:S(2)}) collective-permute-start(bf16[64,4096]{1,0:T(8,128)(2,1)S(1)} %copy-done.141), channel_id=1, source_target_pairs={{0,4},{2,6},{8,0},{10,2},{16,8},{18,10},{24,16},{26,18},{28,24},{3... | collective-permute-start | bytes 1572872 | tf_op jit(solution)/shard_map/ppermute | solution.py:282
  287.5 81.3 %collective-permute-start.59 = (bf16[64,4096]{1,0:T(8,128)(2,1)S(1)}, bf16[64,4096]{1,0:T(8,128)(2,1)S(1)}, u32[]{:S(2)}, u32[]{:S(2)}) collective-permute-start(bf16[64,4096]{1,0:T(8,128)(2,1)S(1)} %copy-done.140), channel_id=1, source_target_pairs={{0,2},{2,0},{4,6},{6,4},{8,10},{10,8},{12,14},{14,12},{16,18},{18,... | collective-permute-start | bytes 1572872 | tf_op jit(solution)/shard_map/ppermute | solution.py:328
  296.0 77.5 %collective-permute-start.9 = (bf16[64,4096]{1,0:T(8,128)(2,1)S(1)}, bf16[64,4096]{1,0:T(8,128)(2,1)S(1)}, u32[]{:S(2)}, u32[]{:S(2)}) collective-permute-start(bf16[64,4096]{1,0:T(8,128)(2,1)S(1)} %copy-done.141), channel_id=1, source_target_pairs={{0,2},{2,0},{4,6},{6,4},{8,10},{10,8},{12,14},{14,12},{16,18},{18,... | collective-permute-start | bytes 1572872 | tf_op jit(solution)/shard_map/ppermute | solution.py:328
  328.8 163.3 %collective-permute-start.42 = (bf16[64,4096]{1,0:T(8,128)(2,1)}, bf16[64,4096]{1,0:T(8,128)(2,1)S(1)}, u32[]{:S(2)}, u32[]{:S(2)}) collective-permute-start(bf16[64,4096]{1,0:T(8,128)(2,1)} %collective-permute-done.34), channel_id=1, source_target_pairs={{0,2},{2,0},{4,6},{6,4},{8,10},{10,8},{12,14},{14,12},{16,18},{18,... | collective-permute-start | bytes 1572872 | tf_op jit(solution)/shard_map/ppermute | solution.py:337
  338.3 165.0 %collective-permute-start.33 = (bf16[64,4096]{1,0:T(8,128)(2,1)}, bf16[64,4096]{1,0:T(8,128)(2,1)S(1)}, u32[]{:S(2)}, u32[]{:S(2)}) collective-permute-start(bf16[64,4096]{1,0:T(8,128)(2,1)} %collective-permute-done.22), channel_id=1, source_target_pairs={{0,2},{2,0},{4,6},{6,4},{8,10},{10,8},{12,14},{14,12},{16,18},{18,... | collective-permute-start | bytes 1572872 | tf_op jit(solution)/shard_map/ppermute | solution.py:336
  362.3 128.2 %collective-permute-start.41 = (bf16[64,4096]{1,0:T(8,128)(2,1)}, bf16[64,4096]{1,0:T(8,128)(2,1)}, u32[]{:S(2)}, u32[]{:S(2)}) collective-permute-start(bf16[64,4096]{1,0:T(8,128)(2,1)} %collective-permute-done.22), channel_id=1, source_target_pairs={{0,1},{1,0},{2,3},{3,2},{4,5},{5,4},{6,7},{7,6},{8,9},{9,8},{10,11... | collective-permute-start | bytes 1572872 | tf_op jit(solution)/shard_map/ppermute | solution.py:314
  490.4 65.8 %collective-permute-start.66 = (bf16[64,4096]{1,0:T(8,128)(2,1)S(1)}, bf16[64,4096]{1,0:T(8,128)(2,1)S(1)}, u32[]{:S(2)}, u32[]{:S(2)}) collective-permute-start(bf16[64,4096]{1,0:T(8,128)(2,1)S(1)} %collective-permute-done.55), channel_id=1, source_target_pairs={{0,2},{2,0},{4,6},{6,4},{8,10},{10,8},{12,14},{14,12},{16,18},{18,... | collective-permute-start | bytes 1572872 | tf_op jit(solution)/shard_map/ppermute | solution.py:328
  501.3 62.8 %collective-permute-start.49 = (bf16[64,4096]{1,0:T(8,128)(2,1)}, bf16[64,4096]{1,0:T(8,128)(2,1)}, u32[]{:S(2)}, u32[]{:S(2)}) collective-permute-start(bf16[64,4096]{1,0:T(8,128)(2,1)} %collective-permute-done.41), channel_id=1, source_target_pairs={{0,2},{2,0},{4,6},{6,4},{8,10},{10,8},{12,14},{14,12},{16,18},{18,... | collective-permute-start | bytes 1572872 | tf_op jit(solution)/shard_map/ppermute | solution.py:337
  503.3 77.7 %collective-permute-start.99 = (bf16[64,4096]{1,0:T(8,128)(2,1)S(1)}, bf16[64,4096]{1,0:T(8,128)(2,1)}, u32[]{:S(2)}, u32[]{:S(2)}) collective-permute-start(bf16[64,4096]{1,0:T(8,128)(2,1)S(1)} %collective-permute-done.91), channel_id=1, source_target_pairs={{0,2},{2,0},{4,6},{6,4},{8,10},{10,8},{12,14},{14,12},{16,18},{18,... | collective-permute-start | bytes 1572872 | tf_op jit(solution)/shard_map/ppermute | solution.py:337
  511.9 43.4 %collective-permute-start.65 = (bf16[64,4096]{1,0:T(8,128)(2,1)S(1)}, bf16[64,4096]{1,0:T(8,128)(2,1)S(1)}, u32[]{:S(2)}, u32[]{:S(2)}) collective-permute-start(bf16[64,4096]{1,0:T(8,128)(2,1)S(1)} %collective-permute-done.56), channel_id=1, source_target_pairs={{0,2},{2,0},{4,6},{6,4},{8,10},{10,8},{12,14},{14,12},{16,18},{18,... | collective-permute-start | bytes 1572872 | tf_op jit(solution)/shard_map/ppermute | solution.py:328
  513.0 39.1 %collective-permute-start.63 = (bf16[64,4096]{1,0:T(8,128)(2,1)S(1)}, bf16[64,4096]{1,0:T(8,128)(2,1)S(1)}, u32[]{:S(2)}, u32[]{:S(2)}) collective-permute-start(bf16[64,4096]{1,0:T(8,128)(2,1)S(1)} %constant_dynamic-update-slice_fusion.127), channel_id=1, source_target_pairs={{0,2},{2,0},{4,6},{6,4},{8,10},{10,8},{12,14},{14,12},{16,18},{18,... | collective-permute-start | bytes 1572872 | tf_op jit(solution)/shard_map/ppermute | solution.py:328
  733.0 119.4 %collective-permute-start.150 = (bf16[512,1024]{1,0:T(8,128)(2,1)}, bf16[512,1024]{1,0:T(8,128)(2,1)}, u32[]{:S(2)}, u32[]{:S(2)}) collective-permute-start(bf16[512,1024]{1,0:T(8,128)(2,1)} %convolution_convert_fusion.10), channel_id=1, source_target_pairs={{0,2},{2,0},{4,6},{6,4},{8,10},{10,8},{12,14},{14,12},{16,18},{18,... | collective-permute-start | bytes 3145736 | tf_op jit(solution)/shard_map/ppermute | solution.py:359
  733.0 147.1 %collective-permute-start.121 = (bf16[512,1024]{1,0:T(8,128)(2,1)}, bf16[512,1024]{1,0:T(8,128)(2,1)}, u32[]{:S(2)}, u32[]{:S(2)}) collective-permute-start(bf16[512,1024]{1,0:T(8,128)(2,1)} %convolution_convert_fusion.12), channel_id=1, source_target_pairs={{0,2},{2,0},{4,6},{6,4},{8,10},{10,8},{12,14},{14,12},{16,18},{18,... | collective-permute-start | bytes 3145736 | tf_op jit(solution)/shard_map/ppermute | solution.py:359
  736.5 36.2 %collective-permute-start.100 = (bf16[512,1024]{0,1:T(8,128)(2,1)}, bf16[512,1024]{0,1:T(8,128)(2,1)}, u32[]{:S(2)}, u32[]{:S(2)}) collective-permute-start(bf16[512,1024]{0,1:T(8,128)(2,1)} %fusion.72), channel_id=1, source_target_pairs={{1,0},{3,2},{5,4},{7,6},{9,8},{11,10},{13,12},{15,14},{17,16},{19,... | collective-permute-start | bytes 3145736 | tf_op jit(solution)/shard_map/ppermute | solution.py:496
  738.9 224.4 %collective-permute-start.194 = (bf16[512,2048]{1,0:T(8,128)(2,1)}, bf16[512,2048]{1,0:T(8,128)(2,1)}, u32[]{:S(2)}, u32[]{:S(2)}) collective-permute-start(bf16[512,2048]{1,0:T(8,128)(2,1)} %convolution_convert_fusion), channel_id=1, source_target_pairs={{0,2},{2,0},{4,6},{6,4},{8,10},{10,8},{12,14},{14,12},{16,18},{18,... | collective-permute-start | bytes 6291464 | tf_op jit(solution)/shard_map/ppermute | solution.py:359
  739.0 230.3 %collective-permute-start.172 = (bf16[512,2048]{1,0:T(8,128)(2,1)}, bf16[512,2048]{1,0:T(8,128)(2,1)}, u32[]{:S(2)}, u32[]{:S(2)}) collective-permute-start(bf16[512,2048]{1,0:T(8,128)(2,1)} %convolution_convert_fusion.4), channel_id=1, source_target_pairs={{0,2},{2,0},{4,6},{6,4},{8,10},{10,8},{12,14},{14,12},{16,18},{18,... | collective-permute-start | bytes 6291464 | tf_op jit(solution)/shard_map/ppermute | solution.py:359
  772.7 185.7 %collective-permute-start.130 = (bf16[512,2048]{1,0:T(8,128)(2,1)}, bf16[512,2048]{1,0:T(8,128)(2,1)}, u32[]{:S(2)}, u32[]{:S(2)}) collective-permute-start(bf16[512,2048]{1,0:T(8,128)(2,1)} %add_convert_fusion.15), channel_id=1, source_target_pairs={{0,2},{2,0},{4,6},{6,4},{8,10},{10,8},{12,14},{14,12},{16,18},{18,... | collective-permute-start | bytes 6291464 | tf_op jit(solution)/shard_map/ppermute | solution.py:359
  856.0 34.5 %collective-permute-start.151 = (bf16[32,1024]{1,0:T(8,128)(2,1)}, bf16[32,1024]{1,0:T(8,128)(2,1)}, u32[]{:S(2)}, u32[]{:S(2)}) collective-permute-start(bf16[32,1024]{1,0:T(8,128)(2,1)} %get-tuple-element.169), channel_id=1, source_target_pairs={{0,8},{2,10},{8,16},{10,18},{16,24},{18,26},{24,28},{26,30},{28,20... | collective-permute-start | bytes 196616 | tf_op jit(solution)/shard_map/ppermute | solution.py:295
  946.2 323.0 %collective-permute-start.193 = (bf16[512,2048]{1,0:T(8,128)(2,1)}, bf16[512,2048]{1,0:T(8,128)(2,1)}, u32[]{:S(2)}, u32[]{:S(2)}) collective-permute-start(bf16[512,2048]{1,0:T(8,128)(2,1)} %convolution_convert_fusion.1), channel_id=1, source_target_pairs={{0,2},{2,0},{4,6},{6,4},{8,10},{10,8},{12,14},{14,12},{16,18},{18,... | collective-permute-start | bytes 6291464 | tf_op jit(solution)/shard_map/ppermute | solution.py:359
  958.3 58.9 %collective-permute-start.102 = (bf16[512,1024]{1,0:T(8,128)(2,1)}, bf16[512,1024]{1,0:T(8,128)(2,1)}, u32[]{:S(2)}, u32[]{:S(2)}) collective-permute-start(bf16[512,1024]{1,0:T(8,128)(2,1)} %convolution_convert_fusion.13), channel_id=1, source_target_pairs={{0,2},{2,0},{4,6},{6,4},{8,10},{10,8},{12,14},{14,12},{16,18},{18,... | collective-permute-start | bytes 3145736 | tf_op jit(solution)/shard_map/ppermute | solution.py:359
  969.3 242.3 %collective-permute-start.183 = (bf16[512,2048]{1,0:T(8,128)(2,1)}, bf16[512,2048]{1,0:T(8,128)(2,1)}, u32[]{:S(2)}, u32[]{:S(2)}) collective-permute-start(bf16[512,2048]{1,0:T(8,128)(2,1)} %convolution_convert_fusion.2), channel_id=1, source_target_pairs={{0,2},{2,0},{4,6},{6,4},{8,10},{10,8},{12,14},{14,12},{16,18},{18,... | collective-permute-start | bytes 6291464 | tf_op jit(solution)/shard_map/ppermute | solution.py:359
  974.5 164.9 %collective-permute-start.131 = (bf16[32,2048]{1,0:T(8,128)(2,1)}, bf16[32,2048]{1,0:T(8,128)(2,1)}, u32[]{:S(2)}, u32[]{:S(2)}) collective-permute-start(bf16[32,2048]{1,0:T(8,128)(2,1)} %get-tuple-element.161), channel_id=1, source_target_pairs={{0,8},{2,10},{8,16},{10,18},{16,24},{18,26},{24,28},{26,30},{28,20... | collective-permute-start | bytes 393224 | tf_op jit(solution)/shard_map/ppermute | solution.py:295
  990.7 141.0 %collective-permute-start.141 = (bf16[32,1024]{1,0:T(8,128)(2,1)}, bf16[32,1024]{1,0:T(8,128)(2,1)}, u32[]{:S(2)}, u32[]{:S(2)}) collective-permute-start(bf16[32,1024]{1,0:T(8,128)(2,1)} %get-tuple-element.165), channel_id=1, source_target_pairs={{0,8},{2,10},{8,16},{10,18},{16,24},{18,26},{24,28},{26,30},{28,20... | collective-permute-start | bytes 196616 | tf_op jit(solution)/shard_map/ppermute | solution.py:295
  1017.2 135.6 %collective-permute-start.145 = (bf16[32,1024]{1,0:T(8,128)(2,1)}, bf16[32,1024]{1,0:T(8,128)(2,1)}, u32[]{:S(2)}, u32[]{:S(2)}) collective-permute-start(bf16[32,1024]{1,0:T(8,128)(2,1)} %get-tuple-element.166), channel_id=1, source_target_pairs={{0,4},{2,6},{8,0},{10,2},{16,8},{18,10},{24,16},{26,18},{28,24},{3... | collective-permute-start | bytes 196616 | tf_op jit(solution)/shard_map/ppermute | solution.py:296
  1158.5 51.7 %collective-permute-start.111 = (bf16[512,2048]{1,0:T(8,128)(2,1)}, bf16[512,2048]{1,0:T(8,128)(2,1)S(1)}, u32[]{:S(2)}, u32[]{:S(2)}) collective-permute-start(bf16[512,2048]{1,0:T(8,128)(2,1)} %add_convert_fusion.17), channel_id=1, source_target_pairs={{0,2},{2,0},{4,6},{6,4},{8,10},{10,8},{12,14},{14,12},{16,18},{18,... | collective-permute-start | bytes 6291464 | tf_op jit(solution)/shard_map/ppermute | solution.py:359
  1196.5 50.0 %collective-permute-start.161 = (bf16[512,2048]{1,0:T(8,128)(2,1)}, bf16[512,2048]{1,0:T(8,128)(2,1)}, u32[]{:S(2)}, u32[]{:S(2)}) collective-permute-start(bf16[512,2048]{1,0:T(8,128)(2,1)} %convolution_convert_fusion.6), channel_id=1, source_target_pairs={{0,2},{2,0},{4,6},{6,4},{8,10},{10,8},{12,14},{14,12},{16,18},{18,... | collective-permute-start | bytes 6291464 | tf_op jit(solution)/shard_map/ppermute | solution.py:359
  1208.4 61.4 %collective-permute-start.195 = (bf16[512,2048]{1,0:T(8,128)(2,1)}, bf16[512,2048]{1,0:T(8,128)(2,1)}, u32[]{:S(2)}, u32[]{:S(2)}) collective-permute-start(bf16[512,2048]{1,0:T(8,128)(2,1)} %add_convert_fusion.3), channel_id=1, source_target_pairs={{0,1},{1,0},{2,3},{3,2},{4,5},{5,4},{6,7},{7,6},{8,9},{9,8},{10,11... | collective-permute-start | bytes 6291464 | tf_op jit(solution)/shard_map/ppermute | solution.py:314
  1240.3 35.0 %collective-permute-start.171 = (bf16[512,2048]{1,0:T(8,128)(2,1)}, bf16[512,2048]{1,0:T(8,128)(2,1)S(1)}, u32[]{:S(2)}, u32[]{:S(2)}) collective-permute-start(bf16[512,2048]{1,0:T(8,128)(2,1)} %convolution_convert_fusion.5), channel_id=1, source_target_pairs={{0,2},{2,0},{4,6},{6,4},{8,10},{10,8},{12,14},{14,12},{16,18},{18,... | collective-permute-start | bytes 6291464 | tf_op jit(solution)/shard_map/ppermute | solution.py:359
  1246.5 59.8 %collective-permute-start.173 = (bf16[512,2048]{1,0:T(8,128)(2,1)}, bf16[512,2048]{1,0:T(8,128)(2,1)S(1)}, u32[]{:S(2)}, u32[]{:S(2)}) collective-permute-start(bf16[512,2048]{1,0:T(8,128)(2,1)} %add_convert_fusion.9), channel_id=1, source_target_pairs={{0,1},{1,0},{2,3},{3,2},{4,5},{5,4},{6,7},{7,6},{8,9},{9,8},{10,11... | collective-permute-start | bytes 6291464 | tf_op jit(solution)/shard_map/ppermute | solution.py:314
  1268.1 116.7 %collective-permute-start.182 = (bf16[512,2048]{1,0:T(8,128)(2,1)}, bf16[512,2048]{1,0:T(8,128)(2,1)}, u32[]{:S(2)}, u32[]{:S(2)}) collective-permute-start(bf16[512,2048]{1,0:T(8,128)(2,1)} %convolution_convert_fusion.3), channel_id=1, source_target_pairs={{0,2},{2,0},{4,6},{6,4},{8,10},{10,8},{12,14},{14,12},{16,18},{18,... | collective-permute-start | bytes 6291464 | tf_op jit(solution)/shard_map/ppermute | solution.py:359
  1269.2 121.0 %collective-permute-start.160 = (bf16[512,2048]{1,0:T(8,128)(2,1)}, bf16[512,2048]{1,0:T(8,128)(2,1)}, u32[]{:S(2)}, u32[]{:S(2)}) collective-permute-start(bf16[512,2048]{1,0:T(8,128)(2,1)} %convolution_convert_fusion.7), channel_id=1, source_target_pairs={{0,2},{2,0},{4,6},{6,4},{8,10},{10,8},{12,14},{14,12},{16,18},{18,... | collective-permute-start | bytes 6291464 | tf_op jit(solution)/shard_map/ppermute | solution.py:359
  1269.8 116.6 %collective-permute-start.184 = (bf16[512,2048]{1,0:T(8,128)(2,1)}, bf16[512,2048]{1,0:T(8,128)(2,1)}, u32[]{:S(2)}, u32[]{:S(2)}) collective-permute-start(bf16[512,2048]{1,0:T(8,128)(2,1)} %add_convert_fusion.6), channel_id=1, source_target_pairs={{0,1},{1,0},{2,3},{3,2},{4,5},{5,4},{6,7},{7,6},{8,9},{9,8},{10,11... | collective-permute-start | bytes 6291464 | tf_op jit(solution)/shard_map/ppermute | solution.py:314
  1275.3 56.0 %collective-permute-start.115 = (bf16[64,2048]{1,0:T(8,128)(2,1)S(1)}, bf16[64,2048]{1,0:T(8,128)(2,1)S(1)}, u32[]{:S(2)}, u32[]{:S(2)}) collective-permute-start(bf16[64,2048]{1,0:T(8,128)(2,1)S(1)} %get-tuple-element.155), channel_id=1, source_target_pairs={{0,8},{2,10},{8,16},{10,18},{16,24},{18,26},{24,28},{26,30},{28,20... | collective-permute-start | bytes 786440 | tf_op jit(solution)/shard_map/ppermute | solution.py:301
  1361.1 43.5 %collective-permute-start.162 = (bf16[512,2048]{1,0:T(8,128)(2,1)S(1)}, bf16[512,2048]{1,0:T(8,128)(2,1)S(1)}, u32[]{:S(2)}, u32[]{:S(2)}) collective-permute-start(bf16[512,2048]{1,0:T(8,128)(2,1)S(1)} %copy-done.166), channel_id=1, source_target_pairs={{0,1},{1,0},{2,3},{3,2},{4,5},{5,4},{6,7},{7,6},{8,9},{9,8},{10,11... | collective-permute-start | bytes 6291464 | tf_op jit(solution)/shard_map/ppermute | solution.py:314
  1384.7 53.7 %collective-permute-start.177 = (bf16[64,2048]{1,0:T(8,128)(2,1)S(1)}, bf16[64,2048]{1,0:T(8,128)(2,1)S(1)}, u32[]{:S(2)}, u32[]{:S(2)}) collective-permute-start(bf16[64,2048]{1,0:T(8,128)(2,1)S(1)} %get-tuple-element.151), channel_id=1, source_target_pairs={{0,8},{2,10},{8,16},{10,18},{16,24},{18,26},{24,28},{26,30},{28,20... | collective-permute-start | bytes 786440 | tf_op jit(solution)/shard_map/ppermute | solution.py:301
  1409.7 39.0 %collective-permute-start.167 = (bf16[32,2048]{1,0:T(8,128)(2,1)S(1)}, bf16[32,2048]{1,0:T(8,128)(2,1)S(1)}, u32[]{:S(2)}, u32[]{:S(2)}) collective-permute-start(bf16[32,2048]{1,0:T(8,128)(2,1)S(1)} %get-tuple-element.150), channel_id=1, source_target_pairs={{0,4},{2,6},{8,0},{10,2},{16,8},{18,10},{24,16},{26,18},{28,24},{3... | collective-permute-start | bytes 393224 | tf_op jit(solution)/shard_map/ppermute | solution.py:296
  (354 other events, 6681.9 us)
Sparse Core Ops, SparseCore 0:
  1004.3 119.3 all-reduce.25

commit v2 on v1

--- a/solution.py
+++ b/solution.py
@@ -243,21 +243,14 @@
     return 0.5 * values * (1.0 + jnp.tanh(0.7978845608028654 * (values + 0.044715 * values * values * values)))
 
 
+MESH = pl.DeviceIdType.MESH
+
+
 class Ring:
     def __init__(self, devices):
         self.chips = devices // 2
         self.order = list(range(0, self.chips, 2)) + list(range(self.chips - 1, 0, -2))
         self.place = {chip: spot for spot, chip in enumerate(self.order)}
-        self.ahead = self.pairs(1)
-        self.behind = self.pairs(-1)
-        self.sibling = [(i, i ^ 1) for i in range(devices)]
-
-    def pairs(self, step):
-        return [
-            (2 * self.order[spot] + core, 2 * self.order[(spot + step) % self.chips] + core)
-            for spot in range(self.chips)
-            for core in range(2)
-        ]
 
     def owners(self):
         table = []
@@ -272,97 +265,396 @@
             )
         return np.array(table, np.int32)
 
-    def gather(self, block):
+    def spot_chip(self, spot):
         half = self.chips // 2
-        blocks = [None] * self.chips
-        blocks[0] = block
-        up = down = block
-        for hop in range(1, half):
-            up = lax.ppermute(up, "dp", self.ahead)
-            down = lax.ppermute(down, "dp", self.behind)
-            blocks[hop] = up
-            blocks[self.chips - hop] = down
-        middle = block.shape[0] // 2
-        blocks[half] = jnp.concatenate(
-            [lax.ppermute(up[:middle], "dp", self.ahead), lax.ppermute(down[middle:], "dp", self.behind)], axis=0
+        return jnp.where(spot < half, 2 * spot, 2 * (self.chips - 1 - spot) + 1)
+
+    def neighbours(self):
+        here, side = (lax.axis_index("dp"), lax.axis_index("tensor"))
+        chip, core = (here // 2, here % 2)
+        spot = jnp.where(chip % 2 == 0, chip // 2, self.chips - 1 - chip // 2)
+        ahead = self.spot_chip((spot + 1) % self.chips) * 2 + core
+        behind = self.spot_chip((spot + self.chips - 1) % self.chips) * 2 + core
+        sibling = chip * 2 + (1 - core)
+        return ((ahead, side), (behind, side), (sibling, side), (here, 1 - side))
+
+
+def greet(targets):
+    barrier = pltpu.get_barrier_semaphore()
+    for target in targets:
+        pl.semaphore_signal(barrier, inc=1, device_id=target, device_id_type=MESH)
+    pl.semaphore_wait(barrier, len(targets))
+
+
+class Copies:
+    def __init__(self, send, recv, near):
+        self.send, self.recv, self.near = (send, recv, near)
+        self.sent, self.moved = ([], [])
+
+    def push(self, source, target, device):
+        spot = len(self.sent)
+        copy = pltpu.make_async_remote_copy(
+            src_ref=source,
+            dst_ref=target,
+            send_sem=self.send.at[spot],
+            recv_sem=self.recv.at[spot],
+            device_id=device,
+            device_id_type=MESH,
         )
-        return blocks
-
-    def scatter(self, parts):
-        half = self.chips // 2
-        middle = parts[0].shape[0] // 2
-        low = jnp.bfloat16
-        up = lax.ppermute(parts[half][middle:].astype(low), "dp", self.ahead)
-        down = lax.ppermute(parts[half][:middle].astype(low), "dp", self.behind)
-        zeros = jnp.zeros_like(up)
-        up = jnp.concatenate([zeros, up], axis=0)
-        down = jnp.concatenate([down, zeros], axis=0)
-        for hop in range(half - 1, 0, -1):
-            up = lax.ppermute(wide_sum(parts[self.chips - hop], up).astype(low), "dp", self.ahead)
-            down = lax.ppermute(wide_sum(parts[hop], down).astype(low), "dp", self.behind)
-        return wide_sum(wide_sum(parts[0], up), down)
+        copy.start()
+        self.sent.append(copy)
+        return copy
+
+    def move(self, source, target):
+        copy = pltpu.make_async_copy(source, target, self.near.at[len(self.moved)])
+        copy.start()
+        self.moved.append(copy)
+        return copy
+
+    def finish(self):
+        for copy in self.sent:
+            copy.wait_send()
+
+
+def run_all(steps):
+    for unused in steps:
+        pass
+
+
+def gather_steps(copies, ids, chips, arrays):
+    ahead, behind, sibling, across = ids
+    half = chips // 2
+    local, siblings, early_in, late_in, up, down = ([], [], [], [], {}, {})
+    for shard, own, other, early in arrays:
+        early_in.append(copies.push(shard.at[:, pl.ds(0, early)], other.at[0, 0, :, pl.ds(0, early)], across))
+    for i, (shard, own, other, early) in enumerate(arrays):
+        local.append(copies.move(shard, own.at[0, 0]))
+        up[i, 1] = [copies.push(shard, own.at[0, 1], ahead)]
+        down[i, 1] = [copies.push(shard, own.at[0, chips - 1], behind)]
+        siblings.append(copies.push(shard, own.at[1, 0], sibling))
+    for shard, own, other, early in arrays:
+        width = shard.shape[1] - early
+        late_in.append(copies.push(shard.at[:, pl.ds(early, width)], other.at[0, 0, :, pl.ds(early, width)], across))
+    yield
+    for i, (shard, own, other, early) in enumerate(arrays):
+        early_in[i].wait_recv()
+        part = other.at[0, 0, :, pl.ds(0, early)]
+        up[i, 1].append(copies.push(part, other.at[0, 1, :, pl.ds(0, early)], ahead))
+        down[i, 1].append(copies.push(part, other.at[0, chips - 1, :, pl.ds(0, early)], behind))
+    late = [(0, late_in)]
+    for hop in range(1, half + 1):
+        yield
+        spots = [(hop, up, ahead), (chips - hop, down, behind)]
+        crossing = {}
+        if hop < half:
+            for spot, arrivals, target in spots:
+                crossing[spot] = []
+                step = 1 if target is ahead else -1
+                for i, (shard, own, other, early) in enumerate(arrays):
+                    size = shard.shape[1]
+                    arrivals[i, hop][0].wait_recv()
+                    if hop + 1 < half:
+                        window, slim = (pl.ds(0, size), pl.ds(0, early))
+                    elif step == 1:
+                        window, slim = (pl.ds(0, size // 2), pl.ds(0, early // 2))
+                    else:
+                        window, slim = (pl.ds(size // 2, size // 2), pl.ds(early // 2, early // 2))
+                    arrivals[i, hop + 1] = [
+                        copies.push(own.at[0, spot, :, window], own.at[0, spot + step, :, window], target)
+                    ]
+                    rest = pl.ds(early, size - early)
+                    crossing[spot].append(copies.push(own.at[0, spot, :, rest], other.at[0, spot, :, rest], across))
+                    siblings.append(copies.push(own.at[0, spot], own.at[1, spot], sibling))
+                    arrivals[i, hop][1].wait_recv()
+                    arrivals[i, hop + 1].append(
+                        copies.push(other.at[0, spot, :, slim], other.at[0, spot + step, :, slim], target)
+                    )
+        else:
+            crossing[half] = []
+            for i, (shard, own, other, early) in enumerate(arrays):
+                up[i, half][0].wait_recv()
+                down[i, half][0].wait_recv()
+                rest = pl.ds(early, shard.shape[1] - early)
+                crossing[half].append(copies.push(own.at[0, half, :, rest], other.at[0, half, :, rest], across))
+                siblings.append(copies.push(own.at[0, half], own.at[1, half], sibling))
+                up[i, half][1].wait_recv()
+                down[i, half][1].wait_recv()
+        for spot, arrivals in late:
+            for i, (shard, own, other, early) in enumerate(arrays):
+                arrivals[i].wait_recv()
+                siblings.append(copies.push(other.at[0, spot], other.at[1, spot], sibling))
+        late = list(crossing.items())
+    yield
+    for spot, arrivals in late:
+        for i, (shard, own, other, early) in enumerate(arrays):
+            arrivals[i].wait_recv()
+            siblings.append(copies.push(other.at[0, spot], other.at[1, spot], sibling))
+    for copy in local:
+        copy.wait()
+    yield
+    for copy in siblings:
+        copy.wait_recv()
+
+
+def gather_count(chips, arrays):
+    half = chips // 2
+    return arrays * (5 + 2 + (half - 1) * 2 * 4 + 2 + chips)
+
+
+def gather_weights(ring, groups, collective):
+    flat = [member for group in groups for member in group]
+    count = sum(gather_count(ring.chips, len(group)) for group in groups)
+    shapes = [
+        jax.ShapeDtypeStruct((2, ring.chips) + shard.shape, shard.dtype) for shard, early in flat for unused in range(2)
+    ]
+
+    def kernel(*refs):
+        shards, outs = (refs[: len(flat)], refs[len(flat) : 3 * len(flat)])
+        ids = ring.neighbours()
+        greet(ids)
+        copies = Copies(*refs[3 * len(flat) :])
+        members = [(shards[i], outs[2 * i], outs[2 * i + 1], flat[i][1]) for i in range(len(flat))]
+        at = 0
+        running = []
+        for group in groups:
+            running.append(gather_steps(copies, ids, ring.chips, members[at : at + len(group)]))
+            at += len(group)
+        run_staggered(running, 3)
+        copies.finish()
+
+    outs = pl.pallas_call(
+        kernel,
+        in_specs=[pl.BlockSpec(memory_space=pl.ANY)] * len(flat),
+        out_specs=[pl.BlockSpec(memory_space=pl.ANY)] * len(shapes),
+        out_shape=shapes,
+        scratch_shapes=[
+            pltpu.SemaphoreType.DMA((count,)),
+            pltpu.SemaphoreType.DMA((count,)),
+            pltpu.SemaphoreType.DMA((len(flat),)),
+        ],
+        compiler_params=pltpu.CompilerParams(collective_id=collective, has_side_effects=True),
+        name="gather_weights",
+    )(*[shard for shard, early in flat])
+    return [out.reshape(-1, out.shape[-1]) for out in outs]
+
+
+def run_staggered(running, lead):
+    waiting = list(running)
+    active = []
+    youngest = lead
+    while waiting or active:
+        if waiting and youngest >= lead:
+            active.append(waiting.pop(0))
+            youngest = 0
+        youngest += 1
+        for steps in list(active):
+            try:
+                next(steps)
+            except StopIteration:
+                active.remove(steps)
+
+
+def add_rows(target, source):
+    rows, columns = target.shape
+    step = 256 if columns % 256 == 0 else 128
+
+    @pl.loop(0, columns // step)
+    def tile(i):
+        window = pl.ds(pl.multiple_of(i * step, step), step)
+        target[:, window] = (target[:, window].astype(jnp.float32) + source[:, window].astype(jnp.float32)).astype(
+            target.dtype
+        )
+
+
+def scatter_steps(copies, ids, chips, arrays):
+    ahead, behind, sibling, across = ids
+    half = chips // 2
+    blocks = [half] + [spot for hop in range(half - 1, 0, -1) for spot in (chips - hop, hop)] + [0]
+    loaded, near = ({}, {})
+    for spot in blocks:
+        for i, (parts, early, out, room) in enumerate(arrays):
+            for e in range(2):
+                near[i, e, spot] = copies.push(parts[e][1].at[spot], room["near"].at[e, spot], sibling)
+                loaded[i, e, spot] = copies.move(parts[e][0].at[spot], room["sum"].at[e, spot])
+    crossed = {}
+
+    def first(spot):
+        for e in (1, 0):
+            for i, (parts, early, out, room) in enumerate(arrays):
+                loaded[i, e, spot].wait()
+                near[i, e, spot].wait_recv()
+                add_rows(room["sum"].at[e, spot], room["near"].at[e, spot])
+                if e == 1:
+                    rest = pl.ds(early, out.shape[1] - early)
+                    crossed[i, spot] = copies.push(room["sum"].at[1, spot, :, rest], room["far"].at[spot], across)
+
+    def second(spot):
+        for i, (parts, early, out, room) in enumerate(arrays):
+            rest = pl.ds(early, out.shape[1] - early)
+            crossed[i, spot].wait_recv()
+            add_rows(room["sum"].at[0, spot, :, rest], room["far"].at[spot])
+
+    def windows(size, hop, upward):
+        if hop > 0:
+            return pl.ds(0, size)
+        return pl.ds(size // 2, size // 2) if upward else pl.ds(0, size // 2)
+
+    def send(hop, spot, upward):
+        target = ahead if upward else behind
+        kinds = ("up", "up_slim") if upward else ("down", "down_slim")
+        out_copies = []
+        for i, (parts, early, out, room) in enumerate(arrays):
+            for e, size in ((0, out.shape[1]), (1, early)):
+                window = windows(size, hop, upward)
+                out_copies.append(
+                    copies.push(room["sum"].at[e, spot, :, window], room[kinds[e]].at[hop, :, window], target)
+                )
+        return out_copies
+
+    def receive(hop, spot, upward, arrivals):
+        kinds = ("up", "up_slim") if upward else ("down", "down_slim")
+        at = 0
+        for i, (parts, early, out, room) in enumerate(arrays):
+            for e, size in ((0, out.shape[1]), (1, early)):
+                window = windows(size, hop, upward)
+                arrivals[at].wait_recv()
+                add_rows(room["sum"].at[e, spot, :, window], room[kinds[e]].at[hop, :, window])
+                at += 1
+
+    yield
+    first(half)
+    yield
+    for spot in blocks[1:3]:
+        first(spot)
+    second(half)
+    up = send(0, half, True)
+    down = send(0, half, False)
+    for hop in range(1, half):
+        yield
+        for spot in blocks[2 * hop + 1 : 2 * hop + 3]:
+            first(spot)
+        second(chips - half + hop)
+        second(half - hop)
+        receive(hop - 1, chips - half + hop, True, up)
+        up = send(hop, chips - half + hop, True)
+        receive(hop - 1, half - hop, False, down)
+        down = send(hop, half - hop, False)
+    yield
+    second(0)
+    yield
+    final = []
+    at = 0
+    for i, (parts, early, out, room) in enumerate(arrays):
+        for e in range(2):
+            up[at].wait_recv()
+            down[at].wait_recv()
+            at += 1
+        size = out.shape[1]
+        part = room["sum"][1, 0, :, :early].astype(jnp.float32)
+        part = part + room["up_slim"][half - 1].astype(jnp.float32) + room["down_slim"][half - 1].astype(jnp.float32)
+        room["slim_out"][...] = part.astype(room["slim_out"].dtype)
+        final.append(copies.push(room["slim_out"], room["slim_in"], across))
+    yield
+    for i, (parts, early, out, room) in enumerate(arrays):
+        total = room["sum"][0, 0].astype(jnp.float32) + room["up"][half - 1].astype(jnp.float32)
+        out[...] = total + room["down"][half - 1].astype(jnp.float32)
+        final[i].wait_recv()
+        out[:, :early] += room["slim_in"][...].astype(jnp.float32)
+
+
+def scatter_count(chips, arrays):
+    half = chips // 2
+    return arrays * (2 * chips + chips + half * 4 + 1)
+
+
+ROOM = ("sum", "near", "far", "up", "down", "up_slim", "down_slim", "slim_out", "slim_in")
+
+
+def scatter_room(chips, rows, columns, early, dtype):
+    half = chips // 2
+    shapes = (
+        (2, chips, rows, columns),
+        (2, chips, rows, columns),
+        (chips, rows, columns - early),
+        (half, rows, columns),
+        (half, rows, columns),
+        (half, rows, early),
+        (half, rows, early),
+        (rows, early),
+        (rows, early),
+    )
+    return [pltpu.VMEM(shape, dtype) for shape in shapes]
+
+
+def scatter_grads(ring, arrays, collective):
+    chips = ring.chips
+    inputs, shapes, rooms = ([], [], [])
+    for parts, early in arrays:
+        height, columns = parts[0][0].shape
+        rows = height // chips
+        inputs += [parts[e][c].reshape(chips, rows, columns) for e in range(2) for c in range(2)]
+        shapes.append(jax.ShapeDtypeStruct((rows, columns), jnp.float32))
+        rooms += scatter_room(chips, rows, columns, early, parts[0][0].dtype)
+    total = len(arrays)
+
+    def kernel(*refs):
+        ins, outs, scratch = (refs[: 4 * total], refs[4 * total : 5 * total], refs[5 * total :])
+        ids = ring.neighbours()
+        greet(ids)
+        copies = Copies(*scratch[len(rooms) :])
+        members = []
+        for i in range(total):
+            parts = [[ins[4 * i + 2 * e + c] for c in range(2)] for e in range(2)]
+            room = dict(zip(ROOM, scratch[i * len(ROOM) : (i + 1) * len(ROOM)]))
+            members.append((parts, arrays[i][1], outs[i], room))
+        run_all(scatter_steps(copies, ids, chips, members))
+        copies.finish()
+
+    return pl.pallas_call(
+        kernel,
+        in_specs=[pl.BlockSpec(memory_space=pl.ANY)] * (4 * total),
+        out_specs=[pl.BlockSpec(memory_space=pltpu.VMEM)] * total,
+        out_shape=shapes,
+        scratch_shapes=rooms
+        + [
+            pltpu.SemaphoreType.DMA((scatter_count(chips, total),)),
+            pltpu.SemaphoreType.DMA((scatter_count(chips, total),)),
+            pltpu.SemaphoreType.DMA((2 * chips * total,)),
+        ],
+        compiler_params=pltpu.CompilerParams(
+            collective_id=collective, has_side_effects=True, vmem_limit_bytes=56 * 1024 * 1024
+        ),
+        name="scatter_grads",
+    )(*inputs)
 
 
 def wide_sum(left, right):
     return left.astype(jnp.float32) + right.astype(jnp.float32)
 
 
-SWAP = [(0, 1), (1, 0)]
-
-
-def swap(block):
-    return lax.ppermute(block, "tensor", SWAP)
-
-
-def rows_of(blocks, low, high):
-    return jnp.concatenate([block[:, low:high] for block in blocks], axis=0)
-
-
-def fetch_attention(ring, qkv_shard, out_shard):
-    rows = qkv_shard.shape[0]
-    own = jnp.concatenate([qkv_shard.reshape(rows, -1), out_shard.T], axis=1)
-    other = swap(own)
-    size = own.shape[1] // 4
-    both = [side[:, i * size : (i + 1) * size] for i in range(4) for side in (own, other)]
-    blocks = ring.gather(jnp.concatenate(both, axis=1))
-    blocks = blocks + [lax.ppermute(block, "dp", ring.sibling) for block in blocks]
-    return (rows_of(blocks, 0, 6 * size), rows_of(blocks, 6 * size, 8 * size))
-
-
-def fetch_mlp(ring, up_shard, down_shard):
-    size = up_shard.shape[1]
-    own = ring.gather(jnp.concatenate([up_shard, down_shard.T], axis=1))
-    other = [swap(block) for block in own]
-    own = own + [lax.ppermute(block, "dp", ring.sibling) for block in own]
-    other = other + [lax.ppermute(block, "dp", ring.sibling) for block in other]
-    return (
-        [rows_of(own, 0, size), rows_of(other, 0, size)],
-        [rows_of(own, size, 2 * size), rows_of(other, size, 2 * size)],
-    )
-
-
-def grad_rows(left, right, extra=None):
+def grad_parts(left, right, extra=None):
     half = left.shape[1] // 2
-
-    def product(part):
-        columns = slice(part * half, (part + 1) * half)
+    parts = []
+    for core in range(2):
+        columns = slice(core * half, (core + 1) * half)
         out = lax.dot_general(left[:, columns], right, ROWS_CONTRACT, preferred_element_type=jnp.float32)
         if extra is not None:
             more = lax.dot_general(extra[0][:, columns], extra[1], ROWS_CONTRACT, preferred_element_type=jnp.float32)
             out = out + more
-        return out
-
-    return product
-
-
-def sibling_sum(ring, product):
-    arrived = lax.ppermute(product(1).astype(jnp.bfloat16), "dp", ring.sibling)
-    return (product(0) + arrived.astype(jnp.float32)).astype(jnp.bfloat16)
-
-
-def ring_sum(ring, total):
-    rows = total.shape[0] // ring.chips
-    return ring.scatter([total[i * rows : (i + 1) * rows] for i in range(ring.chips)])
+        parts.append(out.astype(jnp.bfloat16))
+    return parts
+
+
+def small_parts(vector_grads, bias_grads, by_half, placed, piece, lane):
+    layers, dp = (len(vector_grads), placed.shape[0])
+    vectors = jnp.stack([vector_grads[layer][i] for i in range(6) for layer in range(layers)])
+    vectors = by_half(vectors.reshape(6 * layers, dp, 2, piece).transpose(2, 1, 0, 3), 0).reshape(2, dp, -1)
+    shifts = [jnp.stack([bias_grads[layer][i] for layer in range(layers)], axis=1) for i in range(2)]
+    shifts = jnp.concatenate([member.reshape(2, -1, dp, lane) for member in shifts], axis=1)
+    shifts = jnp.einsum("tndl,bd->tbnl", shifts, placed, precision=lax.Precision.HIGHEST).reshape(2, dp, -1)
+    packed = jnp.concatenate([vectors, shifts], axis=2)
+    packed = jnp.pad(packed, ((0, 0), (0, 0), (0, 8 * 512 - packed.shape[2]))).reshape(2, 2, -1, 512)
+    return [[packed[e, c] for c in range(2)] for e in range(2)]
 
 
 def local(
@@ -399,6 +691,8 @@
     columns = (owners[:, None] * rows + jnp.arange(rows, dtype=jnp.int32)[None]).reshape(1, width)
     to_ring = (jnp.arange(width, dtype=jnp.int32)[:, None] == columns).astype(low)
 
+    placed = (owners[:, None] == jnp.arange(dp, dtype=jnp.int32)[None]).astype(f32)
+
     def into_ring(values):
         return jnp.dot(values, to_ring, preferred_element_type=f32)
 
@@ -412,15 +706,26 @@
     packed = jnp.concatenate(
         [vectors.reshape(-1), qkv_bias.reshape(-1), up_bias.reshape(-1), jnp.stack([count // 256, count % 256]).astype(low)]
     )
-    everything = lax.all_gather(packed, ("dp", "tensor"), axis=0, tiled=False)
     first, second, third = (vectors.size, vectors.size + qkv_bias.size, vectors.size + qkv_bias.size + up_bias.size)
-    vectors = everything[:, :first].reshape(dp * tensor, 6 * layers, piece).transpose(1, 0, 2)
-    small = into_ring(vectors.reshape(6 * layers, width)).reshape(6, layers, 1, width)
-    qkv_add = everything[:, first:second].reshape((dp, tensor) + qkv_bias.shape).transpose(2, 3, 1, 4, 0, 5)
-    qkv_add = by_half(qkv_add, 2).reshape(layers, 1, 3 * width).astype(f32)
-    up_add = everything[:, second:third].reshape((dp, tensor) + up_bias.shape).transpose(2, 1, 3, 0, 4)
-    up_add = by_half(up_add, 1).reshape(layers, tensor, 1, -1).astype(f32)
-    counts = jnp.sum(everything[:, third:].astype(f32), axis=0)
+    packed = jnp.pad(packed, (0, 16 * 512 - packed.size)).reshape(16, 512)
+    groups = []
+    for layer in range(layers):
+        groups.append([(qkv_weight[layer].reshape(rows, -1), 512), (out_weight[layer].T, 256)])
+        groups.append([(up_weight[layer], 768), (down_weight[layer].T, 768)])
+    groups[0].insert(0, (packed, 256))
+    gathered = gather_weights(ring, groups, 1)
+    everything = by_half(jnp.stack([member.reshape(dp, -1) for member in gathered[:2]]), 0)
+    gathered = gathered[2:]
+    vectors = everything[:, :, :first].reshape(tensor, dp, 6, layers, piece).transpose(2, 3, 1, 0, 4)
+    small = vectors.reshape(6, layers, 1, width).astype(f32)
+    lane = qkv_bias.shape[3]
+    biases = everything[:, :, first:third].reshape(tensor, dp, -1, lane)
+    biases = jnp.einsum("tbnl,bd->tndl", biases, placed.astype(low), preferred_element_type=f32)
+    biases = by_half(biases.reshape(tensor, -1, dp * lane), 0)
+    split = (second - first) // lane
+    qkv_add = biases[:, :split].reshape(tensor, layers, 1, -1).transpose(1, 0, 2, 3)
+    up_add = biases[:, split:].reshape(tensor, layers, 1, -1).transpose(1, 0, 2, 3)
+    counts = jnp.sum(everything[:, :, third : third + 2].astype(f32), axis=(0, 1))
     valid_count = counts[0] * 256.0 + counts[1]
 
     scale = HD ** (-0.5)
@@ -431,28 +736,27 @@
     meta = jnp.stack([side.astype(jnp.int32), prefix_len[0]])
 
     before_first = lax.ppermute(states_in[0], "tensor", [(0, 1)])
-    attention = []
-    mlp = []
-    for layer in range(layers):
-        attention.append(fetch_attention(ring, qkv_weight[layer], out_weight[layer]))
-        mlp.append(fetch_mlp(ring, up_weight[layer], down_weight[layer]))
-
     states = into_ring(states_in[0])
     target = into_ring(teacher[0])
     kept = []
     for layer in range(layers):
-        qkv_proj, out_proj = attention[layer]
-        up_proj, down_proj = mlp[layer]
+        qkv_proj, out_proj, up_proj, down_proj = [gathered[8 * layer + i : 8 * layer + i + 2] for i in (0, 2, 4, 6)]
         normed = norm_rows(states, small[0][layer], small[1][layer]).astype(low)
         if layer == 0:
             normed_first = norm_rows(into_ring(before_first), small[0][layer], small[1][layer]).astype(low)
         else:
             normed_first = lax.ppermute(normed, "tensor", [(0, 1)])
-        qkv = (jnp.dot(normed, qkv_proj, preferred_element_type=f32) + qkv_add[layer]).astype(low)
-        kv_first = jnp.dot(normed_first, qkv_proj[:, width:], preferred_element_type=f32) + qkv_add[layer][:, width:]
-        kv_first = kv_first.astype(low)
-        heads_out, lse = attention_forward(meta, slopes, qkv, kv_first, scale)
-        middle = states + mm(heads_out, out_proj, NT) + small[2][layer]
+        qkv, kv_first, heads_out, lse = ([], [], [], [])
+        for i in range(tensor):
+            query = qkv_proj[i].shape[1] // 3
+            mixed = jnp.dot(normed, qkv_proj[i], preferred_element_type=f32) + qkv_add[layer][i]
+            qkv.append(mixed.astype(low))
+            mixed = jnp.dot(normed_first, qkv_proj[i][:, query:], preferred_element_type=f32)
+            kv_first.append((mixed + qkv_add[layer][i][:, query:]).astype(low))
+            made, total = attention_forward(meta, slopes[i * heads_half : (i + 1) * heads_half], qkv[i], kv_first[i], scale)
+            heads_out.append(made)
+            lse.append(total)
+        middle = states + mm(heads_out[0], out_proj[0], NT) + mm(heads_out[1], out_proj[1], NT) + small[2][layer]
         normed_two = norm_rows(middle, small[3][layer], small[4][layer]).astype(low)
         hidden = [jnp.dot(normed_two, up_proj[i], preferred_element_type=f32) + up_add[layer][i] for i in range(tensor)]
         active = [gelu_tanh(values).astype(low) for values in hidden]
@@ -467,61 +771,60 @@
     bias_grads = [None] * layers
     for layer in reversed(range(layers)):
         before, normed, normed_first, qkv, kv_first, lse, heads_out, middle, normed_two, hidden, active = kept[layer]
-        qkv_proj, out_proj = attention[layer]
-        up_proj, down_proj = mlp[layer]
+        qkv_proj, out_proj, up_proj, down_proj = [gathered[8 * layer + i : 8 * layer + i + 2] for i in (0, 2, 4, 6)]
         grad_mlp = grad.astype(low)
         down_shift = jnp.sum(grad_mlp.astype(f32), axis=0)
         grad_hidden = []
         for i in range(tensor):
             grad_active = jnp.dot(grad_mlp, down_proj[i], preferred_element_type=f32)
             grad_hidden.append(jax.vjp(gelu_tanh, hidden[i])[1](grad_active)[0].astype(low))
-        down_grads = [sibling_sum(ring, grad_rows(grad_mlp, active[i])) for i in range(tensor)]
-        down_grad = ring_sum(ring, wide_sum(down_grads[0], swap(down_grads[1])).astype(low))
+        down_parts = [grad_parts(grad_mlp, active[i]) for i in range(tensor)]
         up_shift = jnp.stack([jnp.sum(values.astype(f32), axis=0) for values in grad_hidden])
         grad_normed = mm(grad_hidden[0], up_proj[0], NT) + mm(grad_hidden[1], up_proj[1], NT)
-        up_grads = [sibling_sum(ring, grad_rows(normed_two, grad_hidden[i])) for i in range(tensor)]
-        up_grad = ring_sum(ring, wide_sum(up_grads[0], swap(up_grads[1])).astype(low))
+        up_parts = [grad_parts(normed_two, grad_hidden[i]) for i in range(tensor)]
+        up_grad, down_grad = scatter_grads(ring, [(up_parts, 768), (down_parts, 768)], 2 + 2 * layer)
         part, gain_two, shift_two = norm_back(middle, small[3][layer], grad_normed)
         grad_middle = grad + part
         grad_attn = grad_middle.astype(low)
         out_shift = jnp.sum(grad_attn.astype(f32), axis=0)
-        grad_heads = jnp.dot(grad_attn, out_proj, preferred_element_type=f32).astype(low)
-        out_grad = ring_sum(ring, sibling_sum(ring, grad_rows(grad_attn, heads_out)))
-        half = out_grad.shape[1] // 2
-        out_grad = wide_sum(out_grad[:, :half], swap(out_grad[:, half:].astype(low)))
-        grads = attention_backward(meta, slopes, qkv, kv_first, grad_heads, lse, scale)
-        grad_qkv = jnp.concatenate(grads[:3], axis=1)
-        grad_first = jnp.concatenate(grads[3:], axis=1)
-        sent = mm(grad_first, qkv_proj[:, width:], NT).astype(low)
-        arrived = lax.ppermute(sent, "tensor", [(1, 0)])
-        qkv_shift = jnp.sum(grad_qkv.astype(f32), axis=0)
-        first_shift = jnp.sum(grad_first.astype(f32), axis=0)
-        qkv_shift = qkv_shift + jnp.pad(first_shift, (width, 0))
-        query_grad = sibling_sum(ring, grad_rows(normed, grad_qkv[:, :width]))
-        rest_grad = sibling_sum(ring, grad_rows(normed, grad_qkv[:, width:], (normed_first, grad_first)))
-        qkv_grad = jnp.concatenate([ring_sum(ring, query_grad), ring_sum(ring, rest_grad)], axis=1)
-        qkv_grad = qkv_grad.reshape(rows, 3, tensor, -1)
-        qkv_grad = wide_sum(qkv_grad[:, :, 0], swap(qkv_grad[:, :, 1].astype(low)))
-        grad_normed = mm(grad_qkv, qkv_proj, NT) + arrived.astype(f32)
+        grad_normed = 0.0
+        qkv_shift = []
+        sent = 0.0
+        query_parts, rest_parts, out_parts = ([], [], [])
+        for i in range(tensor):
+            grad_heads = jnp.dot(grad_attn, out_proj[i], preferred_element_type=f32).astype(low)
+            out_parts.append(grad_parts(grad_attn, heads_out[i]))
+            grads = attention_backward(
+                meta, slopes[i * heads_half : (i + 1) * heads_half], qkv[i], kv_first[i], grad_heads, lse[i], scale
+            )
+            grad_qkv = jnp.concatenate(grads[:3], axis=1)
+            grad_first = jnp.concatenate(grads[3:], axis=1)
+            query = grads[0].shape[1]
+            sent = sent + mm(grad_first, qkv_proj[i][:, query:], NT)
+            query_parts.append(grad_parts(normed, grads[0]))
+            rest_parts.append(grad_parts(normed, grad_qkv[:, query:], (normed_first, grad_first)))
+            shift = jnp.sum(grad_qkv.astype(f32), axis=0)
+            qkv_shift.append(shift + jnp.pad(jnp.sum(grad_first.astype(f32), axis=0), (query, 0)))
+            grad_normed = grad_normed + mm(grad_qkv, qkv_proj[i], NT)
+        arrived = lax.ppermute(sent.astype(low), "tensor", [(1, 0)])
+        qkv_shift = jnp.stack(qkv_shift)
+        projections = [(query_parts, 256), (rest_parts, 256), (out_parts, 256)]
+        grad_normed = grad_normed + arrived.astype(f32)
         part, gain_one, shift_one = norm_back(before, small[0][layer], grad_normed)
         grad = grad_middle + part
-        weight_grads[layer] = (qkv_grad, out_grad.T, up_grad, down_grad)
         vector_grads[layer] = (gain_one, shift_one, out_shift, gain_two, shift_two, down_shift)
         bias_grads[layer] = (qkv_shift, up_shift)
+        if layer == 0:
+            projections.append((small_parts(vector_grads, bias_grads, by_half, placed, piece, lane), 256))
+        query_grad, rest_grad, out_grad, *last = scatter_grads(ring, projections, 3 + 2 * layer)
+        qkv_grad = jnp.concatenate([query_grad, rest_grad], axis=1).reshape(rows, 3, -1)
+        weight_grads[layer] = (qkv_grad, out_grad.T, up_grad, down_grad)
 
     input_grad = from_ring(grad, lax.Precision.HIGHEST)[None]
     qkv_grad, out_grad, up_grad, down_grad = [
         jnp.stack([weight_grads[layer][i] for layer in range(layers)]) for i in range(4)
     ]
-    vectors = jnp.stack([vector_grads[layer][i] for i in range(6) for layer in range(layers)])
-    vectors = from_ring(vectors, lax.Precision.HIGHEST).reshape(6 * layers, dp, tensor, piece).transpose(1, 2, 0, 3)
-    qkv_shift = jnp.stack([bias_grads[layer][0] for layer in range(layers)])
-    lane = qkv_bias.shape[3]
-    qkv_shift = by_half(qkv_shift.reshape(layers, 3, tensor, -1, dp, lane), 2).transpose(4, 2, 0, 1, 3, 5)
-    up_shift = jnp.stack([bias_grads[layer][1] for layer in range(layers)])
-    up_shift = by_half(up_shift.reshape(layers, tensor, -1, dp, lane), 1).transpose(3, 1, 0, 2, 4)
-    packed = jnp.concatenate([member.reshape(dp * tensor, -1) for member in (vectors, qkv_shift, up_shift)], axis=1)
-    summed = lax.psum_scatter(packed, ("dp", "tensor"), scatter_dimension=0, tiled=True)[0]
+    summed = last[0].reshape(-1)
     vectors = summed[:first].reshape(6, layers, piece)
     return (
         final_states,

time: 1490 us -> 949 us (0.64)
  waiting for transfers between devices: 684 us -> 18.4 us
  Pallas kernels: 83.2 us -> 588 us
  starting transfers between devices: 187 us -> 13.2 us
  local copies, waits for them, and re-layouts: 151 us -> 53.6 us
  other arithmetic: 83.7 us -> 25.5 us
  blocking collectives: 42.8 us -> 0 us
  between operations: 22.7 us -> 7.55 us
    ppermute x202 -> x2, waiting for transfers between devices: 568 us -> 0.01 us  [local(): arrived = lax.ppermute(sent.astype(low), 'tensor', [(1, 0)])]
    pallas_call x0 -> x5, Pallas kernels: none -> 505 us  [the longest x4 309 us: scatter_grads(): pl.pallas_call(kernel, in_specs=[pl.BlockSpec(memory_space=pl.ANY)] * (4...]
    ppermute x202 -> x2, starting transfers between devices: 180 us -> 2.82 us  [local(): arrived = lax.ppermute(sent.astype(low), 'tensor', [(1, 0)])]
    unnamed x2 -> x0, waiting for transfers between devices: 102 us -> none
    unnamed x545 -> x291, local copies, waits for them, and re-layouts: 96.7 us -> 29.7 us
    convert_element_type x57 -> x1, other arithmetic: 44.1 us -> 0.01 us  [local(): small = vectors.reshape(6, layers, 1, width).astype(f32)]
    unnamed x1 -> x0, blocking collectives: 42.8 us -> none
    dot_general x14 -> x20, matrix products: 47.8 us -> 53.5 us  [mm(): return lax.dot_general(a, b, dims, preferred_element_type=jnp.float32)]
  transfers between devices with their start and end apart: 205 -> 4, of which waited for: 105 -> 1; matrix products, arithmetic and copies ran while one was open for 24% -> 7% of each run, Pallas kernels for 3% -> 48%
where the time goes in v2:
time: 949 us; the launch traced here: 939 us
  Pallas kernels  588 us (62%)
  matrix products  233 us (25%)
  local copies, waits for them, and re-layouts  53.6 us (6%)
  other arithmetic  25.5 us (3%)
  waiting for transfers between devices  18.4 us (2%)
  starting transfers between devices  13.2 us (1%)
    pallas_call x4, Pallas kernels, scatter_grads(): pl.pallas_call(kernel, in_specs=[pl.BlockSpec(memory_space=pl.ANY)] * (4...  309 us
    pallas_call x1, Pallas kernels, gather_weights(): pl.pallas_call(kernel, in_specs=[pl.BlockSpec(memory_space=pl.ANY)] * len...  196 us
    dot_general x40, matrix products, grad_parts(): lax.dot_general(left[:, columns], right, ROWS_CONTRACT, preferred_element...  79.8 us
    dot_general x20, matrix products, mm(): return lax.dot_general(a, b, dims, preferred_element_type=jnp.float32)  53.5 us
    pallas_call x4, Pallas kernels, attention_backward(): pl.pallas_call(functools.partial(backward_kernel, scale=scale, step=rows...  45.4 us
    pallas_call x4, Pallas kernels, attention_forward(): pl.pallas_call(functools.partial(forward_kernel, scale=scale * LOG2E, ste...  38 us
    unnamed x291, local copies, waits for them, and re-layouts  29.7 us
    dot_general x4, matrix products, local(): grad_active = jnp.dot(grad_mlp, down_proj[i], preferred_element_type=f32)  29.1 us
  transfers between devices with their start and end apart: 4, of which 1 were waited for; matrix products, arithmetic and copies ran while one was open for 7% of the time, Pallas kernels for 48%

profile of v2, /device:TPU:0, one launch (start us, length us, event | category | flops | bytes accessed | tf_op | source)
XLA Modules:
  0.0 938.7 jit_solution(9600063722461212136)
XLA Ops:
  0.7 5.9 collective-permute-start
  24.7 195.8 %gather_weights.1 = (bf16[2,8,16,512]{3,2,1,0:T(8,128)(2,1)}, bf16[2,8,16,512]{3,2,1,0:T(8,128)(2,1)}, bf16[2,8,64,1536]{3,2,1,0:T(8,128)(2,1)}, bf16[2,8,64,153...) custom-call(bf16[16,512]{1,0:T(8,128)(2,1)} %reshape.514.refs_0_, ...), custom_call_target="tpu_custom_call" | custom-call | tf_op jit(solution)/shard_map/gather_weights/pallas_call | solution.py:425
  238.4 3.1 fusion.183
  244.8 9.3 attention_forward.4
  255.0 9.7 %attention_forward.5 = (bf16[512,512]{1,0:T(8,128)(2,1)S(1)}, f32[4,2,512]{2,1,0:T(2,128)S(1)}) custom-call(s32[2]{0:T(128)S(1)} %pad_add_fusion.4.meta, f32[8]{0:T(128)S(1)} %get-tuple-element.265.slopes, bf16[512,1536]{1,0:T(8,128)(2,1)S(1)} %fusion.34.q_ref.k_ref.v_ref.refs_0_.refs_1_.refs_2_, ...), custom_call_target="tpu_custom_call" | custom-call | flops 2147483648 | bytes 3145728 | tf_op jit(solution)/shard_map/attention_forward/pallas_call | solution.py:114
  269.0 5.5 multiply_convert_fusion.2
  274.5 5.5 multiply_convert_fusion.3
  286.4 4.4 collective-permute-start.1
  295.9 18.4 %collective-permute-done.1 = bf16[512,1024]{0,1:T(8,128)(2,1)S(1)} collective-permute-done((bf16[512,1024]{0,1:T(8,128)(2,1)S(1)}, bf16[512,1024]{0,1:T(8,128)(2,1)S(1)}, u32[]{:S(2)}, u32[]{:S(2)}) %collective-permute-start.1) | collective-permute-done | bytes 1048608 | tf_op jit(solution)/shard_map/ppermute | solution.py:748
  315.5 9.3 attention_forward.7
  326.2 9.5 %attention_forward.6 = (bf16[512,512]{1,0:T(8,128)(2,1)S(1)}, f32[4,2,512]{2,1,0:T(2,128)S(1)}) custom-call(s32[2]{0:T(128)S(1)} %pad_add_fusion.4.meta, f32[8]{0:T(128)S(1)} %get-tuple-element.266.slopes, bf16[512,1536]{1,0:T(8,128)(2,1)S(1)} %fusion.35.q_ref.k_ref.v_ref.refs_0_.refs_1_.refs_2_, ...), custom_call_target="tpu_custom_call" | custom-call | flops 2147483648 | bytes 3145728 | tf_op jit(solution)/shard_map/attention_forward/pallas_call | solution.py:114
  340.0 5.5 multiply_convert_fusion
  345.6 5.7 multiply_convert_fusion.1
  351.2 3.7 fusion.190
  354.9 4.4 add_add_fusion
  360.8 9.1 convert_reduce_fusion
  369.9 8.2 convert_reduce_fusion.1
  380.5 3.1 multiply_reduce_fusion
  387.3 11.6 %attention_backward.5 = (bf16[512,512]{1,0:T(8,128)(2,1)S(1)}, bf16[512,512]{1,0:T(8,128)(2,1)S(1)}, bf16[512,512]{1,0:T(8,128)(2,1)S(1)}, bf16[512,512]{1,0:T(8,128)(2,1)S(1)}, bf16[512,512]{1,0:T(8,128)(2,1)S(1)}) custom-call(s32[2]{0:T(128)S(1)} %pad_add_fusion.4.meta, f32[8]{0:T(128)S(1)} %get-tuple-element.265.slopes, ...), custom_call_target="tpu_custom_call" | custom-call | flops 5368709120 | bytes 6291456 | tf_op jit(solution)/shard_map/attention_backward/pallas_call | solution.py:192
  401.3 11.1 %attention_backward.4 = (bf16[512,512]{1,0:T(8,128)(2,1)S(1)}, bf16[512,512]{1,0:T(8,128)(2,1)S(1)}, bf16[512,512]{1,0:T(8,128)(2,1)S(1)}, bf16[512,512]{1,0:T(8,128)(2,1)S(1)}, bf16[512,512]{1,0:T(8,128)(2,1)S(1)}) custom-call(s32[2]{0:T(128)S(1)} %pad_add_fusion.4.meta, f32[8]{0:T(128)S(1)} %get-tuple-element.266.slopes, ...), custom_call_target="tpu_custom_call" | custom-call | flops 5368709120 | bytes 6291456 | tf_op jit(solution)/shard_map/attention_backward/pallas_call | solution.py:192
  422.2 2.6 fusion.51
  433.5 2.6 convolution_convert_fusion.5
  436.1 2.6 convolution_convert_fusion.4
  438.7 2.6 convolution_convert_fusion.7
  441.3 2.6 convolution_convert_fusion.6
  443.9 2.7 convolution_convert_fusion
  446.6 2.6 convolution_convert_fusion.1
  449.2 2.6 convolution_convert_fusion.2
  456.1 4.0 add_convert_fusion.9
  468.6 69.8 %scatter_grads.5 = (f32[64,512]{1,0:T(8,128)}, f32[64,1024]{1,0:T(8,128)}, f32[64,512]{1,0:T(8,128)}) custom-call(bf16[8,64,512]{2,1,0:T(8,128)(2,1)} %bitcast.399, bf16[8,64,512]{2,1,0:T(8,128)(2,1)} %bitcast.398, bf16[8,64,512]{2,1,0:T(8,128)(2,1)} %bitcast.397, bf16[8,64,512]{2,1,0:T(8,128)(2,1)} %bitcast.396, bf16[8,64,1024]{2,1,0:T(8,128)(2,1)} %bitcast.354, ...), custom_call_target="tpu_custom_call" | custom-call | tf_op jit(solution)/shard_map/scatter_grads/pallas_call | solution.py:613
  540.5 4.3 convolution_convert_fusion.3
  544.9 87.0 %scatter_grads.7 = (f32[64,2048]{1,0:T(8,128)}, f32[64,2048]{1,0:T(8,128)}) custom-call(bf16[8,64,2048]{2,1,0:T(8,128)(2,1)} %bitcast.361, bf16[8,64,2048]{2,1,0:T(8,128)(2,1)} %bitcast.362, bf16[8,64,2048]{2,1,0:T(8,128)(2,1)} %bitcast.359, bf16[8,64,2048]{2,1,0:T(8,128)(2,1)} %bitcast.360, bf16[8,64,2048]{2,1,0:T(8,128)(2,1)} %bitcast.370, ...), custom_call_target="tpu_custom_call" | custom-call | tf_op jit(solution)/shard_map/scatter_grads/pallas_call | solution.py:613
  636.6 4.0 multiply_reduce_fusion.2
  644.2 6.1 convert_reduce_fusion.2
  650.3 5.7 convert_reduce_fusion.3
  658.9 3.1 multiply_reduce_fusion.1
  667.1 11.3 %attention_backward.7 = (bf16[512,512]{1,0:T(8,128)(2,1)S(1)}, bf16[512,512]{1,0:T(8,128)(2,1)S(1)}, bf16[512,512]{1,0:T(8,128)(2,1)S(1)}, bf16[512,512]{1,0:T(8,128)(2,1)S(1)}, bf16[512,512]{1,0:T(8,128)(2,1)S(1)}) custom-call(s32[2]{0:T(128)S(1)} %pad_add_fusion.4.meta, f32[8]{0:T(128)S(1)} %get-tuple-element.265.slopes, bf16[512,1536]{1,0:T(8,128)(2,1)S(1)} %copy-done.9, ...), custom_call_target="tpu_custom_call" | custom-call | flops 5368709120 | bytes 6291456 | tf_op jit(solution)/shard_map/attention_backward/pallas_call | solution.py:192
  680.9 11.4 %attention_backward.6 = (bf16[512,512]{1,0:T(8,128)(2,1)S(1)}, bf16[512,512]{1,0:T(8,128)(2,1)S(1)}, bf16[512,512]{1,0:T(8,128)(2,1)S(1)}, bf16[512,512]{1,0:T(8,128)(2,1)S(1)}, bf16[512,512]{1,0:T(8,128)(2,1)S(1)}) custom-call(s32[2]{0:T(128)S(1)} %pad_add_fusion.4.meta, f32[8]{0:T(128)S(1)} %get-tuple-element.266.slopes, bf16[512,1536]{1,0:T(8,128)(2,1)S(1)} %copy-done.7, ...), custom_call_target="tpu_custom_call" | custom-call | flops 5368709120 | bytes 6291456 | tf_op jit(solution)/shard_map/attention_backward/pallas_call | solution.py:192
  701.7 2.6 fusion.59
  715.5 2.6 convolution_convert_fusion.12
  720.7 2.6 convolution_convert_fusion.14
  728.4 2.6 convolution_convert_fusion.10
  731.0 3.0 convolution_convert_fusion.11
  740.6 4.6 add_convert_fusion.8
  751.8 97.8 %scatter_grads.6 = (f32[64,2048]{1,0:T(8,128)}, f32[64,2048]{1,0:T(8,128)}) custom-call(bf16[8,64,2048]{2,1,0:T(8,128)(2,1)} %bitcast.357, bf16[8,64,2048]{2,1,0:T(8,128)(2,1)} %bitcast.358, bf16[8,64,2048]{2,1,0:T(8,128)(2,1)} %bitcast.355, bf16[8,64,2048]{2,1,0:T(8,128)(2,1)} %bitcast.356, bf16[8,64,2048]{2,1,0:T(8,128)(2,1)} %bitcast.366, ...), custom_call_target="tpu_custom_call" | custom-call | tf_op jit(solution)/shard_map/scatter_grads/pallas_call | solution.py:613
  858.8 5.1 multiply_reduce_fusion.3
  866.2 54.2 %scatter_grads.4 = (f32[64,512]{1,0:T(8,128)}, f32[64,1024]{1,0:T(8,128)}, f32[64,512]{1,0:T(8,128)}, f32[8,512]{1,0:T(8,128)}) custom-call(bf16[8,64,512]{2,1,0:T(8,128)(2,1)} %bitcast.391, bf16[8,64,512]{2,1,0:T(8,128)(2,1)} %bitcast.390, bf16[8,64,512]{2,1,0:T(8,128)(2,1)} %bitcast.389, bf16[8,64,512]{2,1,0:T(8,128)(2,1)} %bitcast.388, ...), custom_call_target="tpu_custom_call" | custom-call | tf_op jit(solution)/shard_map/scatter_grads/pallas_call | solution.py:613
  929.8 8.7 fusion.68
  (512 shorter events, 180.8 us)
Async XLA Ops:
  0.6 358.7 %copy-start = (bf16[1,512,1024]{2,1,0:T(8,128)(2,1)S(1)}, bf16[1,512,1024]{2,1,0:T(8,128)(2,1)}, u32[]{:S(2)}) copy-start(bf16[1,512,1024]{2,1,0:T(8,128)(2,1)} %param.18) | copy-start | bytes 3145732
  0.7 22.3 %copy-start.53 = (bf16[2,64,2048]{2,1,0:T(8,128)(2,1)S(1)}, bf16[2,64,2048]{2,1,0:T(8,128)(2,1)}, u32[]{:S(2)}) copy-start(bf16[2,64,2048]{2,1,0:T(8,128)(2,1)} %param.29) | copy-start | bytes 1572868
  0.7 23.2 %copy-start.54 = (bf16[2,2048,64]{1,2,0:T(8,128)(2,1)S(1)}, bf16[2,2048,64]{1,2,0:T(8,128)(2,1)}, u32[]{:S(2)}) copy-start(bf16[2,2048,64]{1,2,0:T(8,128)(2,1)} %param.31) | copy-start | bytes 1572868
  0.7 237.7 %collective-permute-start = (bf16[512,1024]{1,0:T(8,128)(2,1)}, bf16[512,1024]{1,0:T(8,128)(2,1)}, u32[]{:S(2)}, u32[]{:S(2)}) collective-permute-start(bf16[512,1024]{1,0:T(8,128)(2,1)} %bitcast.489), channel_id=1, source_target_pairs={{0,1},{2,3},{4,5},{6,7},{8,9},{10,11},{12,13},{14,15},{16,17},{18,... | collective-permute-start | bytes 3145736 | tf_op jit(solution)/shard_map/ppermute | solution.py:738
  11.3 220.0 %copy-start.83 = (s32[16]{0:T(128)}, s32[16]{0:T(128)S(1)}, u32[]{:S(2)}) copy-start(s32[16]{0:T(128)S(1)} %dynamic-slice_bitcast_fusion) | copy-start | bytes 196
  226.3 38.5 %copy-start.16 = (f32[1024,512]{1,0:T(8,128)}, f32[1024,512]{1,0:T(8,128)S(1)}, u32[]{:S(2)}) copy-start(f32[1024,512]{1,0:T(8,128)S(1)} %get-tuple-element.268) | copy-start | bytes 6291460
  226.3 5.9 copy-start.74
  226.6 6.0 copy-start.76
  231.1 34.9 %copy-start.62 = (f32[1,1,1,1024]{3,1,0,2:T(1,128)}, f32[1,1,1,1024]{3,1,0,2:T(1,128)S(1)}, u32[]{:S(2)}) copy-start(f32[1,1,1,1024]{3,1,0,2:T(1,128)S(1)} %get-tuple-element.251) | copy-start | bytes 12292
  231.1 54.9 %copy-start.64 = (f32[1,1,1,1024]{3,1,0,2:T(1,128)}, f32[1,1,1,1024]{3,1,0,2:T(1,128)S(1)}, u32[]{:S(2)}) copy-start(f32[1,1,1,1024]{3,1,0,2:T(1,128)S(1)} %get-tuple-element.248) | copy-start | bytes 12292
  231.1 59.7 %copy-start.60 = (f32[1,1,1,1024]{3,1,0,2:T(1,128)}, f32[1,1,1,1024]{3,1,0,2:T(1,128)S(1)}, u32[]{:S(2)}) copy-start(f32[1,1,1,1024]{3,1,0,2:T(1,128)S(1)} %get-tuple-element.254) | copy-start | bytes 12292
  232.2 34.3 %copy-start.81 = (f32[1,1,1,2048]{3,0,1,2:T(1,128)}, f32[1,1,1,2048]{3,0,1,2:T(1,128)S(1)}, u32[]{:S(2)}) copy-start(f32[1,1,1,2048]{3,0,1,2:T(1,128)S(1)} %get-tuple-element.257) | copy-start | bytes 24580
  232.2 42.3 %copy-start.79 = (f32[1,1,1,2048]{3,0,1,2:T(1,128)}, f32[1,1,1,2048]{3,0,1,2:T(1,128)S(1)}, u32[]{:S(2)}) copy-start(f32[1,1,1,2048]{3,0,1,2:T(1,128)S(1)} %get-tuple-element.258) | copy-start | bytes 24580
  236.3 18.7 %copy-start.8 = (bf16[512,1536]{1,0:T(8,128)(2,1)}, bf16[512,1536]{1,0:T(8,128)(2,1)S(1)}, u32[]{:S(2)}) copy-start(bf16[512,1536]{1,0:T(8,128)(2,1)S(1)} %fusion.34.q_ref.k_ref.v_ref.refs_0_.refs_1_.refs_2_) | copy-start | bytes 4718596
  238.4 6.4 copy-start.6
  244.8 10.2 %copy-start.12 = (bf16[512,1024]{1,0:T(8,128)(2,1)}, bf16[512,1024]{1,0:T(8,128)(2,1)S(1)}, u32[]{:S(2)}) copy-start(bf16[512,1024]{1,0:T(8,128)(2,1)S(1)} %add_convert_fusion.15.k0_ref.v0_ref.refs_3_.refs_4_) | copy-start | bytes 3145732
  244.8 9.4 copy-start.45
  255.0 9.8 %copy-start.47 = (bf16[2,8,64,512]{3,2,1,0:T(8,128)(2,1)S(1)}, bf16[2,8,64,512]{3,2,1,0:T(8,128)(2,1)}, u32[]{:S(2)}) copy-start(bf16[2,8,64,512]{3,2,1,0:T(8,128)(2,1)} %get-tuple-element.78) | copy-start | bytes 3145732
  265.6 16.8 %copy-start.14 = (f32[512,1024]{0,1:T(8,128)}, f32[512,1024]{0,1:T(8,128)S(1)}, u32[]{:S(2)}) copy-start(f32[512,1024]{0,1:T(8,128)S(1)} %get-tuple-element.272) | copy-start | bytes 6291460
  265.9 8.5 copy-start.70
  266.6 7.9 copy-start.51
  269.0 5.5 copy-start.87
  274.5 8.0 copy-start.109
  274.5 5.6 copy-start.89
  285.9 6.2 copy-start.72
  286.4 5.8 copy-start.102
  286.4 27.9 %collective-permute-start.1 = (bf16[512,1024]{0,1:T(8,128)(2,1)S(1)}, bf16[512,1024]{0,1:T(8,128)(2,1)S(1)}, u32[]{:S(2)}, u32[]{:S(2)}) collective-permute-start(bf16[512,1024]{0,1:T(8,128)(2,1)S(1)} %add_convert_fusion.13), channel_id=1, source_target_pairs={{0,1},{2,3},{4,5},{6,7},{8,9},{10,11},{12,13},{14,15},{16,17},{18,... | collective-permute-start | bytes 3145736 | tf_op jit(solution)/shard_map/ppermute | solution.py:748
  314.3 10.6 %copy-start.32 = (bf16[512,1024]{0,1:T(8,128)(2,1)}, bf16[512,1024]{0,1:T(8,128)(2,1)S(1)}, u32[]{:S(2)}) copy-start(bf16[512,1024]{0,1:T(8,128)(2,1)S(1)} %collective-permute-done.1) | copy-start | bytes 3145732
  326.2 9.6 %copy-start.49 = (bf16[2,8,64,512]{3,2,1,0:T(8,128)(2,1)S(1)}, bf16[2,8,64,512]{3,2,1,0:T(8,128)(2,1)}, u32[]{:S(2)}) copy-start(bf16[2,8,64,512]{3,2,1,0:T(8,128)(2,1)} %get-tuple-element.85) | copy-start | bytes 3145732
  340.0 5.6 copy-start.94
  345.5 9.4 copy-start.115
  345.5 5.7 copy-start.95
  360.8 9.1 copy-start.125
  369.8 10.7 %copy-start.117 = (bf16[512,2048]{1,0:T(8,128)(2,1)}, bf16[512,2048]{1,0:T(8,128)(2,1)S(1)}, u32[]{:S(2)}) copy-start(bf16[512,2048]{1,0:T(8,128)(2,1)S(1)} %get-tuple-element.208) | copy-start | bytes 6291460
  456.1 5.4 copy-start.28
  456.1 5.4 copy-start.33
  460.1 176.0 %collective-permute-start.2 = (bf16[512,1024]{0,1:T(8,128)(2,1)}, bf16[512,1024]{0,1:T(8,128)(2,1)}, u32[]{:S(2)}, u32[]{:S(2)}) collective-permute-start(bf16[512,1024]{0,1:T(8,128)(2,1)} %add_convert_fusion.9), channel_id=1, source_target_pairs={{1,0},{3,2},{5,4},{7,6},{9,8},{11,10},{13,12},{15,14},{17,16},{19,... | collective-permute-start | bytes 3145736 | tf_op jit(solution)/shard_map/ppermute | solution.py:809
  544.9 87.0 %copy-start.122 = (f32[512,1024]{0,1:T(8,128)S(1)}, f32[512,1024]{0,1:T(8,128)}, u32[]{:S(2)}) copy-start(f32[512,1024]{0,1:T(8,128)} %copy-done.121) | copy-start | bytes 6291460
  644.2 6.1 copy-start.80
  644.2 6.1 copy-start.90
  644.2 6.1 copy-start.123
  650.3 5.7 copy-start.88
  667.1 11.4 %copy-start.22 = (bf16[512,1024]{0,1:T(8,128)(2,1)S(1)}, bf16[512,1024]{0,1:T(8,128)(2,1)}, u32[]{:S(2)}) copy-start(bf16[512,1024]{0,1:T(8,128)(2,1)} %copy-done.21) | copy-start | bytes 3145732
  740.6 6.1 copy-start.20
  740.6 6.1 copy-start.25
  745.3 112.3 %collective-permute-start.3 = (bf16[512,1024]{0,1:T(8,128)(2,1)}, bf16[512,1024]{0,1:T(8,128)(2,1)}, u32[]{:S(2)}, u32[]{:S(2)}) collective-permute-start(bf16[512,1024]{0,1:T(8,128)(2,1)} %add_convert_fusion.8), channel_id=1, source_target_pairs={{1,0},{3,2},{5,4},{7,6},{9,8},{11,10},{13,12},{15,14},{17,16},{19,... | collective-permute-start | bytes 3145736 | tf_op jit(solution)/shard_map/ppermute | solution.py:809
  751.8 97.8 %copy-start.56 = (f32[64,2048]{1,0:T(8,128)S(1)}, f32[64,2048]{1,0:T(8,128)}, u32[]{:S(2)}) copy-start(f32[64,2048]{1,0:T(8,128)} %get-tuple-element.125) | copy-start | bytes 1572868
  929.8 8.7 copy-start.1
  (83 other events, 202.3 us)

commit v3 on v2

--- a/solution.py
+++ b/solution.py
@@ -64,10 +64,9 @@
     return parts
 
 
-def forward_body(half, slopes, prefix, scale, q_ref, k_ref, v_ref, k0_ref, v0_ref, o_ref, lse_ref, step):
+def forward_body(half, pair, slopes, prefix, scale, q_ref, k_ref, v_ref, k0_ref, v0_ref, o_ref, lse_ref, step):
     rows, width = q_ref.shape
     masks = lane_masks(width)
-    pair = pl.program_id(0)
     head = width // 2
     values = v_ref[...].T
     values0 = v0_ref[...].T if half else None
@@ -95,47 +94,10 @@
         o_ref[start : start + step] = jnp.concatenate(outs, axis=0).T.astype(jnp.bfloat16)
 
 
-def forward_kernel(meta, slopes, q_ref, k_ref, v_ref, k0_ref, v0_ref, o_ref, lse_ref, *, scale, step):
-    args = (slopes, meta[1], scale, q_ref, k_ref, v_ref, k0_ref, v0_ref, o_ref, lse_ref, step)
-
-    @pl.when(meta[0] == 0)
-    def first():
-        forward_body(0, *args)
-
-    @pl.when(meta[0] != 0)
-    def second():
-        forward_body(1, *args)
-
-
-def attention_forward(meta, slopes, qkv, kv0, scale):
-    rows, width = qkv.shape
-    pairs = width // 3 // 128
-    block = lambda base: pl.BlockSpec((rows, 128), lambda j, *_: (0, base + j))
-    return pl.pallas_call(
-        functools.partial(forward_kernel, scale=scale * LOG2E, step=rows // 2),
-        grid_spec=pltpu.PrefetchScalarGridSpec(
-            num_scalar_prefetch=2,
-            grid=(pairs,),
-            in_specs=[block(0), block(pairs), block(2 * pairs), block(0), block(pairs)],
-            out_specs=[block(0), pl.BlockSpec((1, 2, rows), lambda j, *_: (j, 0, 0))],
-        ),
-        out_shape=[
-            jax.ShapeDtypeStruct((rows, width // 3), jnp.bfloat16),
-            jax.ShapeDtypeStruct((pairs, 2, rows), jnp.float32),
-        ],
-        compiler_params=pltpu.CompilerParams(vmem_limit_bytes=40 * 1024 * 1024),
-        cost_estimate=pl.CostEstimate(
-            flops=pairs * 2 * rows * rows * 128 * 8, bytes_accessed=rows * width * 4, transcendentals=pairs * 4 * rows * rows
-        ),
-        name="attention_forward",
-    )(meta, slopes, qkv, qkv, qkv, kv0, kv0)
-
-
-def backward_body(half, slopes, prefix, scale, refs, step):
+def backward_body(half, pair, slopes, prefix, scale, refs, step):
     q_ref, k_ref, v_ref, k0_ref, v0_ref, g_ref, lse_ref, gq_ref, gk_ref, gv_ref, gk0_ref, gv0_ref, sums = refs
     rows, width = q_ref.shape
     masks = lane_masks(width)
-    pair = pl.program_id(0)
     head = width // 2
     keys = k_ref[...].T
     keys0 = k0_ref[...].T if half else None
@@ -174,45 +136,59 @@
     gv0_ref[...] = sums[3].astype(jnp.bfloat16)
 
 
-def backward_kernel(meta, slopes, *refs, scale, step):
-    @pl.when(meta[0] == 0)
-    def first():
-        backward_body(0, slopes, meta[1], scale, refs, step)
-
-    @pl.when(meta[0] != 0)
-    def second():
-        backward_body(1, slopes, meta[1], scale, refs, step)
-
-
-def attention_backward(meta, slopes, qkv, kv0, grad_heads, lse, scale):
-    rows, width = qkv.shape
-    pairs = width // 3 // 128
-    block = lambda base: pl.BlockSpec((rows, 128), lambda j, *_: (0, base + j))
-    full = jax.ShapeDtypeStruct((rows, width // 3), jnp.bfloat16)
-    return pl.pallas_call(
-        functools.partial(backward_kernel, scale=scale, step=rows // 2),
-        grid_spec=pltpu.PrefetchScalarGridSpec(
-            num_scalar_prefetch=2,
-            grid=(pairs,),
-            in_specs=[
-                block(0),
-                block(pairs),
-                block(2 * pairs),
-                block(0),
-                block(pairs),
-                block(0),
-                pl.BlockSpec((1, 2, rows), lambda j, *_: (j, 0, 0)),
-            ],
-            out_specs=[block(0)] * 5,
-            scratch_shapes=[pltpu.VMEM((4, rows, 128), jnp.float32)],
-        ),
-        out_shape=[full] * 5,
-        compiler_params=pltpu.CompilerParams(vmem_limit_bytes=40 * 1024 * 1024),
-        cost_estimate=pl.CostEstimate(
-            flops=pairs * 2 * rows * rows * 128 * 20, bytes_accessed=rows * width * 8, transcendentals=pairs * 4 * rows * rows
-        ),
-        name="attention_backward",
-    )(meta, slopes, qkv, qkv, qkv, kv0, kv0, grad_heads, lse)
+def head_pairs(low, high, body):
+    @pl.loop(low, high)
+    def step(pair):
+        columns = pl.multiple_of(pair * 128, 128)
+        for half in range(2):
+            @pl.when(lax.axis_index("tensor") == half)
+            def one():
+                body(half, pair, columns)
+
+
+def forward_work(parts, slopes, prefix, scale):
+    work = []
+    for e, (qkv, first, out, lse) in enumerate(parts):
+        pairs = out.shape[1] // 128
+        rows = out.shape[0]
+
+        def body(half, pair, columns, e=e, qkv=qkv, first=first, out=out, lse=lse, pairs=pairs, rows=rows):
+            at = lambda ref, base: ref.at[:, pl.ds(columns + base * pairs * 128, 128)]
+            forward_body(
+                half,
+                pair + e * pairs,
+                slopes,
+                prefix,
+                scale * LOG2E,
+                at(qkv, 0),
+                at(qkv, 1),
+                at(qkv, 2),
+                at(first, 0),
+                at(first, 1),
+                at(out, 0),
+                lse.at[pl.ds(pair, 1)],
+                rows // 2,
+            )
+
+        work.append(functools.partial(head_pairs, 0, pairs, body))
+    return work
+
+
+def backward_work(parts, slopes, prefix, scale, sums):
+    work = []
+    for e, (qkv, first, grad, lse, outs) in enumerate(parts):
+        pairs = grad.shape[1] // 128
+        rows = grad.shape[0]
+
+        def body(half, pair, columns, e=e, qkv=qkv, first=first, grad=grad, lse=lse, outs=outs, pairs=pairs, rows=rows):
+            at = lambda ref, base: ref.at[:, pl.ds(columns + base * pairs * 128, 128)]
+            refs = [at(qkv, 0), at(qkv, 1), at(qkv, 2), at(first, 0), at(first, 1), at(grad, 0), lse.at[pl.ds(pair, 1)]]
+            refs += [at(out, 0) for out in outs] + [sums]
+            backward_body(half, pair + e * pairs, slopes, prefix, scale, refs, rows // 2)
+
+        for low in range(0, pairs, 2):
+            work.append(functools.partial(head_pairs, low, low + 2, body))
+    return work
 
 
 EPS = 1e-05
@@ -251,6 +227,8 @@
         self.chips = devices // 2
         self.order = list(range(0, self.chips, 2)) + list(range(self.chips - 1, 0, -2))
         self.place = {chip: spot for spot, chip in enumerate(self.order)}
+        half = self.chips // 2
+        self.turns = [half] + [step for hop in range(half - 1, 0, -1) for step in (self.chips - hop, hop)] + [0]
 
     def owners(self):
         table = []
@@ -260,7 +238,7 @@
                 [
                     2 * self.order[(spot - step) % self.chips] + ((device % 2) ^ core)
                     for core in range(2)
-                    for step in range(self.chips)
+                    for step in self.turns
                 ]
             )
         return np.array(table, np.int32)
@@ -289,10 +267,10 @@
 class Copies:
     def __init__(self, send, recv, near):
         self.send, self.recv, self.near = (send, recv, near)
-        self.sent, self.moved = ([], [])
+        self.sent, self.moved, self.spots = ([], [], 0)
 
     def push(self, source, target, device):
-        spot = len(self.sent)
+        spot = self.spots
         copy = pltpu.make_async_remote_copy(
             src_ref=source,
             dst_ref=target,
@@ -303,6 +281,7 @@
         )
         copy.start()
         self.sent.append(copy)
+        self.spots += 1
         return copy
 
     def move(self, source, target):
@@ -311,6 +290,10 @@
         self.moved.append(copy)
         return copy
 
+    def settle(self, copy):
+        copy.wait_send()
+        self.sent = [other for other in self.sent if other is not copy]
+
     def finish(self):
         for copy in self.sent:
             copy.wait_send()
@@ -321,26 +304,28 @@
         pass
 
 
-def gather_steps(copies, ids, chips, arrays):
+def gather_steps(copies, ids, ring, arrays):
     ahead, behind, sibling, across = ids
+    chips = ring.chips
     half = chips // 2
+    slot = ring.turns.index
     local, siblings, early_in, late_in, up, down = ([], [], [], [], {}, {})
     for shard, own, other, early in arrays:
-        early_in.append(copies.push(shard.at[:, pl.ds(0, early)], other.at[0, 0, :, pl.ds(0, early)], across))
+        early_in.append(copies.push(shard.at[:, pl.ds(0, early)], other.at[0, slot(0), :, pl.ds(0, early)], across))
     for i, (shard, own, other, early) in enumerate(arrays):
-        local.append(copies.move(shard, own.at[0, 0]))
-        up[i, 1] = [copies.push(shard, own.at[0, 1], ahead)]
-        down[i, 1] = [copies.push(shard, own.at[0, chips - 1], behind)]
-        siblings.append(copies.push(shard, own.at[1, 0], sibling))
+        local.append(copies.move(shard, own.at[0, slot(0)]))
+        up[i, 1] = [copies.push(shard, own.at[0, slot(1)], ahead)]
+        down[i, 1] = [copies.push(shard, own.at[0, slot(chips - 1)], behind)]
+        siblings.append(copies.push(shard, own.at[1, slot(0)], sibling))
     for shard, own, other, early in arrays:
         width = shard.shape[1] - early
-        late_in.append(copies.push(shard.at[:, pl.ds(early, width)], other.at[0, 0, :, pl.ds(early, width)], across))
+        late_in.append(copies.push(shard.at[:, pl.ds(early, width)], other.at[0, slot(0), :, pl.ds(early, width)], across))
     yield
     for i, (shard, own, other, early) in enumerate(arrays):
         early_in[i].wait_recv()
-        part = other.at[0, 0, :, pl.ds(0, early)]
-        up[i, 1].append(copies.push(part, other.at[0, 1, :, pl.ds(0, early)], ahead))
-        down[i, 1].append(copies.push(part, other.at[0, chips - 1, :, pl.ds(0, early)], behind))
+        part = other.at[0, slot(0), :, pl.ds(0, early)]
+        up[i, 1].append(copies.push(part, other.at[0, slot(1), :, pl.ds(0, early)], ahead))
+        down[i, 1].append(copies.push(part, other.at[0, slot(chips - 1), :, pl.ds(0, early)], behind))
     late = [(0, late_in)]
     for hop in range(1, half + 1):
         yield
@@ -360,14 +345,14 @@
                     else:
                         window, slim = (pl.ds(size // 2, size // 2), pl.ds(early // 2, early // 2))
                     arrivals[i, hop + 1] = [
-                        copies.push(own.at[0, spot, :, window], own.at[0, spot + step, :, window], target)
+                        copies.push(own.at[0, slot(spot), :, window], own.at[0, slot(spot + step), :, window], target)
                     ]
                     rest = pl.ds(early, size - early)
-                    crossing[spot].append(copies.push(own.at[0, spot, :, rest], other.at[0, spot, :, rest], across))
-                    siblings.append(copies.push(own.at[0, spot], own.at[1, spot], sibling))
+                    crossing[spot].append(copies.push(own.at[0, slot(spot), :, rest], other.at[0, slot(spot), :, rest], across))
+                    siblings.append(copies.push(own.at[0, slot(spot)], own.at[1, slot(spot)], sibling))
                     arrivals[i, hop][1].wait_recv()
                     arrivals[i, hop + 1].append(
-                        copies.push(other.at[0, spot, :, slim], other.at[0, spot + step, :, slim], target)
+                        copies.push(other.at[0, slot(spot), :, slim], other.at[0, slot(spot + step), :, slim], target)
                     )
         else:
             crossing[half] = []
@@ -375,20 +360,20 @@
                 up[i, half][0].wait_recv()
                 down[i, half][0].wait_recv()
                 rest = pl.ds(early, shard.shape[1] - early)
-                crossing[half].append(copies.push(own.at[0, half, :, rest], other.at[0, half, :, rest], across))
-                siblings.append(copies.push(own.at[0, half], own.at[1, half], sibling))
+                crossing[half].append(copies.push(own.at[0, slot(half), :, rest], other.at[0, slot(half), :, rest], across))
+                siblings.append(copies.push(own.at[0, slot(half)], own.at[1, slot(half)], sibling))
                 up[i, half][1].wait_recv()
                 down[i, half][1].wait_recv()
         for spot, arrivals in late:
             for i, (shard, own, other, early) in enumerate(arrays):
                 arrivals[i].wait_recv()
-                siblings.append(copies.push(other.at[0, spot], other.at[1, spot], sibling))
+                siblings.append(copies.push(other.at[0, slot(spot)], other.at[1, slot(spot)], sibling))
         late = list(crossing.items())
     yield
     for spot, arrivals in late:
         for i, (shard, own, other, early) in enumerate(arrays):
             arrivals[i].wait_recv()
-            siblings.append(copies.push(other.at[0, spot], other.at[1, spot], sibling))
+            siblings.append(copies.push(other.at[0, slot(spot)], other.at[1, slot(spot)], sibling))
     for copy in local:
         copy.wait()
     yield
@@ -401,45 +386,73 @@
     return arrays * (5 + 2 + (half - 1) * 2 * 4 + 2 + chips)
 
 
-def gather_weights(ring, groups, collective):
+def on_vmem(count):
+    return [pl.BlockSpec(memory_space=pltpu.VMEM)] * count
+
+
+def on_smem(count):
+    return [pl.BlockSpec(memory_space=pltpu.SMEM)] * count
+
+
+def anywhere(count):
+    return [pl.BlockSpec(memory_space=pl.ANY)] * count
+
+
+def gather_weights(ring, groups, collective, attention=None):
     flat = [member for group in groups for member in group]
+    total = len(flat)
     count = sum(gather_count(ring.chips, len(group)) for group in groups)
     shapes = [
         jax.ShapeDtypeStruct((2, ring.chips) + shard.shape, shard.dtype) for shard, early in flat for unused in range(2)
     ]
+    inputs, more = ([], [])
+    if attention is not None:
+        qkv, first, slopes, prefix, scale = attention
+        inputs = list(qkv) + list(first) + [slopes, prefix]
+        rows, width = (qkv[0].shape[0], qkv[0].shape[1] // 3)
+        more = [jax.ShapeDtypeStruct((rows, width), jnp.bfloat16)] * 2
+        more += [jax.ShapeDtypeStruct((width // 128, 2, rows), jnp.float32)] * 2
 
     def kernel(*refs):
-        shards, outs = (refs[: len(flat)], refs[len(flat) : 3 * len(flat)])
+        shards, extra, refs = (refs[:total], refs[total : total + len(inputs)], refs[total + len(inputs) :])
+        outs, made, scratch = (refs[: 2 * total], refs[2 * total : 2 * total + len(more)], refs[2 * total + len(more) :])
         ids = ring.neighbours()
         greet(ids)
-        copies = Copies(*refs[3 * len(flat) :])
-        members = [(shards[i], outs[2 * i], outs[2 * i + 1], flat[i][1]) for i in range(len(flat))]
+        copies = Copies(*scratch)
+        members = [(shards[i], outs[2 * i], outs[2 * i + 1], flat[i][1]) for i in range(total)]
         at = 0
         running = []
         for group in groups:
-            running.append(gather_steps(copies, ids, ring.chips, members[at : at + len(group)]))
+            running.append(gather_steps(copies, ids, ring, members[at : at + len(group)]))
             at += len(group)
-        run_staggered(running, 3)
+        work = []
+        if attention is not None:
+            parts = [(extra[e], extra[2 + e], made[e], made[2 + e]) for e in range(2)]
+            work = forward_work(parts, extra[4], extra[5][0], scale)
+        run_staggered(running, 3, work)
         copies.finish()
 
     outs = pl.pallas_call(
         kernel,
-        in_specs=[pl.BlockSpec(memory_space=pl.ANY)] * len(flat),
-        out_specs=[pl.BlockSpec(memory_space=pl.ANY)] * len(shapes),
-        out_shape=shapes,
+        in_specs=anywhere(total) + (on_vmem(4) + on_smem(2) if inputs else []),
+        out_specs=anywhere(len(shapes)) + on_vmem(len(more)),
+        out_shape=shapes + more,
         scratch_shapes=[
             pltpu.SemaphoreType.DMA((count,)),
             pltpu.SemaphoreType.DMA((count,)),
-            pltpu.SemaphoreType.DMA((len(flat),)),
+            pltpu.SemaphoreType.DMA((total,)),
         ],
-        compiler_params=pltpu.CompilerParams(collective_id=collective, has_side_effects=True),
+        compiler_params=pltpu.CompilerParams(
+            collective_id=collective, has_side_effects=True, vmem_limit_bytes=40 * 1024 * 1024
+        ),
         name="gather_weights",
-    )(*[shard for shard, early in flat])
-    return [out.reshape(-1, out.shape[-1]) for out in outs]
-
-
-def run_staggered(running, lead):
-    waiting = list(running)
+    )(*[shard for shard, early in flat], *inputs)
+    weights = [out.reshape(-1, out.shape[-1]) for out in outs[: 2 * total]]
+    return (weights, outs[2 * total : 2 * total + 2], outs[2 * total + 2 :])
+
+
+def run_staggered(running, lead, work=()):
+    waiting, work = (list(running), list(work))
     active = []
     youngest = lead
     while waiting or active:
@@ -452,6 +465,10 @@
                 next(steps)
             except StopIteration:
                 active.remove(steps)
+        if work:
+            work.pop(0)()
+    for piece in work:
+        piece()
 
 
 def add_rows(target, source):
@@ -466,33 +483,71 @@
         )
 
 
-def scatter_steps(copies, ids, chips, arrays):
+def products(lefts, rights, held, columns, target, near):
+    for i, left in enumerate(lefts):
+        held[i] = left[:, columns].T
+    blocks, rows, width = target.shape
+    step = 512
+
+    @pl.loop(0, width // step)
+    def tile(i):
+        window = pl.ds(pl.multiple_of(i * step, step), step)
+        out = mm(held[0], rights[0][:, window], NN)
+        for j in range(1, len(rights)):
+            out = out + mm(held[j], rights[j][:, window], NN)
+        out = out.reshape(blocks, rows, step)
+        if near is not None:
+            out = out + near[:, :, window].astype(jnp.float32)
+        target[:, :, window] = out.astype(target.dtype)
+
+
+def scatter_steps(copies, ids, ring, arrays, held):
     ahead, behind, sibling, across = ids
+    chips = ring.chips
     half = chips // 2
-    blocks = [half] + [spot for hop in range(half - 1, 0, -1) for spot in (chips - hop, hop)] + [0]
-    loaded, near = ({}, {})
-    for spot in blocks:
-        for i, (parts, early, out, room) in enumerate(arrays):
-            for e in range(2):
-                near[i, e, spot] = copies.push(parts[e][1].at[spot], room["near"].at[e, spot], sibling)
-                loaded[i, e, spot] = copies.move(parts[e][0].at[spot], room["sum"].at[e, spot])
+    group_blocks = chips // 2
+    slot = ring.turns.index
+    near = {}
     crossed = {}
 
-    def first(spot):
+    def outgoing(group):
+        blocks = pl.ds(group * group_blocks, group_blocks)
+        for i, (source, early, out, room) in enumerate(arrays):
+            for e in (1, 0):
+                if source[0] == "given":
+                    sent = source[1][e][1].at[blocks]
+                else:
+                    sent = room["outbox"].at[e]
+                    if group > 0:
+                        copies.settle(near[i, e, group - 1])
+                    height = group_blocks * out.shape[0]
+                    columns = slice((chips // group_blocks + group) * height, (chips // group_blocks + group + 1) * height)
+                    products(source[1], source[2][e], held, columns, sent, None)
+                near[i, e, group] = copies.push(sent, room["near"].at[e, blocks], sibling)
+
+    def own(group):
+        blocks = pl.ds(group * group_blocks, group_blocks)
         for e in (1, 0):
-            for i, (parts, early, out, room) in enumerate(arrays):
-                loaded[i, e, spot].wait()
-                near[i, e, spot].wait_recv()
-                add_rows(room["sum"].at[e, spot], room["near"].at[e, spot])
+            for i, (source, early, out, room) in enumerate(arrays):
+                near[i, e, group].wait_recv()
+                target = room["sum"].at[e, blocks]
+                if source[0] == "given":
+                    target[...] = source[1][e][0][blocks] + room["near"][e, blocks]
+                else:
+                    height = group_blocks * out.shape[0]
+                    columns = slice(group * height, (group + 1) * height)
+                    products(source[1], source[2][e], held, columns, target, room["near"].at[e, blocks])
                 if e == 1:
                     rest = pl.ds(early, out.shape[1] - early)
-                    crossed[i, spot] = copies.push(room["sum"].at[1, spot, :, rest], room["far"].at[spot], across)
+                    for block in range(group * group_blocks, (group + 1) * group_blocks):
+                        crossed[i, block] = copies.push(room["sum"].at[1, block, :, rest], room["far"].at[block], across)
 
     def second(spot):
-        for i, (parts, early, out, room) in enumerate(arrays):
+        block = slot(spot)
+        for i, (source, early, out, room) in enumerate(arrays):
             rest = pl.ds(early, out.shape[1] - early)
-            crossed[i, spot].wait_recv()
-            add_rows(room["sum"].at[0, spot, :, rest], room["far"].at[spot])
+            crossed[i, block].wait_recv()
+            add_rows(room["sum"].at[0, block, :, rest], room["far"].at[block])
 
     def windows(size, hop, upward):
         if hop > 0:
@@ -503,76 +558,86 @@
         target = ahead if upward else behind
         kinds = ("up", "up_slim") if upward else ("down", "down_slim")
         out_copies = []
-        for i, (parts, early, out, room) in enumerate(arrays):
+        for i, (source, early, out, room) in enumerate(arrays):
             for e, size in ((0, out.shape[1]), (1, early)):
                 window = windows(size, hop, upward)
                 out_copies.append(
-                    copies.push(room["sum"].at[e, spot, :, window], room[kinds[e]].at[hop, :, window], target)
+                    copies.push(room["sum"].at[e, slot(spot), :, window], room[kinds[e]].at[hop, :, window], target)
                 )
         return out_copies
 
     def receive(hop, spot, upward, arrivals):
         kinds = ("up", "up_slim") if upward else ("down", "down_slim")
         at = 0
-        for i, (parts, early, out, room) in enumerate(arrays):
+        for i, (source, early, out, room) in enumerate(arrays):
             for e, size in ((0, out.shape[1]), (1, early)):
                 window = windows(size, hop, upward)
                 arrivals[at].wait_recv()
-                add_rows(room["sum"].at[e, spot, :, window], room[kinds[e]].at[hop, :, window])
+                add_rows(room["sum"].at[e, slot(spot), :, window], room[kinds[e]].at[hop, :, window])
                 at += 1
 
+    outgoing(0)
     yield
-    first(half)
+    own(0)
     yield
-    for spot in blocks[1:3]:
-        first(spot)
+    outgoing(1)
+    own(1)
+    yield
     second(half)
     up = send(0, half, True)
     down = send(0, half, False)
+    yield
     for hop in range(1, half):
-        yield
-        for spot in blocks[2 * hop + 1 : 2 * hop + 3]:
-            first(spot)
         second(chips - half + hop)
         second(half - hop)
         receive(hop - 1, chips - half + hop, True, up)
         up = send(hop, chips - half + hop, True)
         receive(hop - 1, half - hop, False, down)
         down = send(hop, half - hop, False)
-    yield
+        yield
     second(0)
-    yield
     final = []
     at = 0
-    for i, (parts, early, out, room) in enumerate(arrays):
+    for i, (source, early, out, room) in enumerate(arrays):
         for e in range(2):
             up[at].wait_recv()
             down[at].wait_recv()
             at += 1
-        size = out.shape[1]
-        part = room["sum"][1, 0, :, :early].astype(jnp.float32)
+        part = room["sum"][1, slot(0), :, :early].astype(jnp.float32)
         part = part + room["up_slim"][half - 1].astype(jnp.float32) + room["down_slim"][half - 1].astype(jnp.float32)
         room["slim_out"][...] = part.astype(room["slim_out"].dtype)
         final.append(copies.push(room["slim_out"], room["slim_in"], across))
     yield
-    for i, (parts, early, out, room) in enumerate(arrays):
-        total = room["sum"][0, 0].astype(jnp.float32) + room["up"][half - 1].astype(jnp.float32)
+    for i, (source, early, out, room) in enumerate(arrays):
+        total = room["sum"][0, slot(0)].astype(jnp.float32) + room["up"][half - 1].astype(jnp.float32)
         out[...] = total + room["down"][half - 1].astype(jnp.float32)
         final[i].wait_recv()
         out[:, :early] += room["slim_in"][...].astype(jnp.float32)
 
 
+def scatter_order(chips, groups):
+    hops = chips // 2 - 1
+    order = [0] * 4
+    for group in range(1, groups):
+        order += [group] * 3
+    order += [0, -1] * hops
+    for group in range(1, groups):
+        order += [group, group - 1] + [group, -1] * hops
+    return order + [groups - 1] + list(range(groups))
+
+
 def scatter_count(chips, arrays):
     half = chips // 2
-    return arrays * (2 * chips + chips + half * 4 + 1)
-
-
-ROOM = ("sum", "near", "far", "up", "down", "up_slim", "down_slim", "slim_out", "slim_in")
+    return arrays * (4 + chips + half * 4 + 1)
+
+
+ROOM = ("outbox", "sum", "near", "far", "up", "down", "up_slim", "down_slim", "slim_out", "slim_in")
 
 
 def scatter_room(chips, rows, columns, early, dtype):
     half = chips // 2
     shapes = (
+        (2, half, rows, columns),
         (2, chips, rows, columns),
         (2, chips, rows, columns),
         (chips, rows, columns - early),
@@ -586,63 +651,91 @@
     return [pltpu.VMEM(shape, dtype) for shape in shapes]
 
 
-def scatter_grads(ring, arrays, collective):
+def scatter_grads(ring, groups, collective, attention=None):
     chips = ring.chips
-    inputs, shapes, rooms = ([], [], [])
-    for parts, early in arrays:
-        height, columns = parts[0][0].shape
-        rows = height // chips
-        inputs += [parts[e][c].reshape(chips, rows, columns) for e in range(2) for c in range(2)]
+    arrays = [member for group in groups for member in group]
+    inputs, counts, shapes, rooms = ([], [], [], [])
+    tokens = 0
+    for lefts, rights, early in arrays:
+        if lefts is None:
+            height, columns = rights[0][0].shape
+            rows = height // chips
+            dtype = rights[0][0].dtype
+            members = [rights[e][c].reshape(chips, rows, columns) for e in range(2) for c in range(2)]
+        else:
+            tokens, height = lefts[0].shape
+            columns = rights[0][0].shape[1]
+            rows = height // chips // 2
+            dtype = jnp.bfloat16
+            members = list(lefts) + list(rights[0]) + list(rights[1])
+        counts.append(len(members))
+        inputs += members
         shapes.append(jax.ShapeDtypeStruct((rows, columns), jnp.float32))
-        rooms += scatter_room(chips, rows, columns, early, parts[0][0].dtype)
+        rooms += scatter_room(chips, rows, columns, early, dtype)
     total = len(arrays)
+    extra, made = ([], [])
+    if attention is not None:
+        qkv, first, grad_heads, lse, slopes, prefix, scale = attention
+        extra = list(qkv) + list(first) + list(grad_heads) + list(lse) + [slopes, prefix]
+        made = [jax.ShapeDtypeStruct(grad_heads[0].shape, jnp.bfloat16)] * 10
 
     def kernel(*refs):
-        ins, outs, scratch = (refs[: 4 * total], refs[4 * total : 5 * total], refs[5 * total :])
+        ins, refs = (refs[: len(inputs)], refs[len(inputs) :])
+        more, refs = (refs[: len(extra)], refs[len(extra) :])
+        outs, refs = (refs[:total], refs[total:])
+        back, scratch = (refs[: len(made)], refs[len(made) :])
         ids = ring.neighbours()
         greet(ids)
-        copies = Copies(*scratch[len(rooms) :])
+        held, sums, send, recv, near = scratch[len(rooms) :]
+        copies = Copies(send, recv, near)
         members = []
-        for i in range(total):
-            parts = [[ins[4 * i + 2 * e + c] for c in range(2)] for e in range(2)]
-            room = dict(zip(ROOM, scratch[i * len(ROOM) : (i + 1) * len(ROOM)]))
-            members.append((parts, arrays[i][1], outs[i], room))
-        run_all(scatter_steps(copies, ids, chips, members))
+        at = 0
+        for i, (lefts, rights, early) in enumerate(arrays):
+            mine = ins[at : at + counts[i]]
+            at += counts[i]
+            if lefts is None:
+                source = ("given", (mine[:2], mine[2:]))
+            else:
+                terms = len(lefts)
+                source = ("product", mine[:terms], (mine[terms : 2 * terms], mine[2 * terms :]))
+            members.append((source, early, outs[i], dict(zip(ROOM, scratch[i * len(ROOM) : (i + 1) * len(ROOM)]))))
+        work = []
+        if attention is not None:
+            parts = [(more[e], more[2 + e], more[4 + e], more[6 + e], back[5 * e : 5 * e + 5]) for e in range(2)]
+            work = backward_work(parts, more[8], more[9][0], scale, sums)
+        running = []
+        for group in groups:
+            running.append(scatter_steps(copies, ids, ring, members[: len(group)], held))
+            members = members[len(group) :]
+        for turn in scatter_order(chips, len(groups)):
+            if turn >= 0:
+                next(running[turn], None)
+            elif work:
+                work.pop(0)()
+        for piece in work:
+            piece()
         copies.finish()
 
-    return pl.pallas_call(
+    pieces = chips // 2 * (inputs[0].shape[1] // chips // 2)
+    outs = pl.pallas_call(
         kernel,
-        in_specs=[pl.BlockSpec(memory_space=pl.ANY)] * (4 * total),
-        out_specs=[pl.BlockSpec(memory_space=pltpu.VMEM)] * total,
-        out_shape=shapes,
+        in_specs=on_vmem(len(inputs)) + (on_vmem(8) + on_smem(2) if extra else []),
+        out_specs=on_vmem(total + len(made)),
+        out_shape=shapes + made,
         scratch_shapes=rooms
         + [
+            pltpu.VMEM((2, pieces, tokens), jnp.bfloat16),
+            pltpu.VMEM((4, tokens, 128), jnp.float32),
             pltpu.SemaphoreType.DMA((scatter_count(chips, total),)),
             pltpu.SemaphoreType.DMA((scatter_count(chips, total),)),
-            pltpu.SemaphoreType.DMA((2 * chips * total,)),
+            pltpu.SemaphoreType.DMA((1,)),
         ],
         compiler_params=pltpu.CompilerParams(
-            collective_id=collective, has_side_effects=True, vmem_limit_bytes=56 * 1024 * 1024
+            collective_id=collective, has_side_effects=True, vmem_limit_bytes=62 * 1024 * 1024
         ),
         name="scatter_grads",
-    )(*inputs)
-
-
-def wide_sum(left, right):
-    return left.astype(jnp.float32) + right.astype(jnp.float32)
-
-
-def grad_parts(left, right, extra=None):
-    half = left.shape[1] // 2
-    parts = []
-    for core in range(2):
-        columns = slice(core * half, (core + 1) * half)
-        out = lax.dot_general(left[:, columns], right, ROWS_CONTRACT, preferred_element_type=jnp.float32)
-        if extra is not None:
-            more = lax.dot_general(extra[0][:, columns], extra[1], ROWS_CONTRACT, preferred_element_type=jnp.float32)
-            out = out + more
-        parts.append(out.astype(jnp.bfloat16))
-    return parts
+    )(*inputs, *extra)
+    return (outs[:total], outs[total:])
 
 
 def small_parts(vector_grads, bias_grads, by_half, placed, piece, lane):
@@ -712,10 +805,9 @@
     for layer in range(layers):
         groups.append([(qkv_weight[layer].reshape(rows, -1), 512), (out_weight[layer].T, 256)])
         groups.append([(up_weight[layer], 768), (down_weight[layer].T, 768)])
-    groups[0].insert(0, (packed, 256))
-    gathered = gather_weights(ring, groups, 1)
-    everything = by_half(jnp.stack([member.reshape(dp, -1) for member in gathered[:2]]), 0)
-    gathered = gathered[2:]
+    weights = gather_weights(ring, [[(packed, 256)] + groups[0]], 1)[0]
+    everything = by_half(jnp.stack([member.reshape(dp, -1) for member in weights[:2]]), 0)
+    gathered = weights[2:]
     vectors = everything[:, :, :first].reshape(tensor, dp, 6, layers, piece).transpose(2, 3, 1, 0, 4)
     small = vectors.reshape(6, layers, 1, width).astype(f32)
     lane = qkv_bias.shape[3]
@@ -733,29 +825,29 @@
     heads_half = H // tensor
     heads = (pieces // heads_half ^ side) * heads_half + pieces % heads_half
     slopes = jnp.exp2(-(heads.astype(f32) + 1.0) * 8.0 / H) * LOG2E
-    meta = jnp.stack([side.astype(jnp.int32), prefix_len[0]])
 
     before_first = lax.ppermute(states_in[0], "tensor", [(0, 1)])
     states = into_ring(states_in[0])
     target = into_ring(teacher[0])
     kept = []
     for layer in range(layers):
-        qkv_proj, out_proj, up_proj, down_proj = [gathered[8 * layer + i : 8 * layer + i + 2] for i in (0, 2, 4, 6)]
+        qkv_proj, out_proj = (gathered[8 * layer : 8 * layer + 2], gathered[8 * layer + 2 : 8 * layer + 4])
         normed = norm_rows(states, small[0][layer], small[1][layer]).astype(low)
         if layer == 0:
             normed_first = norm_rows(into_ring(before_first), small[0][layer], small[1][layer]).astype(low)
         else:
             normed_first = lax.ppermute(normed, "tensor", [(0, 1)])
-        qkv, kv_first, heads_out, lse = ([], [], [], [])
+        qkv, kv_first = ([], [])
         for i in range(tensor):
             query = qkv_proj[i].shape[1] // 3
             mixed = jnp.dot(normed, qkv_proj[i], preferred_element_type=f32) + qkv_add[layer][i]
             qkv.append(mixed.astype(low))
             mixed = jnp.dot(normed_first, qkv_proj[i][:, query:], preferred_element_type=f32)
             kv_first.append((mixed + qkv_add[layer][i][:, query:]).astype(low))
-            made, total = attention_forward(meta, slopes[i * heads_half : (i + 1) * heads_half], qkv[i], kv_first[i], scale)
-            heads_out.append(made)
-            lse.append(total)
+        coming = groups[2 * layer + 1 : 2 * layer + 3]
+        weights, heads_out, lse = gather_weights(ring, coming, 2 + layer, (qkv, kv_first, slopes, prefix_len, scale))
+        gathered += weights
+        up_proj, down_proj = (gathered[8 * layer + 4 : 8 * layer + 6], gathered[8 * layer + 6 : 8 * layer + 8])
         middle = states + mm(heads_out[0], out_proj[0], NT) + mm(heads_out[1], out_proj[1], NT) + small[2][layer]
         normed_two = norm_rows(middle, small[3][layer], small[4][layer]).astype(low)
         hidden = [jnp.dot(normed_two, up_proj[i], preferred_element_type=f32) + up_add[layer][i] for i in range(tensor)]
@@ -778,45 +870,53 @@
         for i in range(tensor):
             grad_active = jnp.dot(grad_mlp, down_proj[i], preferred_element_type=f32)
             grad_hidden.append(jax.vjp(gelu_tanh, hidden[i])[1](grad_active)[0].astype(low))
-        down_parts = [grad_parts(grad_mlp, active[i]) for i in range(tensor)]
         up_shift = jnp.stack([jnp.sum(values.astype(f32), axis=0) for values in grad_hidden])
         grad_normed = mm(grad_hidden[0], up_proj[0], NT) + mm(grad_hidden[1], up_proj[1], NT)
-        up_parts = [grad_parts(normed_two, grad_hidden[i]) for i in range(tensor)]
-        up_grad, down_grad = scatter_grads(ring, [(up_parts, 768), (down_parts, 768)], 2 + 2 * layer)
         part, gain_two, shift_two = norm_back(middle, small[3][layer], grad_normed)
         grad_middle = grad + part
         grad_attn = grad_middle.astype(low)
         out_shift = jnp.sum(grad_attn.astype(f32), axis=0)
+        grad_heads = [jnp.dot(grad_attn, out_proj[i], preferred_element_type=f32).astype(low) for i in range(tensor)]
+        (down_grad, up_grad), grads = scatter_grads(
+            ring,
+            [
+                [([grad_mlp], [[values] for values in active], 768)],
+                [([normed_two], [[values] for values in grad_hidden], 768)],
+            ],
+            10 + 2 * layer,
+            (qkv, kv_first, grad_heads, lse, slopes, prefix_len, scale),
+        )
         grad_normed = 0.0
         qkv_shift = []
         sent = 0.0
-        query_parts, rest_parts, out_parts = ([], [], [])
+        query_terms, rest_terms = ([], [])
         for i in range(tensor):
-            grad_heads = jnp.dot(grad_attn, out_proj[i], preferred_element_type=f32).astype(low)
-            out_parts.append(grad_parts(grad_attn, heads_out[i]))
-            grads = attention_backward(
-                meta, slopes[i * heads_half : (i + 1) * heads_half], qkv[i], kv_first[i], grad_heads, lse[i], scale
-            )
-            grad_qkv = jnp.concatenate(grads[:3], axis=1)
-            grad_first = jnp.concatenate(grads[3:], axis=1)
-            query = grads[0].shape[1]
+            query = grads[5 * i].shape[1]
+            grad_qkv = jnp.concatenate(grads[5 * i : 5 * i + 3], axis=1)
+            grad_first = jnp.concatenate(grads[5 * i + 3 : 5 * i + 5], axis=1)
             sent = sent + mm(grad_first, qkv_proj[i][:, query:], NT)
-            query_parts.append(grad_parts(normed, grads[0]))
-            rest_parts.append(grad_parts(normed, grad_qkv[:, query:], (normed_first, grad_first)))
+            query_terms.append([grads[5 * i]])
+            rest_terms.append([grad_qkv[:, query:], grad_first])
             shift = jnp.sum(grad_qkv.astype(f32), axis=0)
             qkv_shift.append(shift + jnp.pad(jnp.sum(grad_first.astype(f32), axis=0), (query, 0)))
             grad_normed = grad_normed + mm(grad_qkv, qkv_proj[i], NT)
         arrived = lax.ppermute(sent.astype(low), "tensor", [(1, 0)])
         qkv_shift = jnp.stack(qkv_shift)
-        projections = [(query_parts, 256), (rest_parts, 256), (out_parts, 256)]
+        projections = [
+            [
+                ([grad_attn], [[values] for values in heads_out], 256),
+                ([normed], query_terms, 256),
+                ([normed, normed_first], rest_terms, 256),
+            ]
+        ]
         grad_normed = grad_normed + arrived.astype(f32)
         part, gain_one, shift_one = norm_back(before, small[0][layer], grad_normed)
         grad = grad_middle + part
         vector_grads[layer] = (gain_one, shift_one, out_shift, gain_two, shift_two, down_shift)
         bias_grads[layer] = (qkv_shift, up_shift)
         if layer == 0:
-            projections.append((small_parts(vector_grads, bias_grads, by_half, placed, piece, lane), 256))
-        query_grad, rest_grad, out_grad, *last = scatter_grads(ring, projections, 3 + 2 * layer)
+            projections[0].append((None, small_parts(vector_grads, bias_grads, by_half, placed, piece, lane), 256))
+        (out_grad, query_grad, rest_grad, *last), unused = scatter_grads(ring, projections, 11 + 2 * layer)
         qkv_grad = jnp.concatenate([query_grad, rest_grad], axis=1).reshape(rows, 3, -1)
         weight_grads[layer] = (qkv_grad, out_grad.T, up_grad, down_grad)
 

time: 949 us -> 864 us (0.910)
  matrix products: 233 us -> 139 us
  Pallas kernels: 588 us -> 537 us
  waiting for transfers between devices: 18.4 us -> 48.1 us
  local copies, waits for them, and re-layouts: 53.6 us -> 80.1 us
    dot_general x48 -> x0, matrix products: 93.6 us -> none  [the longest x40 79.8 us: grad_parts(): lax.dot_general(left[:, columns], right, ROWS_CONTRACT, preferred_element...]
    pallas_call x13 -> x7, Pallas kernels: 588 us -> 537 us  [the longest x4 313 us: scatter_grads(): pl.pallas_call(kernel, in_specs=on_vmem(len(inputs)) + (on_vmem(8) + on_s...]
    ppermute x2, waiting for transfers between devices: 0.01 us -> 29.9 us  [local(): arrived = lax.ppermute(sent.astype(low), 'tensor', [(1, 0)])]
    unnamed x291 -> x341, local copies, waits for them, and re-layouts: 29.7 us -> 40.5 us
  transfers between devices with their start and end apart: 4 -> 4, of which waited for: 1 -> 3; matrix products, arithmetic and copies ran while one was open for 7% -> 7% of each run, Pallas kernels for 48% -> 5%
where the time goes in v3:
time: 864 us; the launch traced here: 855 us
  Pallas kernels  537 us (62%)
  matrix products  139 us (16%)
  local copies, waits for them, and re-layouts  80.1 us (9%)
  waiting for transfers between devices  48.1 us (6%)
  other arithmetic  32.9 us (4%)
  starting transfers between devices  10.8 us (1%)
    pallas_call x4, Pallas kernels, scatter_grads(): pl.pallas_call(kernel, in_specs=on_vmem(len(inputs)) + (on_vmem(8) + on_s...  313 us
    pallas_call x3, Pallas kernels, gather_weights(): pl.pallas_call(kernel, in_specs=anywhere(total) + (on_vmem(4) + on_smem(2...  224 us
    dot_general x20, matrix products, mm(): return lax.dot_general(a, b, dims, preferred_element_type=jnp.float32)  53.6 us
    unnamed x341, local copies, waits for them, and re-layouts  40.5 us
    ppermute x2, waiting for transfers between devices, local(): arrived = lax.ppermute(sent.astype(low), 'tensor', [(1, 0)])  29.9 us
    dot_general x4, matrix products, local(): grad_active = jnp.dot(grad_mlp, down_proj[i], preferred_element_type=f32)  24.9 us
    dot_general x4, matrix products, local(): jnp.dot(normed_two, up_proj[i], preferred_element_type=f32)  20.9 us
    ppermute x1, waiting for transfers between devices, local(): normed_first = lax.ppermute(normed, 'tensor', [(0, 1)])  18.1 us
  transfers between devices with their start and end apart: 4, of which 3 were waited for; matrix products, arithmetic and copies ran while one was open for 7% of the time, Pallas kernels for 5%

profile of v3, /device:TPU:0, one launch (start us, length us, event | category | flops | bytes accessed | tf_op | source)
XLA Modules:
  0.0 855.2 jit_solution(7897025560676422069)
XLA Ops:
  0.7 6.0 collective-permute-start
  20.8 43.4 %gather_weights.3 = (bf16[2,8,16,512]{3,2,1,0:T(8,128)(2,1)S(1)}, bf16[2,8,16,512]{3,2,1,0:T(8,128)(2,1)S(1)}, bf16[2,8,64,1536]{3,2,1,0:T(8,128)(2,1)S(1)}, bf1...) custom-call(bf16[16,512]{1,0:T(8,128)(2,1)S(1)} %reshape.394.refs_0_, ...), custom_call_target="tpu_custom_call" | custom-call | tf_op jit(solution)/shard_map/gather_weights/pallas_call | solution.py:435
  71.4 2.6 fusion.122
  74.0 2.9 copy.81
  90.1 2.1 add_convert_fusion.10.refs_3_.refs_6_
  93.4 3.0 fusion.29.refs_5_.refs_7_
  96.4 3.0 fusion.28.refs_4_.refs_6_
  99.3 3.8 fusion.123
  103.2 3.4 copy.92
  106.6 2.1 multiply_reduce_fusion.11
  114.3 105.6 %gather_weights.4 = (bf16[2,8,64,2048]{3,2,1,0:T(8,128)(2,1)}, bf16[2,8,64,2048]{3,2,1,0:T(8,128)(2,1)}, bf16[2,8,64,2048]{3,2,1,0:T(8,128)(2,1)}, bf16[2,8,64,2...) custom-call(bf16[64,2048]{1,0:T(8,128)(2,1)S(1)} %get-tuple-element., ...), custom_call_target="tpu_custom_call" | custom-call | tf_op jit(solution)/shard_map/gather_weights/pallas_call | solution.py:435
  225.6 2.1 copy-done.132
  227.7 5.2 multiply_convert_fusion.2
  232.9 5.2 multiply_convert_fusion.3
  238.2 2.4 fusion.128
  241.1 3.1 fusion.125
  252.2 18.1 %collective-permute-done.1.refs_7_ = bf16[512,1024]{1,0:T(8,128)(2,1)S(1)} collective-permute-done((bf16[512,1024]{1,0:T(8,128)(2,1)S(1)}, bf16[512,1024]{1,0:T(8,128)(2,1)S(1)}, u32[]{:S(2)}, u32[]{:S(2)}) %collective-permute-start.1) | collective-permute-done | bytes 1048608 | tf_op jit(solution)/shard_map/ppermute | solution.py:839
  272.9 74.6 %gather_weights.5 = (bf16[2,8,64,2048]{3,2,1,0:T(8,128)(2,1)S(1)}, bf16[2,8,64,2048]{3,2,1,0:T(8,128)(2,1)}, bf16[2,8,64,2048]{3,2,1,0:T(8,128)(2,1)}, bf16[2,8,...) custom-call(bf16[64,2048]{1,0:T(8,128)(2,1)S(1)} %get-tuple-element., ...), custom_call_target="tpu_custom_call" | custom-call | tf_op jit(solution)/shard_map/gather_weights/pallas_call | solution.py:435
  351.9 5.2 multiply_convert_fusion
  357.1 5.3 multiply_convert_fusion.1
  362.4 2.4 fusion.130
  364.9 4.9 add_add_fusion
  373.1 7.4 convert_reduce_fusion
  380.5 6.1 convert_reduce_fusion.1
  386.6 2.4 fusion.131
  389.0 3.0 multiply_reduce_fusion
  392.0 2.1 convert_reduce_fusion.14
  397.1 99.1 %scatter_grads.4 = (f32[64,2048]{1,0:T(8,128)}, f32[64,2048]{1,0:T(8,128)}, bf16[512,512]{1,0:T(8,128)(2,1)}, bf16[512,512]{1,0:T(8,128)(2,1)}, bf16[512,512]{1,...) custom-call(bf16[512,1024]{1,0:T(8,128)(2,1)} %copy-done.88, ...), custom_call_target="tpu_custom_call" | custom-call | tf_op jit(solution)/shard_map/scatter_grads/pallas_call | solution.py:720
  498.8 2.7 fusion.50
  507.5 56.2 %scatter_grads.7 = (f32[64,512]{1,0:T(8,128)}, f32[64,512]{1,0:T(8,128)}, f32[64,1024]{1,0:T(8,128)}) custom-call(bf16[512,1024]{1,0:T(8,128)(2,1)} %copy-done.50, bf16[512,512]{1,0:T(8,128)(2,1)} %copy-done.10, bf16[512,512]{1,0:T(8,128)(2,1)} %copy-done.11, bf16[512,1024]{1,0:T(8,128)(2,1)} %copy-done.42, bf16[512,512]{1,0:T(8,128)(2,1)} %get-tuple-element.95.refs_4_, ...), custom_call_target="tpu_custom_call" | custom-call | tf_op jit(solution)/shard_map/scatter_grads/pallas_call | solution.py:720
  565.8 3.7 add_convert_fusion.1
  572.8 2.3 fusion.83
  577.0 18.3 %collective-permute-done.2 = bf16[512,1024]{1,0:T(8,128)(2,1)S(1)} collective-permute-done((bf16[512,1024]{1,0:T(8,128)(2,1)S(1)}, bf16[512,1024]{1,0:T(8,128)(2,1)S(1)}, u32[]{:S(2)}, u32[]{:S(2)}) %collective-permute-start.2) | collective-permute-done | bytes 1048608 | tf_op jit(solution)/shard_map/ppermute | solution.py:903
  595.3 2.6 multiply_reduce_fusion.2
  601.9 5.8 convert_reduce_fusion.2
  607.8 5.7 convert_reduce_fusion.3
  613.5 2.4 fusion.133
  617.0 3.0 multiply_reduce_fusion.1
  625.3 94.0 %scatter_grads.5 = (f32[64,2048]{1,0:T(8,128)}, f32[64,2048]{1,0:T(8,128)}, bf16[512,512]{1,0:T(8,128)(2,1)}, bf16[512,512]{1,0:T(8,128)(2,1)}, bf16[512,512]{1,...) custom-call(bf16[512,1024]{1,0:T(8,128)(2,1)} %copy-done.51, ...), custom_call_target="tpu_custom_call" | custom-call | tf_op jit(solution)/shard_map/scatter_grads/pallas_call | solution.py:720
  722.0 2.6 fusion.58
  730.9 2.3 pad_maximum_fusion.refs_8_
  739.6 4.9 add_convert_fusion
  750.3 2.4 pad_maximum_fusion.5
  753.8 3.4 fusion.134
  757.2 11.6 %collective-permute-done.3 = bf16[512,1024]{1,0:T(8,128)(2,1)} collective-permute-done((bf16[512,1024]{1,0:T(8,128)(2,1)}, bf16[512,1024]{1,0:T(8,128)(2,1)}, u32[]{:S(2)}, u32[]{:S(2)}) %collective-permute-start.3) | collective-permute-done | bytes 1048608 | tf_op jit(solution)/shard_map/ppermute | solution.py:903
  768.8 5.0 multiply_reduce_fusion.3
  776.2 63.6 %scatter_grads.6 = (f32[64,512]{1,0:T(8,128)}, f32[64,512]{1,0:T(8,128)}, f32[64,1024]{1,0:T(8,128)}, f32[8,512]{1,0:T(8,128)}) custom-call(bf16[512,1024]{1,0:T(8,128)(2,1)} %copy-done.54, bf16[512,512]{1,0:T(8,128)(2,1)} %copy-done.12, bf16[512,512]{1,0:T(8,128)(2,1)} %copy-done.13, bf16[512,1024]{1,0:T(8,128)(2,1)} %copy-done.43, ...), custom_call_target="tpu_custom_call" | custom-call | tf_op jit(solution)/shard_map/scatter_grads/pallas_call | solution.py:720
  847.6 7.4 fusion.67
  (512 shorter events, 121.0 us)
Async XLA Ops:
  0.6 369.1 %copy-start = (bf16[1,512,1024]{2,1,0:T(8,128)(2,1)S(1)}, bf16[1,512,1024]{2,1,0:T(8,128)(2,1)}, u32[]{:S(2)}) copy-start(bf16[1,512,1024]{2,1,0:T(8,128)(2,1)} %param.18) | copy-start | bytes 3145732
  0.7 98.7 %collective-permute-start = (bf16[512,1024]{1,0:T(8,128)(2,1)}, bf16[512,1024]{1,0:T(8,128)(2,1)}, u32[]{:S(2)}, u32[]{:S(2)}) collective-permute-start(bf16[512,1024]{1,0:T(8,128)(2,1)} %bitcast.360), channel_id=1, source_target_pairs={{0,1},{2,3},{4,5},{6,7},{8,9},{10,11},{12,13},{14,15},{16,17},{18,... | collective-permute-start | bytes 3145736 | tf_op jit(solution)/shard_map/ppermute | solution.py:829
  11.2 74.4 %copy-start.129 = (s32[16]{0:T(128)}, s32[16]{0:T(128)S(1)}, u32[]{:S(2)}) copy-start(s32[16]{0:T(128)S(1)} %dynamic-slice_bitcast_fusion) | copy-start | bytes 196
  68.4 151.6 %copy-start.14 = (bf16[2,8,64,512]{3,2,1,0:T(8,128)(2,1)}, bf16[2,8,64,512]{3,2,1,0:T(8,128)(2,1)S(1)}, u32[]{:S(2)}) copy-start(bf16[2,8,64,512]{3,2,1,0:T(8,128)(2,1)S(1)} %get-tuple-element.76) | copy-start | bytes 3145732
  84.8 140.0 %copy-start.99 = (f32[1,1,1,1024]{3,1,0,2:T(1,128)}, f32[1,1,1,1024]{3,1,0,2:T(1,128)S(1)}, u32[]{:S(2)}) copy-start(f32[1,1,1,1024]{3,1,0,2:T(1,128)S(1)} %get-tuple-element.235) | copy-start | bytes 12292
  84.8 159.7 %copy-start.101 = (f32[1,1,1,1024]{3,1,0,2:T(1,128)}, f32[1,1,1,1024]{3,1,0,2:T(1,128)S(1)}, u32[]{:S(2)}) copy-start(f32[1,1,1,1024]{3,1,0,2:T(1,128)S(1)} %get-tuple-element.232) | copy-start | bytes 12292
  84.8 162.3 %copy-start.97 = (f32[1,1,1,1024]{3,1,0,2:T(1,128)}, f32[1,1,1,1024]{3,1,0,2:T(1,128)S(1)}, u32[]{:S(2)}) copy-start(f32[1,1,1,1024]{3,1,0,2:T(1,128)S(1)} %get-tuple-element.238) | copy-start | bytes 12292
  86.9 6.1 copy-start.89
  92.3 180.6 %copy-start.23 = (f32[16]{0:T(128)}, f32[16]{0:T(128)S(1)}, u32[]{:S(2)}) copy-start(f32[16]{0:T(128)S(1)} %fusion.108.refs_8_.refs_6_.refs_14_) | copy-start | bytes 196
  113.7 106.2 %copy-start.7 = (bf16[512,1024]{1,0:T(8,128)(2,1)}, bf16[512,1024]{1,0:T(8,128)(2,1)S(1)}, u32[]{:S(2)}) copy-start(bf16[512,1024]{1,0:T(8,128)(2,1)S(1)} %add_convert_fusion.7.refs_7_.refs_9_) | copy-start | bytes 3145732
  220.0 51.6 %copy-start.32 = (bf16[2,8,64,1536]{3,2,1,0:T(8,128)(2,1)}, bf16[2,8,64,1536]{3,2,1,0:T(8,128)(2,1)S(1)}, u32[]{:S(2)}) copy-start(bf16[2,8,64,1536]{3,2,1,0:T(8,128)(2,1)S(1)} %get-tuple-element.83) | copy-start | bytes 9437188
  224.4 16.2 %copy-start.38 = (f32[512,1024]{1,0:T(8,128)}, f32[512,1024]{1,0:T(8,128)S(1)}, u32[]{:S(2)}) copy-start(f32[512,1024]{1,0:T(8,128)S(1)} %get-tuple-element.254) | copy-start | bytes 6291460
  224.8 8.2 copy-start.106
  225.6 7.3 copy-start.52
  232.9 7.6 copy-start.60
  244.1 104.2 %copy-start.40 = (f32[512,1024]{1,0:T(8,128)}, f32[512,1024]{1,0:T(8,128)S(1)}, u32[]{:S(2)}) copy-start(f32[512,1024]{1,0:T(8,128)S(1)} %get-tuple-element.260) | copy-start | bytes 6291460
  245.3 25.0 %collective-permute-start.1 = (bf16[512,1024]{1,0:T(8,128)(2,1)S(1)}, bf16[512,1024]{1,0:T(8,128)(2,1)S(1)}, u32[]{:S(2)}, u32[]{:S(2)}) collective-permute-start(bf16[512,1024]{1,0:T(8,128)(2,1)S(1)} %add_convert_fusion.5.refs_3_.refs_6_), channel_id=1, source_target_pairs={{0,1},{2,3},{4,5},{6,7},{8,9},{10,11},{12,13},{14,15},{16,17},{18,... | collective-permute-start | bytes 3145736 | tf_op jit(solution)/shard_map/ppermute | solution.py:839
  250.3 22.6 %copy-start.4 = (bf16[512,1536]{1,0:T(8,128)(2,1)}, bf16[512,1536]{1,0:T(8,128)(2,1)S(1)}, u32[]{:S(2)}) copy-start(bf16[512,1536]{1,0:T(8,128)(2,1)S(1)} %fusion.31.refs_3_.refs_7_) | copy-start | bytes 4718596
  252.1 20.8 %copy-start.5 = (bf16[512,1536]{1,0:T(8,128)(2,1)}, bf16[512,1536]{1,0:T(8,128)(2,1)S(1)}, u32[]{:S(2)}) copy-start(bf16[512,1536]{1,0:T(8,128)(2,1)S(1)} %fusion.30.refs_2_.refs_6_) | copy-start | bytes 4718596
  272.9 74.7 %copy-start.9 = (bf16[512,1024]{1,0:T(8,128)(2,1)}, bf16[512,1024]{1,0:T(8,128)(2,1)S(1)}, u32[]{:S(2)}) copy-start(bf16[512,1024]{1,0:T(8,128)(2,1)S(1)} %add_convert_fusion.4.refs_4_.refs_8_) | copy-start | bytes 3145732
  350.4 6.7 copy-start.53
  357.1 7.7 copy-start.62
  357.1 5.3 copy-start.141
  371.2 9.3 %copy-start.88 = (bf16[512,1024]{1,0:T(8,128)(2,1)}, bf16[512,1024]{1,0:T(8,128)(2,1)S(1)}, u32[]{:S(2)}) copy-start(bf16[512,1024]{1,0:T(8,128)(2,1)S(1)} %get-tuple-element.191.refs_0_) | copy-start | bytes 3145732
  373.1 7.4 copy-start.151
  380.5 8.5 copy-start.64
  507.4 58.3 %copy-start.47 = (bf16[512,1024]{1,0:T(8,128)(2,1)S(1)}, bf16[512,1024]{1,0:T(8,128)(2,1)}, u32[]{:S(2)}) copy-start(bf16[512,1024]{1,0:T(8,128)(2,1)} %copy-done.46) | copy-start | bytes 3145732
  571.5 23.8 %collective-permute-start.2 = (bf16[512,1024]{1,0:T(8,128)(2,1)S(1)}, bf16[512,1024]{1,0:T(8,128)(2,1)S(1)}, u32[]{:S(2)}, u32[]{:S(2)}) collective-permute-start(bf16[512,1024]{1,0:T(8,128)(2,1)S(1)} %add_convert_fusion.1), channel_id=1, source_target_pairs={{1,0},{3,2},{5,4},{7,6},{9,8},{11,10},{13,12},{15,14},{17,16},{19,... | collective-permute-start | bytes 3145736 | tf_op jit(solution)/shard_map/ppermute | solution.py:903
  575.2 20.2 %copy-start.41 = (f32[512,1024]{1,0:T(8,128)S(1)}, f32[512,1024]{1,0:T(8,128)}, u32[]{:S(2)}) copy-start(f32[512,1024]{1,0:T(8,128)} %copy-done.40) | copy-start | bytes 6291460
  575.2 20.2 %copy-start.102 = (f32[1,1,1,1024]{3,1,0,2:T(1,128)S(1)}, f32[1,1,1,1024]{3,1,0,2:T(1,128)}, u32[]{:S(2)}) copy-start(f32[1,1,1,1024]{3,1,0,2:T(1,128)} %copy-done.101) | copy-start | bytes 12292
  575.2 20.2 %copy-start.145 = (bf16[2,8,64,1536]{3,2,1,0:T(8,128)(2,1)S(1)}, bf16[2,8,64,1536]{3,2,1,0:T(8,128)(2,1)}, u32[]{:S(2)}) copy-start(bf16[2,8,64,1536]{3,2,1,0:T(8,128)(2,1)} %get-tuple-element.84) | copy-start | bytes 9437188
  577.0 21.0 %copy-start.44 = (f32[512,1024]{1,0:T(8,128)S(1)}, f32[512,1024]{1,0:T(8,128)}, u32[]{:S(2)}) copy-start(f32[512,1024]{1,0:T(8,128)} %get-tuple-element.197) | copy-start | bytes 6291460
  598.9 8.9 %copy-start.51 = (bf16[512,1024]{1,0:T(8,128)(2,1)}, bf16[512,1024]{1,0:T(8,128)(2,1)S(1)}, u32[]{:S(2)}) copy-start(bf16[512,1024]{1,0:T(8,128)(2,1)S(1)} %get-tuple-element.193.refs_0_) | copy-start | bytes 3145732
  601.9 5.9 copy-start.137
  601.9 5.9 copy-start.149
  607.7 8.2 copy-start.65
  607.8 5.7 copy-start.135
  739.6 6.6 copy-start.130
  739.6 6.9 copy-start.72
  739.6 6.9 copy-start.74
  744.5 24.2 %collective-permute-start.3 = (bf16[512,1024]{1,0:T(8,128)(2,1)}, bf16[512,1024]{1,0:T(8,128)(2,1)}, u32[]{:S(2)}, u32[]{:S(2)}) collective-permute-start(bf16[512,1024]{1,0:T(8,128)(2,1)} %add_convert_fusion), channel_id=1, source_target_pairs={{1,0},{3,2},{5,4},{7,6},{9,8},{11,10},{13,12},{15,14},{17,16},{19,... | collective-permute-start | bytes 3145736 | tf_op jit(solution)/shard_map/ppermute | solution.py:903
  753.8 15.0 %copy-start.35 = (f32[1024,512]{0,1:T(8,128)S(1)}, f32[1024,512]{0,1:T(8,128)}, u32[]{:S(2)}) copy-start(f32[1024,512]{0,1:T(8,128)} %copy.81) | copy-start | bytes 6291460
  753.8 15.0 %copy-start.59 = (bf16[512,1536]{1,0:T(8,128)(2,1)S(1)}, bf16[512,1536]{1,0:T(8,128)(2,1)}, u32[]{:S(2)}) copy-start(bf16[512,1536]{1,0:T(8,128)(2,1)} %copy-done.58) | copy-start | bytes 4718596
  753.8 15.0 %copy-start.98 = (f32[1,1,1,1024]{3,1,0,2:T(1,128)S(1)}, f32[1,1,1,1024]{3,1,0,2:T(1,128)}, u32[]{:S(2)}) copy-start(f32[1,1,1,1024]{3,1,0,2:T(1,128)} %copy-done.97) | copy-start | bytes 12292
  753.8 15.0 %copy-start.109 = (f32[512]{0:T(512)S(1)}, f32[512]{0:T(512)}, u32[]{:S(2)}) copy-start(f32[512]{0:T(512)} %copy-done.108) | copy-start | bytes 6148
  753.8 15.0 %copy-start.119 = (f32[512]{0:T(512)S(1)}, f32[512]{0:T(512)}, u32[]{:S(2)}) copy-start(f32[512]{0:T(512)} %add_rsqrt_fusion.4) | copy-start | bytes 6148
  776.2 70.2 %copy-start.95 = (f32[64,512]{1,0:T(8,128)S(1)}, f32[64,512]{1,0:T(8,128)}, u32[]{:S(2)}) copy-start(f32[64,512]{1,0:T(8,128)} %get-tuple-element.123) | copy-start | bytes 393220
  847.6 7.4 copy-start.1
  (108 other events, 285.1 us)

commit v4 on v3

--- a/solution.py
+++ b/solution.py
@@ -170,7 +170,8 @@
                 rows // 2,
             )
 
-        work.append(functools.partial(head_pairs, 0, pairs, body))
+        for low in range(0, pairs, 2):
+            work.append(functools.partial(head_pairs, low, low + 2, body))
     return work
 
 
@@ -428,8 +429,8 @@
         work = []
         if attention is not None:
             parts = [(extra[e], extra[2 + e], made[e], made[2 + e]) for e in range(2)]
-            work = forward_work(parts, extra[4], extra[5][0], scale)
-        run_staggered(running, 3, work)
+            work = [(piece, None) for piece in forward_work(parts, extra[4], extra[5][0], scale)]
+        run_staggered(running, (3,), work)
         copies.finish()
 
     outs = pl.pallas_call(
@@ -451,24 +452,176 @@
     return (weights, outs[2 * total : 2 * total + 2], outs[2 * total + 2 :])
 
 
-def run_staggered(running, lead, work=()):
-    waiting, work = (list(running), list(work))
-    active = []
-    youngest = lead
+def run_staggered(running, leads, work=(), most=1):
+    waiting, work = (list(enumerate(running)), list(work))
+    active, ended = ([], {None})
+    leads = list(leads)
+    needed, youngest = (0, 0)
     while waiting or active:
-        if waiting and youngest >= lead:
+        if waiting and (youngest >= needed or not active):
             active.append(waiting.pop(0))
-            youngest = 0
+            needed, youngest = (leads.pop(0) if leads else 0, 0)
         youngest += 1
-        for steps in list(active):
+        for member in list(active):
             try:
-                next(steps)
+                next(member[1])
             except StopIteration:
-                active.remove(steps)
-        if work:
-            work.pop(0)()
-    for piece in work:
+                active.remove(member)
+                ended.add(member[0])
+        for unused in range(most):
+            if work and work[0][1] in ended:
+                work.pop(0)[0]()
+    for piece, need in work:
         piece()
+
+
+def unit_rows(values):
+    centered = values - jnp.mean(values, axis=-1, keepdims=True)
+    return centered * lax.rsqrt(jnp.mean(centered * centered, axis=-1, keepdims=True) + EPS)
+
+
+def row_chunks(rows, body):
+    step = 256
+
+    @pl.loop(0, rows // step)
+    def chunk(i):
+        body(pl.ds(pl.multiple_of(i * step, step), step))
+
+
+FORWARD_SPANS = ((0, 1536, (512, 512)), (1536, 512, (256, 256)))
+FORWARD_LEADS = (3, 3)
+
+
+def forward_layer(ring, mlp, coming, collective, attention, states, out_proj, vectors, up_add):
+    qkv, first, slopes, prefix, scale = attention
+    shards = list(mlp) + [shard for shard, early in coming]
+    total = len(shards)
+    chips = ring.chips
+    tokens, width = states.shape
+    inner = mlp[0].shape[1]
+    rows = mlp[0].shape[0]
+    heads = qkv[0].shape[1] // 3
+    tile = 512
+    spans = FORWARD_SPANS
+    count = len(spans) * gather_count(chips, 2) + gather_count(chips, max(len(coming), 1)) + 1
+    shapes = [jax.ShapeDtypeStruct((2, chips) + shard.shape, shard.dtype) for shard in shards for unused in range(2)]
+    f32, low = (jnp.float32, jnp.bfloat16)
+    more = [jax.ShapeDtypeStruct((tokens, heads), low)] * 2
+    more += [jax.ShapeDtypeStruct((heads // 128, 2, tokens), f32)] * 2
+    more += [jax.ShapeDtypeStruct((tokens, width), f32), jax.ShapeDtypeStruct((tokens, width), low)]
+    more += [jax.ShapeDtypeStruct((tokens, inner), f32)] * 2 + [jax.ShapeDtypeStruct((tokens, inner), low)] * 2
+    more += [jax.ShapeDtypeStruct((tokens, width), f32)]
+    if coming:
+        more += [jax.ShapeDtypeStruct((tokens, width), low)] * 2
+    inputs = list(qkv) + list(first) + [states] + list(out_proj) + [vectors, up_add, slopes, prefix]
+
+    def kernel(*refs):
+        sources, refs = (refs[:total], refs[total:])
+        qkv, first, (states, out_0, out_1, vectors, up_add, slopes, prefix) = (refs[:2], refs[2:4], refs[4:11])
+        outs, refs = (refs[11 : 11 + 2 * total], refs[11 + 2 * total :])
+        heads_out, lse, middle, normed, hidden, active, after = (refs[:2], refs[2:4], refs[4], refs[5], refs[6:8], refs[8:10], refs[10])
+        following, scratch = (refs[11 : len(more)], refs[len(more) :])
+        up_tile, down_tile, send, recv, near = scratch
+        ids = ring.neighbours()
+        greet(ids)
+        copies = Copies(send, recv, near)
+        running = []
+        for column, size, earlies in spans:
+            window = pl.ds(column, size)
+            members = []
+            for i, early in enumerate(earlies):
+                views = [outs[2 * i + j].at[:, :, :, window] for j in range(2)]
+                members.append((sources[i].at[:, window], views[0], views[1], early))
+            running.append(gather_steps(copies, ids, ring, members))
+        if coming:
+            members = [(sources[2 + i], outs[4 + 2 * i], outs[5 + 2 * i], coming[i][1]) for i in range(len(coming))]
+            running.append(gather_steps(copies, ids, ring, members))
+        parts = [(qkv[e], first[e], heads_out[e], lse[e]) for e in range(2)]
+        work = [(piece, None) for piece in forward_work(parts, slopes, prefix[0], scale)]
+
+        def project():
+            def body(span):
+                value = states[span] + mm(heads_out[0][span], out_0[...], NT) + mm(heads_out[1][span], out_1[...], NT)
+                value = value + vectors[0:1]
+                middle[span] = value
+                normed[span] = (unit_rows(value) * vectors[1:2] + vectors[2:3]).astype(low)
+                after[span] = value + vectors[3:4]
+
+            row_chunks(tokens, body)
+
+        work.append((project, None))
+        tiles = [
+            (group, e, column + i * tile)
+            for group, (column, size, earlies) in enumerate(spans)
+            for e in range(2)
+            for i in range(size // tile)
+        ]
+        loads = {}
+
+        def load(spot):
+            half, e, column = tiles[spot]
+            window = pl.ds(column, tile)
+            loads[spot] = [
+                copies.move(outs[e].at[:, :, :, window], up_tile.at[spot % 2]),
+                copies.move(outs[2 + e].at[:, :, :, window], down_tile.at[spot % 2]),
+            ]
+
+        def feed(spot):
+            half, e, column = tiles[spot]
+            if spot not in loads:
+                load(spot)
+            for copy in loads[spot]:
+                copy.wait()
+            if spot + 1 < len(tiles) and tiles[spot + 1][0] == half:
+                load(spot + 1)
+            up = up_tile.at[spot % 2]
+            down = down_tile.at[spot % 2]
+
+            def body(span):
+                value = mm(normed[span], up[...].reshape(width, tile), NN) + up_add[e : e + 1, column : column + tile]
+                hidden[e][span, column : column + tile] = value
+                value = gelu_tanh(value).astype(low)
+                active[e][span, column : column + tile] = value
+                after[span] += mm(value, down[...].reshape(width, tile), NT)
+
+            row_chunks(tokens, body)
+
+        work += [(functools.partial(feed, spot), tiles[spot][0]) for spot in range(len(tiles))]
+        crossing = []
+
+        def follow():
+            def body(span):
+                following[0][span] = (unit_rows(after[span]) * vectors[4:5] + vectors[5:6]).astype(low)
+
+            row_chunks(tokens, body)
+            crossing.append(copies.push(following[0], following[1], ids[3]))
+
+        if coming:
+            work.append((follow, None))
+        run_staggered(running, FORWARD_LEADS, work, 2)
+        for copy in crossing:
+            copy.wait_recv()
+        copies.finish()
+
+    outs = pl.pallas_call(
+        kernel,
+        in_specs=anywhere(total) + on_vmem(len(inputs) - 2) + on_smem(2),
+        out_specs=anywhere(len(shapes)) + on_vmem(len(more)),
+        out_shape=shapes + more,
+        scratch_shapes=[
+            pltpu.VMEM((2, 2, chips, rows, tile), low),
+            pltpu.VMEM((2, 2, chips, rows, tile), low),
+            pltpu.SemaphoreType.DMA((count,)),
+            pltpu.SemaphoreType.DMA((count,)),
+            pltpu.SemaphoreType.DMA((total + 2 + 8 * inner // tile,)),
+        ],
+        compiler_params=pltpu.CompilerParams(
+            collective_id=collective, has_side_effects=True, vmem_limit_bytes=58 * 1024 * 1024
+        ),
+        name="forward_layer",
+    )(*shards, *inputs)
+    weights = [out.reshape(-1, out.shape[-1]) for out in outs[: 2 * total]]
+    return (weights, outs[2 * total :])
 
 
 def add_rows(target, source):
@@ -483,25 +636,29 @@
         )
 
 
-def products(lefts, rights, held, columns, target, near):
-    for i, left in enumerate(lefts):
-        held[i] = left[:, columns].T
+def products(lefts, rights, span, target, near):
     blocks, rows, width = target.shape
     step = 512
 
-    @pl.loop(0, width // step)
-    def tile(i):
-        window = pl.ds(pl.multiple_of(i * step, step), step)
-        out = mm(held[0], rights[0][:, window], NN)
+    def tile(window):
+        out = mm(lefts[0][span], rights[0][:, window], NN)
         for j in range(1, len(rights)):
-            out = out + mm(held[j], rights[j][:, window], NN)
+            out = out + mm(lefts[j][span], rights[j][:, window], NN)
         out = out.reshape(blocks, rows, step)
         if near is not None:
             out = out + near[:, :, window].astype(jnp.float32)
         target[:, :, window] = out.astype(target.dtype)
 
-
-def scatter_steps(copies, ids, ring, arrays, held):
+    if width == step:
+        tile(slice(None))
+        return
+
+    @pl.loop(0, width // step)
+    def one(i):
+        tile(pl.ds(pl.multiple_of(i * step, step), step))
+
+
+def scatter_steps(copies, ids, ring, arrays, shared, place):
     ahead, behind, sibling, across = ids
     chips = ring.chips
     half = chips // 2
@@ -509,21 +666,40 @@
     slot = ring.turns.index
     near = {}
     crossed = {}
+    loads = {}
+
+    def rights(i, e):
+        source = arrays[i][0]
+        if not source[3]:
+            return source[2][e]
+        if e in loads:
+            loads.pop(e).wait()
+        return [shared["wide"].at[e]]
 
     def outgoing(group):
         blocks = pl.ds(group * group_blocks, group_blocks)
+        if group == 0:
+            for source, early, out, room in arrays:
+                if source[0] == "product" and source[3]:
+                    for e in (1, 0):
+                        loads[e] = pltpu.make_async_copy(source[2][e][0], shared["wide"].at[e], shared["loaded"].at[e])
+                        loads[e].start()
+        for copy in shared["busy"]:
+            copies.settle(copy)
+        shared["busy"] = []
+        if group == 0 and not place[0]:
+            pl.semaphore_wait(shared["free"], 1)
         for i, (source, early, out, room) in enumerate(arrays):
             for e in (1, 0):
                 if source[0] == "given":
-                    sent = source[1][e][1].at[blocks]
-                else:
-                    sent = room["outbox"].at[e]
-                    if group > 0:
-                        copies.settle(near[i, e, group - 1])
-                    height = group_blocks * out.shape[0]
-                    columns = slice((chips // group_blocks + group) * height, (chips // group_blocks + group + 1) * height)
-                    products(source[1], source[2][e], held, columns, sent, None)
+                    near[i, e, group] = copies.push(source[1][e][1].at[blocks], room["near"].at[e, blocks], sibling)
+                    continue
+                sent = room["outbox"].at[e]
+                height = group_blocks * out.shape[0]
+                span = pl.ds((2 + group) * height, height)
+                products(source[1], rights(i, e), span, sent, None)
                 near[i, e, group] = copies.push(sent, room["near"].at[e, blocks], sibling)
+                shared["busy"].append(near[i, e, group])
 
     def own(group):
         blocks = pl.ds(group * group_blocks, group_blocks)
@@ -535,12 +711,14 @@
                     target[...] = source[1][e][0][blocks] + room["near"][e, blocks]
                 else:
                     height = group_blocks * out.shape[0]
-                    columns = slice(group * height, (group + 1) * height)
-                    products(source[1], source[2][e], held, columns, target, room["near"].at[e, blocks])
+                    span = pl.ds(group * height, height)
+                    products(source[1], rights(i, e), span, target, room["near"].at[e, blocks])
                 if e == 1:
                     rest = pl.ds(early, out.shape[1] - early)
                     for block in range(group * group_blocks, (group + 1) * group_blocks):
                         crossed[i, block] = copies.push(room["sum"].at[1, block, :, rest], room["far"].at[block], across)
+        if group == 1 and not place[1]:
+            pl.semaphore_signal(shared["free"], inc=1, device_id=sibling, device_id_type=MESH)
 
     def second(spot):
         block = slot(spot)
@@ -617,13 +795,10 @@
 
 def scatter_order(chips, groups):
     hops = chips // 2 - 1
-    order = [0] * 4
-    for group in range(1, groups):
-        order += [group] * 3
-    order += [0, -1] * hops
-    for group in range(1, groups):
-        order += [group, group - 1] + [group, -1] * hops
-    return order + [groups - 1] + list(range(groups))
+    if groups == 1:
+        return [0] * (hops + 6)
+    order = [0] * 4 + [1] * 3 + [0, -1] * hops + [1, 0, -1] + [1, -1] * (hops - 1)
+    return order + [-2] + [2] * 3 + [1] + [2, 1] + [2] * hops + [2] + [0, 1, 2]
 
 
 def scatter_count(chips, arrays):
@@ -631,14 +806,12 @@
     return arrays * (4 + chips + half * 4 + 1)
 
 
-ROOM = ("outbox", "sum", "near", "far", "up", "down", "up_slim", "down_slim", "slim_out", "slim_in")
-
-
-def scatter_room(chips, rows, columns, early, dtype):
+ROOM = ("sum", "far", "up", "down", "up_slim", "down_slim", "slim_out", "slim_in", "near")
+
+
+def scatter_room(chips, rows, columns, early, dtype, given):
     half = chips // 2
-    shapes = (
-        (2, half, rows, columns),
-        (2, chips, rows, columns),
+    shapes = [
         (2, chips, rows, columns),
         (chips, rows, columns - early),
         (half, rows, columns),
@@ -647,37 +820,73 @@
         (half, rows, early),
         (rows, early),
         (rows, early),
-    )
+    ]
+    if given:
+        shapes.append((2, chips, rows, columns))
     return [pltpu.VMEM(shape, dtype) for shape in shapes]
 
 
-def scatter_grads(ring, groups, collective, attention=None):
+def scatter_given(ring, parts, early, collective):
+    chips = ring.chips
+    height, columns = parts[0][0].shape
+    rows = height // chips
+    dtype = parts[0][0].dtype
+    room = scatter_room(chips, rows, columns, early, dtype, True)
+    count = scatter_count(chips, 1)
+
+    def kernel(*refs):
+        ids = ring.neighbours()
+        greet(ids)
+        scratch = refs[5:]
+        copies = Copies(scratch[len(room)], scratch[len(room) + 1], None)
+        source = ("given", (refs[:2], refs[2:4]))
+        members = [(source, early, refs[4], dict(zip(ROOM, scratch)))]
+        run_all(scatter_steps(copies, ids, ring, members, {"busy": []}, (True, True)))
+        copies.finish()
+
+    return pl.pallas_call(
+        kernel,
+        in_specs=on_vmem(4),
+        out_specs=on_vmem(1)[0],
+        out_shape=jax.ShapeDtypeStruct((rows, columns), dtype),
+        scratch_shapes=room + [pltpu.SemaphoreType.DMA((count,)), pltpu.SemaphoreType.DMA((count,))],
+        compiler_params=pltpu.CompilerParams(collective_id=collective, has_side_effects=True),
+        name="scatter_given",
+    )(*[parts[e][c].reshape(chips, rows, columns) for e in range(2) for c in range(2)])
+
+
+def backward_layer(ring, groups, collective, attention):
     chips = ring.chips
     arrays = [member for group in groups for member in group]
-    inputs, counts, shapes, rooms = ([], [], [], [])
-    tokens = 0
+    total = len(arrays)
+    qkv, first, grad_heads, lse, slopes, prefix, scale = attention
+    height, tokens = arrays[0][0][0].shape
+    rows = height // chips // 2
+    low = jnp.bfloat16
+    inputs, wide = ([], [])
+
+    def entry(array):
+        if isinstance(array, int):
+            return array
+        for spot, other in enumerate(inputs):
+            if other is array:
+                return ("in", spot)
+        inputs.append(array)
+        wide.append(array.shape[1] > 1024)
+        return ("in", len(inputs) - 1)
+
+    plans, shapes, rooms, widths = ([], [], [], [])
     for lefts, rights, early in arrays:
-        if lefts is None:
-            height, columns = rights[0][0].shape
-            rows = height // chips
-            dtype = rights[0][0].dtype
-            members = [rights[e][c].reshape(chips, rows, columns) for e in range(2) for c in range(2)]
-        else:
-            tokens, height = lefts[0].shape
-            columns = rights[0][0].shape[1]
-            rows = height // chips // 2
-            dtype = jnp.bfloat16
-            members = list(lefts) + list(rights[0]) + list(rights[1])
-        counts.append(len(members))
-        inputs += members
+        plans.append(([entry(left) for left in lefts], [[entry(right) for right in side] for side in rights], early))
+        sample = rights[0][0]
+        columns = grad_heads[0].shape[1] if isinstance(sample, int) else sample.shape[1]
+        widths.append(columns)
         shapes.append(jax.ShapeDtypeStruct((rows, columns), jnp.float32))
-        rooms += scatter_room(chips, rows, columns, early, dtype)
-    total = len(arrays)
-    extra, made = ([], [])
-    if attention is not None:
-        qkv, first, grad_heads, lse, slopes, prefix, scale = attention
-        extra = list(qkv) + list(first) + list(grad_heads) + list(lse) + [slopes, prefix]
-        made = [jax.ShapeDtypeStruct(grad_heads[0].shape, jnp.bfloat16)] * 10
+        rooms += scatter_room(chips, rows, columns, early, low, False)
+    extra = list(qkv) + list(first) + list(grad_heads) + list(lse) + [slopes, prefix]
+    made = [jax.ShapeDtypeStruct(grad_heads[0].shape, low)] * 10
+    sizes = iter(widths)
+    span = max(sum(next(sizes) for unused in group) for group in groups)
 
     def kernel(*refs):
         ins, refs = (refs[: len(inputs)], refs[len(inputs) :])
@@ -686,54 +895,61 @@
         back, scratch = (refs[: len(made)], refs[len(made) :])
         ids = ring.neighbours()
         greet(ids)
-        held, sums, send, recv, near = scratch[len(rooms) :]
-        copies = Copies(send, recv, near)
-        members = []
+        held, outbox, near, sums, send, recv, loaded, free = scratch[len(rooms) :]
+        copies = Copies(send, recv, None)
+        shared = {"wide": held, "loaded": loaded, "free": free, "busy": []}
+        find = lambda spot: back[spot] if isinstance(spot, int) else ins[spot[1]]
+        running = []
         at = 0
-        for i, (lefts, rights, early) in enumerate(arrays):
-            mine = ins[at : at + counts[i]]
-            at += counts[i]
-            if lefts is None:
-                source = ("given", (mine[:2], mine[2:]))
-            else:
-                terms = len(lefts)
-                source = ("product", mine[:terms], (mine[terms : 2 * terms], mine[2 * terms :]))
-            members.append((source, early, outs[i], dict(zip(ROOM, scratch[i * len(ROOM) : (i + 1) * len(ROOM)]))))
-        work = []
-        if attention is not None:
-            parts = [(more[e], more[2 + e], more[4 + e], more[6 + e], back[5 * e : 5 * e + 5]) for e in range(2)]
-            work = backward_work(parts, more[8], more[9][0], scale, sums)
-        running = []
-        for group in groups:
-            running.append(scatter_steps(copies, ids, ring, members[: len(group)], held))
-            members = members[len(group) :]
+        for number, group in enumerate(groups):
+            members = []
+            column = 0
+            for unused in group:
+                lefts, rights, early = plans[at]
+                source = ("product", [find(spot) for spot in lefts], [[find(spot) for spot in half] for half in rights])
+                source += (widths[at] > 1024,)
+                room = dict(zip(ROOM, scratch[at * (len(ROOM) - 1) : (at + 1) * (len(ROOM) - 1)]))
+                window = pl.ds(column, widths[at])
+                room["outbox"] = outbox.at[:, :, :, window]
+                room["near"] = near.at[:, :, :, window]
+                members.append((source, early, outs[at], room))
+                column += widths[at]
+                at += 1
+            place = (number == 0, number == len(groups) - 1)
+            running.append(scatter_steps(copies, ids, ring, members, shared, place))
+        parts = [(more[e], more[2 + e], more[4 + e], more[6 + e], back[5 * e : 5 * e + 5]) for e in range(2)]
+        work = backward_work(parts, more[8], more[9][0], scale, sums)
         for turn in scatter_order(chips, len(groups)):
             if turn >= 0:
                 next(running[turn], None)
-            elif work:
+            elif turn == -1 and work:
                 work.pop(0)()
-        for piece in work:
-            piece()
+            elif turn == -2:
+                while work:
+                    work.pop(0)()
         copies.finish()
 
-    pieces = chips // 2 * (inputs[0].shape[1] // chips // 2)
+    count = scatter_count(chips, total)
     outs = pl.pallas_call(
         kernel,
-        in_specs=on_vmem(len(inputs)) + (on_vmem(8) + on_smem(2) if extra else []),
+        in_specs=[pl.BlockSpec(memory_space=pl.ANY if far else pltpu.VMEM) for far in wide] + on_vmem(8) + on_smem(2),
         out_specs=on_vmem(total + len(made)),
         out_shape=shapes + made,
         scratch_shapes=rooms
         + [
-            pltpu.VMEM((2, pieces, tokens), jnp.bfloat16),
+            pltpu.VMEM((2, tokens, max(widths)), low),
+            pltpu.VMEM((2, chips // 2, rows, span), low),
+            pltpu.VMEM((2, chips, rows, span), low),
             pltpu.VMEM((4, tokens, 128), jnp.float32),
-            pltpu.SemaphoreType.DMA((scatter_count(chips, total),)),
-            pltpu.SemaphoreType.DMA((scatter_count(chips, total),)),
-            pltpu.SemaphoreType.DMA((1,)),
+            pltpu.SemaphoreType.DMA((count,)),
+            pltpu.SemaphoreType.DMA((count,)),
+            pltpu.SemaphoreType.DMA((2,)),
+            pltpu.SemaphoreType.REGULAR,
         ],
         compiler_params=pltpu.CompilerParams(
             collective_id=collective, has_side_effects=True, vmem_limit_bytes=62 * 1024 * 1024
         ),
-        name="scatter_grads",
+        name="backward_layer",
     )(*inputs, *extra)
     return (outs[:total], outs[total:])
 
@@ -832,11 +1048,11 @@
     kept = []
     for layer in range(layers):
         qkv_proj, out_proj = (gathered[8 * layer : 8 * layer + 2], gathered[8 * layer + 2 : 8 * layer + 4])
-        normed = norm_rows(states, small[0][layer], small[1][layer]).astype(low)
         if layer == 0:
+            normed = norm_rows(states, small[0][layer], small[1][layer]).astype(low)
             normed_first = norm_rows(into_ring(before_first), small[0][layer], small[1][layer]).astype(low)
         else:
-            normed_first = lax.ppermute(normed, "tensor", [(0, 1)])
+            normed, normed_first = following
         qkv, kv_first = ([], [])
         for i in range(tensor):
             query = qkv_proj[i].shape[1] // 3
@@ -844,16 +1060,33 @@
             qkv.append(mixed.astype(low))
             mixed = jnp.dot(normed_first, qkv_proj[i][:, query:], preferred_element_type=f32)
             kv_first.append((mixed + qkv_add[layer][i][:, query:]).astype(low))
-        coming = groups[2 * layer + 1 : 2 * layer + 3]
-        weights, heads_out, lse = gather_weights(ring, coming, 2 + layer, (qkv, kv_first, slopes, prefix_len, scale))
+        coming = groups[2 * layer + 2] if layer + 1 < layers else []
+        rest = jnp.stack(
+            [small[i][layer][0] for i in (2, 3, 4, 5)] + [small[i][(layer + 1) % layers][0] for i in (0, 1)]
+        )
+        weights, made = forward_layer(
+            ring,
+            [shard for shard, early in groups[2 * layer + 1]],
+            coming,
+            2 + layer,
+            (qkv, kv_first, slopes, prefix_len, scale),
+            states,
+            out_proj,
+            rest,
+            up_add[layer].reshape(tensor, -1),
+        )
         gathered += weights
-        up_proj, down_proj = (gathered[8 * layer + 4 : 8 * layer + 6], gathered[8 * layer + 6 : 8 * layer + 8])
-        middle = states + mm(heads_out[0], out_proj[0], NT) + mm(heads_out[1], out_proj[1], NT) + small[2][layer]
-        normed_two = norm_rows(middle, small[3][layer], small[4][layer]).astype(low)
-        hidden = [jnp.dot(normed_two, up_proj[i], preferred_element_type=f32) + up_add[layer][i] for i in range(tensor)]
-        active = [gelu_tanh(values).astype(low) for values in hidden]
+        heads_out, lse, middle, normed_two, hidden, active, after = (
+            made[:2],
+            made[2:4],
+            made[4],
+            made[5],
+            made[6:8],
+            made[8:10],
+            made[10],
+        )
         kept.append((states, normed, normed_first, qkv, kv_first, lse, heads_out, middle, normed_two, hidden, active))
-        states = middle + mm(active[0], down_proj[0], NT) + mm(active[1], down_proj[1], NT) + small[5][layer]
+        states, following = (after, made[11:])
 
     final_states = from_ring(states.astype(low)).astype(low)[None]
     factor = local_rows * tensor * dp / valid_count
@@ -877,54 +1110,48 @@
         grad_attn = grad_middle.astype(low)
         out_shift = jnp.sum(grad_attn.astype(f32), axis=0)
         grad_heads = [jnp.dot(grad_attn, out_proj[i], preferred_element_type=f32).astype(low) for i in range(tensor)]
-        (down_grad, up_grad), grads = scatter_grads(
+        lefts = [normed.T, normed_first.T]
+        (down_grad, up_grad, out_grad, *mixed), grads = backward_layer(
             ring,
             [
-                [([grad_mlp], [[values] for values in active], 768)],
-                [([normed_two], [[values] for values in grad_hidden], 768)],
+                [([grad_mlp.T], [[values] for values in active], 512)],
+                [([normed_two.T], [[values] for values in grad_hidden], 512)],
+                [
+                    ([grad_attn.T], [[values] for values in heads_out], 256),
+                    (lefts[:1], [[0], [5]], 256),
+                    (lefts, [[1, 3], [6, 8]], 256),
+                    (lefts, [[2, 4], [7, 9]], 256),
+                ],
             ],
-            10 + 2 * layer,
+            10 + layer,
             (qkv, kv_first, grad_heads, lse, slopes, prefix_len, scale),
         )
+        weight_grads[layer] = (jnp.stack(mixed, axis=1), out_grad.T, up_grad, down_grad)
         grad_normed = 0.0
         qkv_shift = []
         sent = 0.0
-        query_terms, rest_terms = ([], [])
         for i in range(tensor):
             query = grads[5 * i].shape[1]
             grad_qkv = jnp.concatenate(grads[5 * i : 5 * i + 3], axis=1)
             grad_first = jnp.concatenate(grads[5 * i + 3 : 5 * i + 5], axis=1)
             sent = sent + mm(grad_first, qkv_proj[i][:, query:], NT)
-            query_terms.append([grads[5 * i]])
-            rest_terms.append([grad_qkv[:, query:], grad_first])
             shift = jnp.sum(grad_qkv.astype(f32), axis=0)
             qkv_shift.append(shift + jnp.pad(jnp.sum(grad_first.astype(f32), axis=0), (query, 0)))
             grad_normed = grad_normed + mm(grad_qkv, qkv_proj[i], NT)
         arrived = lax.ppermute(sent.astype(low), "tensor", [(1, 0)])
         qkv_shift = jnp.stack(qkv_shift)
-        projections = [
-            [
-                ([grad_attn], [[values] for values in heads_out], 256),
-                ([normed], query_terms, 256),
-                ([normed, normed_first], rest_terms, 256),
-            ]
-        ]
         grad_normed = grad_normed + arrived.astype(f32)
         part, gain_one, shift_one = norm_back(before, small[0][layer], grad_normed)
         grad = grad_middle + part
         vector_grads[layer] = (gain_one, shift_one, out_shift, gain_two, shift_two, down_shift)
         bias_grads[layer] = (qkv_shift, up_shift)
-        if layer == 0:
-            projections[0].append((None, small_parts(vector_grads, bias_grads, by_half, placed, piece, lane), 256))
-        (out_grad, query_grad, rest_grad, *last), unused = scatter_grads(ring, projections, 11 + 2 * layer)
-        qkv_grad = jnp.concatenate([query_grad, rest_grad], axis=1).reshape(rows, 3, -1)
-        weight_grads[layer] = (qkv_grad, out_grad.T, up_grad, down_grad)
-
+
+    summed = scatter_given(ring, small_parts(vector_grads, bias_grads, by_half, placed, piece, lane), 256, 20)
+    summed = summed.reshape(-1)
     input_grad = from_ring(grad, lax.Precision.HIGHEST)[None]
     qkv_grad, out_grad, up_grad, down_grad = [
         jnp.stack([weight_grads[layer][i] for layer in range(layers)]) for i in range(4)
     ]
-    summed = last[0].reshape(-1)
     vectors = summed[:first].reshape(6, layers, piece)
     return (
         final_states,

time: 864 us -> 844 us (0.977)
  Pallas kernels: 537 us -> 585 us
  waiting for transfers between devices: 48.1 us -> 3.37 us
  matrix products: 139 us -> 111 us
  local copies, waits for them, and re-layouts: 80.1 us -> 90.8 us
    pallas_call x4 -> x5, Pallas kernels: 313 us -> 542 us  [the longest x2 274 us: backward_layer(): pl.pallas_call(kernel, in_specs=[pl.BlockSpec(memory_space=pl.ANY if far...]
    pallas_call x3 -> x1, Pallas kernels: 224 us -> 43.3 us  [gather_weights(): pl.pallas_call(kernel, in_specs=anywhere(total) + (on_vmem(4) + on_smem(2...]
    ppermute x2, waiting for transfers between devices: 29.9 us -> 3.37 us  [local(): arrived = lax.ppermute(sent.astype(low), 'tensor', [(1, 0)])]
    dot_general x4 -> x0, matrix products: 20.9 us -> none  [local(): jnp.dot(normed_two, up_proj[i], preferred_element_type=f32)]
    ppermute x1 -> x0, waiting for transfers between devices: 18.1 us -> none  [local(): normed_first = lax.ppermute(normed, 'tensor', [(0, 1)])]
    dot_general x20 -> x12, matrix products: 53.6 us -> 36.8 us  [mm(): return lax.dot_general(a, b, dims, preferred_element_type=jnp.float32)]
    pallas_call x0 -> x8, local copies, waits for them, and re-layouts: none -> 16.7 us  [forward_layer(): pl.pallas_call(kernel, in_specs=anywhere(total) + on_vmem(len(inputs) - 2...]
    unnamed x341 -> x258, local copies, waits for them, and re-layouts: 40.5 us -> 36 us
  transfers between devices with their start and end apart: 4 -> 3, of which waited for: 3 -> 1; matrix products, arithmetic and copies ran while one was open for 7% -> 9% of each run, Pallas kernels for 5% -> 5%
where the time goes in v4:
time: 844 us; the launch traced here: 837 us
  Pallas kernels  585 us (69%)
  matrix products  111 us (13%)
  local copies, waits for them, and re-layouts  90.8 us (11%)
  other arithmetic  30.9 us (4%)
  starting transfers between devices  9.4 us (1%)
    pallas_call x2, Pallas kernels, backward_layer(): pl.pallas_call(kernel, in_specs=[pl.BlockSpec(memory_space=pl.ANY if far...  274 us
    pallas_call x2, Pallas kernels, forward_layer(): pl.pallas_call(kernel, in_specs=anywhere(total) + on_vmem(len(inputs) - 2...  246 us
    pallas_call x1, Pallas kernels, gather_weights(): pl.pallas_call(kernel, in_specs=anywhere(total) + (on_vmem(4) + on_smem(2...  43.3 us
    dot_general x12, matrix products, mm(): return lax.dot_general(a, b, dims, preferred_element_type=jnp.float32)  36.8 us
    unnamed x258, local copies, waits for them, and re-layouts  36 us
    dot_general x4, matrix products, local(): grad_active = jnp.dot(grad_mlp, down_proj[i], preferred_element_type=f32)  24.1 us
    pallas_call x1, Pallas kernels, scatter_given(): pl.pallas_call(kernel, in_specs=on_vmem(4), out_specs=on_vmem(1)[0], out_...  22.5 us
  transfers between devices with their start and end apart: 3, of which 1 were waited for; matrix products, arithmetic and copies ran while one was open for 9% of the time, Pallas kernels for 5%

profile of v4, /device:TPU:0, one launch (start us, length us, event | category | flops | bytes accessed | tf_op | source)
XLA Modules:
  0.0 837.5 jit_solution(13622416140989231202)
XLA Ops:
  0.7 6.0 collective-permute-start
  20.8 43.3 %gather_weights.1 = (bf16[2,8,16,512]{3,2,1,0:T(8,128)(2,1)S(1)}, bf16[2,8,16,512]{3,2,1,0:T(8,128)(2,1)S(1)}, bf16[2,8,64,1536]{3,2,1,0:T(8,128)(2,1)S(1)}, bf1...) custom-call(bf16[16,512]{1,0:T(8,128)(2,1)S(1)} %reshape.375.refs_0_, ...), custom_call_target="tpu_custom_call" | custom-call | tf_op jit(solution)/shard_map/gather_weights/pallas_call | solution.py:436
  73.1 2.5 fusion.121
  76.0 2.3 copy.152.refs_8_
  87.3 2.5 fusion.122
  92.4 3.2 fusion.33.refs_4_.refs_11_
  95.7 3.2 fusion.34.refs_5_.refs_12_
  98.9 2.2 add_convert_fusion.6.refs_6_.refs_13_
  101.1 2.3 add_convert_fusion.5.refs_7_.refs_14_
  103.4 142.7 %forward_layer.2 = (bf16[2,8,64,2048]{3,2,1,0:T(8,128)(2,1)}, bf16[2,8,64,2048]{3,2,1,0:T(8,128)(2,1)}, bf16[2,8,64,2048]{3,2,1,0:T(8,128)(2,1)}, bf16[2,8,64,20...) custom-call(bf16[64,2048]{1,0:T(8,128)(2,1)} %get-tuple-element.249., ...), custom_call_target="tpu_custom_call" | custom-call | tf_op jit(solution)/shard_map/forward_layer/pallas_call | solution.py:606
  246.2 5.3 fusion.35.refs_2_.refs_11_
  251.5 2.9 fusion.36.refs_3_.refs_12_
  254.5 2.2 add_convert_fusion.4.refs_4_.refs_13_
  256.7 2.2 add_convert_fusion.3.refs_5_.refs_14_
  258.9 2.2 copy.158
  261.2 102.8 %forward_layer.3 = (bf16[2,8,64,2048]{3,2,1,0:T(8,128)(2,1)}, bf16[2,8,64,2048]{3,2,1,0:T(8,128)(2,1)}, bf16[2,8,64,2048]{3,2,1,0:T(8,128)(2,1)}, bf16[2,8,64,20...) custom-call(bf16[64,2048]{1,0:T(8,128)(2,1)} %get-tuple-element.250., ...), custom_call_target="tpu_custom_call" | custom-call | tf_op jit(solution)/shard_map/forward_layer/pallas_call | solution.py:606
  364.0 2.9 copy.155
  366.9 1.9 reduce_sum.410
  369.3 2.6 copy.160
  373.2 3.0 copy.154
  381.7 5.6 convert_reduce_fusion.1
  387.3 2.4 fusion.123
  391.5 6.0 convert_reduce_fusion
  397.5 3.0 multiply_reduce_fusion
  400.5 2.2 convert_reduce_fusion.14
  410.3 136.6 %backward_layer.2 = (f32[64,2048]{1,0:T(8,128)}, f32[64,2048]{1,0:T(8,128)}, f32[64,512]{1,0:T(8,128)}, f32[64,512]{1,0:T(8,128)}, f32[64,512]{1,0:T(8,128)}, /*...) custom-call(bf16[1024,512]{1,0:T(8,128)(2,1)} %bitcast.286, ...), custom_call_target="tpu_custom_call" | custom-call | tf_op jit(solution)/shard_map/backward_layer/pallas_call | solution.py:933
  549.1 3.0 fusion.48
  554.7 2.3 add_convert_fusion.2
  562.3 1.9 constant_dynamic-update-slice_fusion.12
  564.2 2.0 constant_dynamic-update-slice_fusion.11
  572.2 2.0 multiply_reduce_fusion.6
  574.5 2.3 fusion.83
  578.8 3.4 collective-permute-done.1
  582.2 4.6 multiply_reduce_fusion.2
  590.7 6.2 convert_reduce_fusion.3
  596.9 2.4 fusion.125
  601.1 6.4 convert_reduce_fusion.2
  607.5 3.7 multiply_reduce_fusion.1
  611.2 2.7 convert_reduce_fusion.15
  617.1 137.1 %backward_layer.3 = (f32[64,2048]{1,0:T(8,128)}, f32[64,2048]{1,0:T(8,128)}, f32[64,512]{1,0:T(8,128)}, f32[64,512]{1,0:T(8,128)}, f32[64,512]{1,0:T(8,128)}, /*...) custom-call(bf16[1024,512]{1,0:T(8,128)(2,1)} %bitcast.272, ...), custom_call_target="tpu_custom_call" | custom-call | tf_op jit(solution)/shard_map/backward_layer/pallas_call | solution.py:933
  756.4 3.0 fusion.56
  761.3 2.2 add_convert_fusion
  770.9 1.9 constant_dynamic-update-slice_fusion.21
  785.4 2.4 pad_maximum_fusion
  788.9 3.4 fusion.126
  792.4 5.1 multiply_reduce_fusion.3
  800.0 22.5 %scatter_given.1 = f32[8,512]{1,0:T(8,128)} custom-call(f32[8,8,512]{2,1,0:T(8,128)} %get-tuple-element.246.refs_0_, f32[8,8,512]{2,1,0:T(8,128)} %get-tuple-element.245.refs_1_, f32[8,8,512]{2,1,0:T(8,128)} %get-tuple-element.244.refs_2_, f32[8,8,512]{2,1,0:T(8,128)} %get-tuple-element.243.refs_3_), custom_call_target="tpu_custom_call" | custom-call | tf_op jit(solution)/shard_map/scatter_given/pallas_call | solution.py:847
  826.4 10.9 %fusion.65 = f32[1,512,1024]{2,1,0:T(8,128)} fusion(s32[1024]{0:T(1024)S(1)} %copy-done.91, f32[512,1024]{0,1:T(8,128)} %get-tuple-element.234, f32[512,1024]{0,1:T(8,128)} %get-tuple-element.296, f32[512]{0:T(512)S(1)} %broadcast_multiply_fusion, f32[512]{0:T(512)S(1)} %broadcast_multiply_fusion.1, f32[1024]{0:T(1024)S(1)} %bitcast.314, ...), kind=kOutput, calls=%fused_computation.135 | convolution fusion | flops 6447693824 | bytes 8404992 | tf_op jit(solution)/shard_map/dot_general | solution.py:1009
  (416 shorter events, 104.7 us)
Async XLA Ops:
  0.6 375.9 %copy-start = (bf16[1,512,1024]{2,1,0:T(8,128)(2,1)S(1)}, bf16[1,512,1024]{2,1,0:T(8,128)(2,1)}, u32[]{:S(2)}) copy-start(bf16[1,512,1024]{2,1,0:T(8,128)(2,1)} %param.18) | copy-start | bytes 3145732
  0.7 86.7 %collective-permute-start = (bf16[512,1024]{1,0:T(8,128)(2,1)}, bf16[512,1024]{1,0:T(8,128)(2,1)}, u32[]{:S(2)}, u32[]{:S(2)}) collective-permute-start(bf16[512,1024]{1,0:T(8,128)(2,1)} %bitcast.349), channel_id=1, source_target_pairs={{0,1},{2,3},{4,5},{6,7},{8,9},{10,11},{12,13},{14,15},{16,17},{18,... | collective-permute-start | bytes 3145736 | tf_op jit(solution)/shard_map/ppermute | solution.py:1045
  12.0 59.2 %copy-start.92 = (s32[16]{0:T(128)}, s32[16]{0:T(128)S(1)}, u32[]{:S(2)}) copy-start(s32[16]{0:T(128)S(1)} %dynamic-slice_bitcast_fusion) | copy-start | bytes 196
  70.1 306.5 %copy-start.89 = (s32[1024]{0:T(1024)}, s32[1024]{0:T(1024)S(1)}, u32[]{:S(2)}) copy-start(s32[1024]{0:T(1024)S(1)} %add.284) | copy-start | bytes 12292
  73.1 22.5 %copy-start.79 = (f32[1,1,1,1024]{3,1,0,2:T(1,128)}, f32[1,1,1,1024]{3,1,0,2:T(1,128)S(1)}, u32[]{:S(2)}) copy-start(f32[1,1,1,1024]{3,1,0,2:T(1,128)S(1)} %get-tuple-element.277) | copy-start | bytes 12292
  75.6 20.0 %copy-start.13 = (f32[1024,512]{1,0:T(8,128)}, f32[1024,512]{1,0:T(8,128)S(1)}, u32[]{:S(2)}) copy-start(f32[1024,512]{1,0:T(8,128)S(1)} %get-tuple-element.289) | copy-start | bytes 6291460
  75.7 20.0 %copy-start.71 = (f32[512]{0:T(512)}, f32[512]{0:T(512)S(1)}, u32[]{:S(2)}) copy-start(f32[512]{0:T(512)S(1)} %broadcast_multiply_fusion.12) | copy-start | bytes 6148
  76.0 5.8 copy-start.86
  90.2 5.5 copy-start.84
  91.9 9.2 %copy-start.25 = (bf16[1024,512]{1,0:T(8,128)(2,1)}, bf16[1024,512]{1,0:T(8,128)(2,1)S(1)}, u32[]{:S(2)}) copy-start(bf16[1024,512]{1,0:T(8,128)(2,1)S(1)} %get-tuple-element.285.refs_10_) | copy-start | bytes 3145732
  246.2 5.4 copy-start.44
  246.2 5.4 copy-start.106
  379.3 10.4 %copy-start.45 = (bf16[512,1024]{0,1:T(8,128)(2,1)}, bf16[512,1024]{0,1:T(8,128)(2,1)S(1)}, u32[]{:S(2)}) copy-start(bf16[512,1024]{0,1:T(8,128)(2,1)S(1)} %get-tuple-element.225) | copy-start | bytes 3145732
  381.7 5.6 copy-start.103
  391.5 6.0 copy-start.100
  554.7 4.8 copy-start.51
  556.9 25.2 %collective-permute-start.1 = (bf16[512,1024]{0,1:T(8,128)(2,1)}, bf16[512,1024]{0,1:T(8,128)(2,1)}, u32[]{:S(2)}, u32[]{:S(2)}) collective-permute-start(bf16[512,1024]{0,1:T(8,128)(2,1)} %add_convert_fusion.2), channel_id=1, source_target_pairs={{1,0},{3,2},{5,4},{7,6},{9,8},{11,10},{13,12},{15,14},{17,16},{19,... | collective-permute-start | bytes 3145736 | tf_op jit(solution)/shard_map/ppermute | solution.py:1141
  560.3 11.9 %copy-start.73 = (f32[512]{0:T(512)}, f32[512]{0:T(512)S(1)}, u32[]{:S(2)}) copy-start(f32[512]{0:T(512)S(1)} %broadcast_multiply_fusion.4) | copy-start | bytes 6148
  561.7 6.2 copy-start.27
  561.7 6.2 copy-start.48
  569.2 5.1 copy-start.63
  569.2 5.1 copy-start.64
  569.2 5.1 copy-start.65
  569.2 5.1 copy-start.90
  577.0 5.2 copy-start.31
  577.0 5.2 copy-start.76
  577.0 5.2 copy-start.82
  577.0 5.2 copy-start.83
  577.0 5.2 copy-start.107
  582.2 4.7 copy-start.21
  588.4 10.9 %copy-start.22 = (bf16[512,1024]{0,1:T(8,128)(2,1)}, bf16[512,1024]{0,1:T(8,128)(2,1)S(1)}, u32[]{:S(2)}) copy-start(bf16[512,1024]{0,1:T(8,128)(2,1)S(1)} %get-tuple-element.227) | copy-start | bytes 3145732
  590.7 6.2 copy-start.97
  596.9 4.2 copy-start.96
  601.1 6.4 copy-start.18
  601.1 6.4 copy-start.74
  601.1 6.4 copy-start.81
  601.1 6.4 copy-start.94
  763.5 28.8 %collective-permute-start.2 = (bf16[512,1024]{0,1:T(8,128)(2,1)}, bf16[512,1024]{0,1:T(8,128)(2,1)}, u32[]{:S(2)}, u32[]{:S(2)}) collective-permute-start(bf16[512,1024]{0,1:T(8,128)(2,1)} %add_convert_fusion), channel_id=1, source_target_pairs={{1,0},{3,2},{5,4},{7,6},{9,8},{11,10},{13,12},{15,14},{17,16},{19,... | collective-permute-start | bytes 3145736 | tf_op jit(solution)/shard_map/ppermute | solution.py:1141
  765.4 4.6 copy-start.50
  770.0 4.5 copy-start.78
  770.0 4.6 copy-start.49
  778.7 9.1 %copy-start.59 = (f32[64,2048]{1,0:T(8,128)S(1)}, f32[64,2048]{1,0:T(8,128)}, u32[]{:S(2)}) copy-start(f32[64,2048]{1,0:T(8,128)} %get-tuple-element.161) | copy-start | bytes 1572868
  778.7 9.1 %copy-start.60 = (f32[64,2048]{1,0:T(8,128)S(1)}, f32[64,2048]{1,0:T(8,128)}, u32[]{:S(2)}) copy-start(f32[64,2048]{1,0:T(8,128)} %get-tuple-element.160) | copy-start | bytes 1572868
  792.3 5.4 copy-start.68
  792.3 5.4 copy-start.67
  792.3 5.5 copy-start.66
  798.8 27.5 %copy-start.91 = (s32[1024]{0:T(1024)S(1)}, s32[1024]{0:T(1024)}, u32[]{:S(2)}) copy-start(s32[1024]{0:T(1024)} %copy-done.89) | copy-start | bytes 12292
  826.3 10.9 %copy-start.1 = (bf16[1,512,1024]{2,1,0:T(8,128)(2,1)S(1)}, bf16[1,512,1024]{2,1,0:T(8,128)(2,1)}, u32[]{:S(2)}) copy-start(bf16[1,512,1024]{2,1,0:T(8,128)(2,1)} %param.18) | copy-start | bytes 3145732
  (66 other events, 169.6 us)

commit v5 on v4

--- a/solution.py
+++ b/solution.py
@@ -754,6 +754,7 @@
                 add_rows(room["sum"].at[e, slot(spot), :, window], room[kinds[e]].at[hop, :, window])
                 at += 1
 
+    place[2]()
     outgoing(0)
     yield
     own(0)
@@ -826,33 +827,68 @@
     return [pltpu.VMEM(shape, dtype) for shape in shapes]
 
 
-def scatter_given(ring, parts, early, collective):
+def last_sum(ring, parts, early, collective, states, grad, to_ring):
     chips = ring.chips
     height, columns = parts[0][0].shape
     rows = height // chips
     dtype = parts[0][0].dtype
+    low = jnp.bfloat16
     room = scatter_room(chips, rows, columns, early, dtype, True)
     count = scatter_count(chips, 1)
 
     def kernel(*refs):
         ids = ring.neighbours()
         greet(ids)
-        scratch = refs[5:]
+        states, grad, to_ring, out, final, back = refs[4:10]
+        scratch = refs[10:]
         copies = Copies(scratch[len(room)], scratch[len(room) + 1], None)
         source = ("given", (refs[:2], refs[2:4]))
-        members = [(source, early, refs[4], dict(zip(ROOM, scratch)))]
-        run_all(scatter_steps(copies, ids, ring, members, {"busy": []}, (True, True)))
+        members = [(source, early, out, dict(zip(ROOM, scratch)))]
+
+        def leave(span):
+            final[span] = mm(states[span].astype(low), to_ring[...], NT).astype(low)
+
+        def leave_grad(span):
+            rest = grad[span]
+            total = None
+            for unused in range(3):
+                part = rest.astype(low)
+                rest = rest - part.astype(jnp.float32)
+                moved = mm(part, to_ring[...], NT)
+                total = moved if total is None else total + moved
+            back[span] = total
+
+        work = [functools.partial(row_chunks, states.shape[0], body) for body in (leave_grad, leave)]
+        for unused in scatter_steps(copies, ids, ring, members, {"busy": []}, (True, True, lambda: None)):
+            if work:
+                work.pop(0)()
         copies.finish()
 
     return pl.pallas_call(
         kernel,
-        in_specs=on_vmem(4),
-        out_specs=on_vmem(1)[0],
-        out_shape=jax.ShapeDtypeStruct((rows, columns), dtype),
+        in_specs=on_vmem(7),
+        out_specs=on_vmem(3),
+        out_shape=[
+            jax.ShapeDtypeStruct((rows, columns), dtype),
+            jax.ShapeDtypeStruct(states.shape, low),
+            jax.ShapeDtypeStruct(grad.shape, jnp.float32),
+        ],
         scratch_shapes=room + [pltpu.SemaphoreType.DMA((count,)), pltpu.SemaphoreType.DMA((count,))],
-        compiler_params=pltpu.CompilerParams(collective_id=collective, has_side_effects=True),
-        name="scatter_given",
-    )(*[parts[e][c].reshape(chips, rows, columns) for e in range(2) for c in range(2)])
+        compiler_params=pltpu.CompilerParams(
+            collective_id=collective, has_side_effects=True, vmem_limit_bytes=40 * 1024 * 1024
+        ),
+        name="last_sum",
+    )(*[parts[e][c].reshape(chips, rows, columns) for e in range(2) for c in range(2)], states, grad, to_ring)
+
+
+def turn_all(order, ins, turned):
+    step = 256
+    for i, (unused, spot) in enumerate(order):
+
+        @pl.loop(0, ins[spot].shape[1] // step)
+        def chunk(j):
+            window = pl.ds(pl.multiple_of(j * step, step), step)
+            turned[i, window] = ins[spot][:, window].T
 
 
 def backward_layer(ring, groups, collective, attention):
@@ -860,7 +896,7 @@
     arrays = [member for group in groups for member in group]
     total = len(arrays)
     qkv, first, grad_heads, lse, slopes, prefix, scale = attention
-    height, tokens = arrays[0][0][0].shape
+    tokens, height = arrays[0][0][0].shape
     rows = height // chips // 2
     low = jnp.bfloat16
     inputs, wide = ([], [])
@@ -895,7 +931,7 @@
         back, scratch = (refs[: len(made)], refs[len(made) :])
         ids = ring.neighbours()
         greet(ids)
-        held, outbox, near, sums, send, recv, loaded, free = scratch[len(rooms) :]
+        held, turned, outbox, near, sums, send, recv, loaded, free = scratch[len(rooms) :]
         copies = Copies(send, recv, None)
         shared = {"wide": held, "loaded": loaded, "free": free, "busy": []}
         find = lambda spot: back[spot] if isinstance(spot, int) else ins[spot[1]]
@@ -903,10 +939,14 @@
         at = 0
         for number, group in enumerate(groups):
             members = []
+            order = []
             column = 0
             for unused in group:
                 lefts, rights, early = plans[at]
-                source = ("product", [find(spot) for spot in lefts], [[find(spot) for spot in half] for half in rights])
+                for spot in lefts:
+                    if spot not in order:
+                        order.append(spot)
+                source = ("product", [turned.at[order.index(spot)] for spot in lefts], [[find(spot) for spot in half] for half in rights])
                 source += (widths[at] > 1024,)
                 room = dict(zip(ROOM, scratch[at * (len(ROOM) - 1) : (at + 1) * (len(ROOM) - 1)]))
                 window = pl.ds(column, widths[at])
@@ -915,7 +955,7 @@
                 members.append((source, early, outs[at], room))
                 column += widths[at]
                 at += 1
-            place = (number == 0, number == len(groups) - 1)
+            place = (number == 0, number == len(groups) - 1, functools.partial(turn_all, order, ins, turned))
             running.append(scatter_steps(copies, ids, ring, members, shared, place))
         parts = [(more[e], more[2 + e], more[4 + e], more[6 + e], back[5 * e : 5 * e + 5]) for e in range(2)]
         work = backward_work(parts, more[8], more[9][0], scale, sums)
@@ -938,6 +978,7 @@
         scratch_shapes=rooms
         + [
             pltpu.VMEM((2, tokens, max(widths)), low),
+            pltpu.VMEM((3, height, tokens), low),
             pltpu.VMEM((2, chips // 2, rows, span), low),
             pltpu.VMEM((2, chips, rows, span), low),
             pltpu.VMEM((4, tokens, 128), jnp.float32),
@@ -1005,24 +1046,22 @@
     def into_ring(values):
         return jnp.dot(values, to_ring, preferred_element_type=f32)
 
-    def from_ring(values, precision=None):
-        return lax.dot_general(
-            values, to_ring.astype(values.dtype), NT, precision=precision, preferred_element_type=f32
-        )
-
     count = jnp.sum(valid_mask)
     vectors = jnp.stack([ln1_gain, ln1_shift, out_bias, ln2_gain, ln2_shift, down_bias])
     packed = jnp.concatenate(
         [vectors.reshape(-1), qkv_bias.reshape(-1), up_bias.reshape(-1), jnp.stack([count // 256, count % 256]).astype(low)]
     )
     first, second, third = (vectors.size, vectors.size + qkv_bias.size, vectors.size + qkv_bias.size + up_bias.size)
+    packed_size = packed.size
     packed = jnp.pad(packed, (0, 16 * 512 - packed.size)).reshape(16, 512)
     groups = []
     for layer in range(layers):
         groups.append([(qkv_weight[layer].reshape(rows, -1), 512), (out_weight[layer].T, 256)])
         groups.append([(up_weight[layer], 768), (down_weight[layer].T, 768)])
     weights = gather_weights(ring, [[(packed, 256)] + groups[0]], 1)[0]
-    everything = by_half(jnp.stack([member.reshape(dp, -1) for member in weights[:2]]), 0)
+    used = -(-packed_size // 512)
+    everything = [member.reshape(dp, -1, 512)[:, :used].reshape(dp, -1) for member in weights[:2]]
+    everything = by_half(jnp.stack(everything), 0)
     gathered = weights[2:]
     vectors = everything[:, :, :first].reshape(tensor, dp, 6, layers, piece).transpose(2, 3, 1, 0, 4)
     small = vectors.reshape(6, layers, 1, width).astype(f32)
@@ -1088,7 +1127,6 @@
         kept.append((states, normed, normed_first, qkv, kv_first, lse, heads_out, middle, normed_two, hidden, active))
         states, following = (after, made[11:])
 
-    final_states = from_ring(states.astype(low)).astype(low)[None]
     factor = local_rows * tensor * dp / valid_count
     grad = factor * valid_mask[0][:, None].astype(f32) * (states - target)
     weight_grads = [None] * layers
@@ -1110,14 +1148,14 @@
         grad_attn = grad_middle.astype(low)
         out_shift = jnp.sum(grad_attn.astype(f32), axis=0)
         grad_heads = [jnp.dot(grad_attn, out_proj[i], preferred_element_type=f32).astype(low) for i in range(tensor)]
-        lefts = [normed.T, normed_first.T]
+        lefts = [normed, normed_first]
         (down_grad, up_grad, out_grad, *mixed), grads = backward_layer(
             ring,
             [
-                [([grad_mlp.T], [[values] for values in active], 512)],
-                [([normed_two.T], [[values] for values in grad_hidden], 512)],
+                [([grad_mlp], [[values] for values in active], 512)],
+                [([normed_two], [[values] for values in grad_hidden], 512)],
                 [
-                    ([grad_attn.T], [[values] for values in heads_out], 256),
+                    ([grad_attn], [[values] for values in heads_out], 256),
                     (lefts[:1], [[0], [5]], 256),
                     (lefts, [[1, 3], [6, 8]], 256),
                     (lefts, [[2, 4], [7, 9]], 256),
@@ -1146,16 +1184,16 @@
         vector_grads[layer] = (gain_one, shift_one, out_shift, gain_two, shift_two, down_shift)
         bias_grads[layer] = (qkv_shift, up_shift)
 
-    summed = scatter_given(ring, small_parts(vector_grads, bias_grads, by_half, placed, piece, lane), 256, 20)
+    parts = small_parts(vector_grads, bias_grads, by_half, placed, piece, lane)
+    summed, final_states, input_grad = last_sum(ring, parts, 256, 20, states, grad, to_ring)
     summed = summed.reshape(-1)
-    input_grad = from_ring(grad, lax.Precision.HIGHEST)[None]
     qkv_grad, out_grad, up_grad, down_grad = [
         jnp.stack([weight_grads[layer][i] for layer in range(layers)]) for i in range(4)
     ]
     vectors = summed[:first].reshape(6, layers, piece)
     return (
-        final_states,
-        input_grad,
+        final_states[None],
+        input_grad[None],
         vectors[0],
         vectors[1],
         qkv_grad,

time: 844 us -> 834 us (0.988)
  local copies, waits for them, and re-layouts: 90.8 us -> 70.4 us
    pallas_call x8 -> x0, local copies, waits for them, and re-layouts: 16.7 us -> none  [forward_layer(): pl.pallas_call(kernel, in_specs=anywhere(total) + on_vmem(len(inputs) - 2...]
    dot_general x2 -> x0, matrix products: 13.2 us -> none  [from_ring(): lax.dot_general(values, to_ring.astype(values.dtype), NT, precision=preci...]
    unnamed x258 -> x296, local copies, waits for them, and re-layouts: 36 us -> 39.6 us
  transfers between devices with their start and end apart: 3 -> 3, of which waited for: 1 -> 2; matrix products, arithmetic and copies ran while one was open for 9% -> 9% of each run, Pallas kernels for 5% -> 5%
where the time goes in v5:
time: 834 us; the launch traced here: 824 us
  Pallas kernels  587 us (70%)
  matrix products  105 us (13%)
  local copies, waits for them, and re-layouts  70.4 us (8%)
  other arithmetic  33.9 us (4%)
  waiting for transfers between devices  11.8 us (1%)
  starting transfers between devices  8.78 us (1%)
    pallas_call x2, Pallas kernels, backward_layer(): pl.pallas_call(kernel, in_specs=[pl.BlockSpec(memory_space=pl.ANY if far...  276 us
    pallas_call x2, Pallas kernels, forward_layer(): pl.pallas_call(kernel, in_specs=anywhere(total) + on_vmem(len(inputs) - 2...  246 us
    pallas_call x1, Pallas kernels, gather_weights(): pl.pallas_call(kernel, in_specs=anywhere(total) + (on_vmem(4) + on_smem(2...  44.8 us
    unnamed x296, local copies, waits for them, and re-layouts  39.6 us
    dot_general x12, matrix products, mm(): return lax.dot_general(a, b, dims, preferred_element_type=jnp.float32)  39.1 us
    dot_general x4, matrix products, local(): grad_active = jnp.dot(grad_mlp, down_proj[i], preferred_element_type=f32)  24.7 us
    pallas_call x1, Pallas kernels, last_sum(): pl.pallas_call(kernel, in_specs=on_vmem(7), out_specs=on_vmem(3), out_sha...  20.8 us
  transfers between devices with their start and end apart: 3, of which 2 were waited for; matrix products, arithmetic and copies ran while one was open for 9% of the time, Pallas kernels for 5%

profile of v5, /device:TPU:0, one launch (start us, length us, event | category | flops | bytes accessed | tf_op | source)
XLA Modules:
  0.0 824.0 jit_solution(5796632814029044762)
XLA Ops:
  0.7 6.0 collective-permute-start
  19.4 44.8 %gather_weights.1 = (bf16[2,8,16,512]{3,2,1,0:T(8,128)(2,1)S(1)}, bf16[2,8,16,512]{3,2,1,0:T(8,128)(2,1)S(1)}, bf16[2,8,64,1536]{3,2,1,0:T(8,128)(2,1)S(1)}, bf1...) custom-call(bf16[16,512]{1,0:T(8,128)(2,1)S(1)} %reshape.375.refs_0_, ...), custom_call_target="tpu_custom_call" | custom-call | tf_op jit(solution)/shard_map/gather_weights/pallas_call | solution.py:436
  71.8 2.6 fusion.94
  74.5 2.2 fusion.25.refs_6_
  79.4 1.9 copy.84
  82.6 1.9 slice_bitcast_fusion
  84.5 1.9 slice_bitcast_fusion.1
  94.6 5.3 fusion.27.refs_5_.refs_12_
  99.9 2.9 fusion.26.refs_4_.refs_11_
  102.9 3.9 fusion.95
  106.7 2.1 copy.91
  111.5 2.2 add_convert_fusion.4.refs_7_.refs_14_
  113.7 2.2 add_convert_fusion.5.refs_6_.refs_13_
  115.9 142.9 %forward_layer.2 = (bf16[2,8,64,2048]{3,2,1,0:T(8,128)(2,1)}, bf16[2,8,64,2048]{3,2,1,0:T(8,128)(2,1)}, bf16[2,8,64,2048]{3,2,1,0:T(8,128)(2,1)}, bf16[2,8,64,20...) custom-call(bf16[64,2048]{1,0:T(8,128)(2,1)} %get-tuple-element.255., ...), custom_call_target="tpu_custom_call" | custom-call | tf_op jit(solution)/shard_map/forward_layer/pallas_call | solution.py:606
  258.8 4.3 add_convert_fusion.2.refs_5_.refs_14_
  263.2 2.3 add_convert_fusion.3.refs_4_.refs_13_
  265.5 2.9 fusion.29.refs_3_.refs_12_
  268.4 3.0 fusion.28.refs_2_.refs_11_
  271.4 103.0 %forward_layer.3 = (bf16[2,8,64,2048]{3,2,1,0:T(8,128)(2,1)}, bf16[2,8,64,2048]{3,2,1,0:T(8,128)(2,1)}, bf16[2,8,64,2048]{3,2,1,0:T(8,128)(2,1)}, bf16[2,8,64,20...) custom-call(bf16[64,2048]{1,0:T(8,128)(2,1)} %get-tuple-element.256., ...), custom_call_target="tpu_custom_call" | custom-call | tf_op jit(solution)/shard_map/forward_layer/pallas_call | solution.py:606
  374.4 1.9 reduce_sum.410
  378.0 2.0 convert_reduce_fusion.12
  380.1 7.7 convert_reduce_fusion.1
  387.9 2.4 fusion.96
  392.1 5.5 convert_reduce_fusion
  397.6 3.5 multiply_reduce_fusion.1
  401.1 2.7 convert_reduce_fusion.14
  407.2 138.5 %backward_layer.2 = (f32[64,2048]{1,0:T(8,128)}, f32[64,2048]{1,0:T(8,128)}, f32[64,512]{1,0:T(8,128)}, f32[64,512]{1,0:T(8,128)}, f32[64,512]{1,0:T(8,128)}, /*...) custom-call(bf16[512,1024]{1,0:T(8,128)(2,1)} %copy-done.48, ...), custom_call_target="tpu_custom_call" | custom-call | tf_op jit(solution)/shard_map/backward_layer/pallas_call | solution.py:973
  547.9 2.9 fusion.32
  554.1 2.3 add_convert_fusion.1
  557.9 1.8 reduce_sum.418
  559.8 2.9 multiply_reduce_fusion.6
  570.4 3.0 fusion.149.refs_10_
  573.4 3.9 fusion.97
  577.3 3.4 collective-permute-done.1
  580.7 4.5 multiply_reduce_fusion.3
  589.1 5.9 convert_reduce_fusion.3
  595.1 2.4 fusion.98
  599.3 5.5 convert_reduce_fusion.2
  604.8 3.6 multiply_reduce_fusion.2
  608.5 2.1 convert_reduce_fusion.15
  613.7 137.0 %backward_layer.3 = (f32[64,2048]{1,0:T(8,128)}, f32[64,2048]{1,0:T(8,128)}, f32[64,512]{1,0:T(8,128)}, f32[64,512]{1,0:T(8,128)}, f32[64,512]{1,0:T(8,128)}, /*...) custom-call(bf16[512,1024]{1,0:T(8,128)(2,1)} %copy-done.27, ...), custom_call_target="tpu_custom_call" | custom-call | tf_op jit(solution)/shard_map/backward_layer/pallas_call | solution.py:973
  753.0 2.9 fusion.40
  758.2 2.3 add_convert_fusion
  774.1 3.4 fusion.99
  777.5 8.4 %collective-permute-done.2 = bf16[512,1024]{1,0:T(8,128)(2,1)} collective-permute-done((bf16[512,1024]{1,0:T(8,128)(2,1)}, bf16[512,1024]{1,0:T(8,128)(2,1)}, u32[]{:S(2)}, u32[]{:S(2)}) %collective-permute-start.2) | collective-permute-done | bytes 1048608 | tf_op jit(solution)/shard_map/ppermute | solution.py:1179
  785.9 5.0 multiply_reduce_fusion
  792.5 3.0 multiply_add_fusion.8.refs_5_
  796.0 20.8 %last_sum.1 = (f32[8,512]{1,0:T(8,128)S(1)}, bf16[512,1024]{1,0:T(8,128)(2,1)S(1)}, f32[512,1024]{1,0:T(8,128)S(1)}) custom-call(f32[8,8,512]{2,1,0:T(8,128)S(1)} %get-tuple-element.252.refs_0_, f32[8,8,512]{2,1,0:T(8,128)S(1)} %get-tuple-element.251.refs_1_, f32[8,8,512]{2,1,0:T(8,128)S(1)} %get-tuple-element.250.refs_2_, ...), custom_call_target="tpu_custom_call" | custom-call | tf_op jit(solution)/shard_map/last_sum/pallas_call | solution.py:867
  (450 shorter events, 87.1 us)
Async XLA Ops:
  0.6 376.4 %copy-start = (bf16[1,512,1024]{2,1,0:T(8,128)(2,1)S(1)}, bf16[1,512,1024]{2,1,0:T(8,128)(2,1)}, u32[]{:S(2)}) copy-start(bf16[1,512,1024]{2,1,0:T(8,128)(2,1)} %param.18) | copy-start | bytes 3145732
  0.7 71.2 %copy-start.128 = (bf16[1,512,1024]{2,1,0:T(8,128)(2,1)S(1)}, bf16[1,512,1024]{2,1,0:T(8,128)(2,1)}, u32[]{:S(2)}) copy-start(bf16[1,512,1024]{2,1,0:T(8,128)(2,1)} %param.17) | copy-start | bytes 3145732
  0.7 102.2 %collective-permute-start = (bf16[512,1024]{1,0:T(8,128)(2,1)}, bf16[512,1024]{1,0:T(8,128)(2,1)}, u32[]{:S(2)}, u32[]{:S(2)}) collective-permute-start(bf16[512,1024]{1,0:T(8,128)(2,1)} %bitcast.332), channel_id=1, source_target_pairs={{0,1},{2,3},{4,5},{6,7},{8,9},{10,11},{12,13},{14,15},{16,17},{18,... | collective-permute-start | bytes 3145736 | tf_op jit(solution)/shard_map/ppermute | solution.py:1084
  71.1 7.0 copy-start.112
  81.3 8.4 %copy-start.19 = (f32[1024,512]{0,1:T(8,128)}, f32[1024,512]{0,1:T(8,128)S(1)}, u32[]{:S(2)}) copy-start(f32[1024,512]{0,1:T(8,128)S(1)} %copy.84) | copy-start | bytes 6291460
  81.3 8.4 %copy-start.83 = (f32[512]{0:T(512)}, f32[512]{0:T(512)S(1)}, u32[]{:S(2)}) copy-start(f32[512]{0:T(512)S(1)} %broadcast_multiply_fusion.12) | copy-start | bytes 6148
  81.7 9.5 %copy-start.85 = (f32[512]{0:T(512)}, f32[512]{0:T(512)S(1)}, u32[]{:S(2)}) copy-start(f32[512]{0:T(512)S(1)} %add_rsqrt_fusion.4) | copy-start | bytes 6148
  86.4 6.9 copy-start.94
  86.4 6.9 copy-start.95
  86.4 6.9 copy-start.96
  86.4 6.9 copy-start.97
  86.4 6.9 copy-start.98
  86.4 6.9 copy-start.99
  89.8 4.8 copy-start.105
  94.6 5.4 copy-start.15
  94.6 5.4 copy-start.30
  94.6 5.4 copy-start.104
  258.8 4.3 copy-start.47
  258.8 4.3 copy-start.126
  379.9 10.4 %copy-start.48 = (bf16[512,1024]{1,0:T(8,128)(2,1)}, bf16[512,1024]{1,0:T(8,128)(2,1)S(1)}, u32[]{:S(2)}) copy-start(bf16[512,1024]{1,0:T(8,128)(2,1)S(1)} %get-tuple-element.231.refs_0_) | copy-start | bytes 3145732
  380.1 7.7 copy-start.122
  392.1 5.5 copy-start.119
  556.5 24.2 %collective-permute-start.1 = (bf16[512,1024]{1,0:T(8,128)(2,1)}, bf16[512,1024]{1,0:T(8,128)(2,1)}, u32[]{:S(2)}, u32[]{:S(2)}) collective-permute-start(bf16[512,1024]{1,0:T(8,128)(2,1)} %add_convert_fusion.1), channel_id=1, source_target_pairs={{1,0},{3,2},{5,4},{7,6},{9,8},{11,10},{13,12},{15,14},{17,16},{19,... | collective-permute-start | bytes 3145736 | tf_op jit(solution)/shard_map/ppermute | solution.py:1179
  564.2 4.2 copy-start.107
  564.2 6.1 copy-start.101
  569.1 4.2 copy-start.36
  573.4 7.3 copy-start.33
  573.4 7.3 copy-start.90
  573.4 7.3 copy-start.93
  573.4 7.3 copy-start.100
  573.4 7.3 copy-start.125
  580.7 4.5 copy-start.26
  586.1 11.4 %copy-start.27 = (bf16[512,1024]{1,0:T(8,128)(2,1)}, bf16[512,1024]{1,0:T(8,128)(2,1)S(1)}, u32[]{:S(2)}) copy-start(bf16[512,1024]{1,0:T(8,128)(2,1)S(1)} %get-tuple-element.233.refs_0_) | copy-start | bytes 3145732
  589.1 6.0 copy-start.116
  599.3 5.5 copy-start.24
  599.3 5.5 copy-start.88
  599.3 5.6 copy-start.92
  599.3 5.6 copy-start.113
  760.5 25.4 %collective-permute-start.2 = (bf16[512,1024]{1,0:T(8,128)(2,1)}, bf16[512,1024]{1,0:T(8,128)(2,1)}, u32[]{:S(2)}, u32[]{:S(2)}) collective-permute-start(bf16[512,1024]{1,0:T(8,128)(2,1)} %add_convert_fusion), channel_id=1, source_target_pairs={{1,0},{3,2},{5,4},{7,6},{9,8},{11,10},{13,12},{15,14},{17,16},{19,... | collective-permute-start | bytes 3145736 | tf_op jit(solution)/shard_map/ppermute | solution.py:1179
  774.0 11.8 %copy-start.13 = (bf16[2,8,64,1536]{3,2,1,0:T(8,128)(2,1)S(1)}, bf16[2,8,64,1536]{3,2,1,0:T(8,128)(2,1)}, u32[]{:S(2)}) copy-start(bf16[2,8,64,1536]{3,2,1,0:T(8,128)(2,1)} %copy-done.11) | copy-start | bytes 9437188
  774.0 11.8 %copy-start.20 = (f32[1024,512]{0,1:T(8,128)S(1)}, f32[1024,512]{0,1:T(8,128)}, u32[]{:S(2)}) copy-start(f32[1024,512]{0,1:T(8,128)} %copy-done.19) | copy-start | bytes 6291460
  774.0 11.8 %copy-start.39 = (bf16[512,1536]{1,0:T(8,128)(2,1)S(1)}, bf16[512,1536]{1,0:T(8,128)(2,1)}, u32[]{:S(2)}) copy-start(bf16[512,1536]{1,0:T(8,128)(2,1)} %copy-done.38) | copy-start | bytes 4718596
  774.0 11.8 %copy-start.84 = (f32[512]{0:T(512)S(1)}, f32[512]{0:T(512)}, u32[]{:S(2)}) copy-start(f32[512]{0:T(512)} %copy-done.83) | copy-start | bytes 6148
  774.0 11.8 %copy-start.86 = (f32[512]{0:T(512)S(1)}, f32[512]{0:T(512)}, u32[]{:S(2)}) copy-start(f32[512]{0:T(512)} %copy-done.85) | copy-start | bytes 6148
  777.4 13.7 %copy-start.80 = (f32[1,16,2,32]{3,2,1,0:T(2,128)S(1)}, f32[1,16,2,32]{3,2,1,0:T(2,128)}, u32[]{:S(2)}) copy-start(f32[1,16,2,32]{3,2,1,0:T(2,128)} %stack.210) | copy-start | bytes 12292
  777.4 13.7 %copy-start.79 = (f32[1,16,2,32]{3,2,1,0:T(2,128)S(1)}, f32[1,16,2,32]{3,2,1,0:T(2,128)}, u32[]{:S(2)}) copy-start(f32[1,16,2,32]{3,2,1,0:T(2,128)} %stack.212) | copy-start | bytes 12292
  777.5 13.7 %copy-start.78 = (f32[1,16,2,32]{3,2,1,0:T(2,128)S(1)}, f32[1,16,2,32]{3,2,1,0:T(2,128)}, u32[]{:S(2)}) copy-start(f32[1,16,2,32]{3,2,1,0:T(2,128)} %stack.214) | copy-start | bytes 12292
  777.5 13.7 %copy-start.77 = (f32[1,16,2,32]{3,2,1,0:T(2,128)S(1)}, f32[1,16,2,32]{3,2,1,0:T(2,128)}, u32[]{:S(2)}) copy-start(f32[1,16,2,32]{3,2,1,0:T(2,128)} %stack.216) | copy-start | bytes 12292
  (84 other events, 213.8 us)
